TPU v7x, 256 devices: a whole 4x4x8 slice. The times are simulated.
256 devices in a mesh: rows: 8 (over x, core), cols: 32 (over y, z).
Axes of the slice: x: 4, y: 4, z: 8, core: 2. Of those that a mesh axis runs over, the one named last changes fastest.
Arguments:
- left: bfloat16 [32, 16, 4096], P(None, 'rows', 'cols'), may hold values from -6 to 6
- right: bfloat16 [32, 16, 4096], P(None, 'rows', 'cols'), may hold values from -6 to 6
- offsets: int32 [32], P('cols'), may hold values from 0 to 384, as said below
- weight_one: bfloat16 [27, 32, 32], replicated, may hold values from -0.21875 to 0.21875
- bias_one: float32 [32], replicated, may hold values from -0.5 to 0.5
- weight_two: bfloat16 [27, 32, 32], replicated, may hold values from -0.21875 to 0.21875
- bias_two: float32 [32], replicated, may hold values from -0.5 to 0.5
Outputs:
- aggregated: bfloat16 [32, 48, 16, 4096], P(None, None, 'rows', 'cols')
Inputs may be any that keep to these rules, and one draw needn't show every extreme that they name: `offsets`: one tile has offset 384 and another has offset 0; the rest are uneven between.
All inputs are finite; a program needn't handle non-finite values.
Results may differ from a plain program's by a relative error of at most 0.0095.
Values may be sent and summed in bfloat16 or wider, within the bound.
No kernel may reach another device: no remote copies, remote signals or barrier semaphores. Data moves between devices by JAX's collectives and lax.ppermute only.
A program may use at most 64 MiB of HBM per device.

v0:
```python
import jax
import jax.numpy as jnp
from jax import lax
from jax.sharding import PartitionSpec as P

D = 48
REACH = 3


def passed_along(shard, axis, by):
    size = lax.axis_size(axis)
    pairs = [(i, i + by) for i in range(size) if 0 <= i + by < size]
    return lax.ppermute(shard, axis, pairs)


def with_halo(block, sides, width):
    for axis, dim in sides:
        count = lax.axis_size(axis)
        forward = [(i, i + 1) for i in range(count - 1)]
        backward = [(target, source) for source, target in forward]
        low = lax.ppermute(
            lax.slice_in_dim(block, block.shape[dim] - width, None, axis=dim), axis, forward
        )
        high = lax.ppermute(lax.slice_in_dim(block, 0, width, axis=dim), axis, backward)
        block = jnp.concatenate([low, block, high], axis=dim)
    return block


def fetch_tile(right, distance):
    return passed_along(right, "cols", distance)


def correlate(left, window, disparities):
    width = left.shape[2]

    def one_disparity(disparity):
        return lax.dynamic_slice_in_dim(window, disparities - 1 - disparity, width, 2)

    stacked = jax.vmap(one_disparity, out_axes=1)(jnp.arange(disparities, dtype=jnp.int32))
    product = left.astype(jnp.float32)[:, None] * stacked.astype(jnp.float32)
    return product.astype(jnp.bfloat16)


def convolve(padded, weight):
    channels = weight.shape[1]
    kernel = jnp.transpose(weight.reshape(3, 3, 3, channels, channels), (3, 4, 0, 1, 2))
    return lax.conv_general_dilated(
        padded[None],
        kernel,
        (1, 1, 1),
        ((1, 1), (0, 0), (0, 0)),
        dimension_numbers=("NCDHW", "OIDHW", "NCDHW"),
        preferred_element_type=jnp.float32,
    )[0]


def body(left, right, offsets, weight_one, bias_one, weight_two, bias_two):
    channels, rows_here, width = left.shape
    offset = offsets[0]
    window_width = width + D - 1
    pieces = [fetch_tile(right, distance) for distance in range(REACH + 1, 0, -1)]
    joined = jnp.concatenate(pieces + [right], axis=2)
    start = (REACH + 1) * width - offset - (D - 1)
    window = lax.dynamic_slice_in_dim(joined, start, window_width, 2)
    volume = correlate(left, window, D)
    padded = with_halo(volume, (("rows", 2), ("cols", 3)), 1)
    hidden = jnp.maximum(convolve(padded, weight_one) + bias_one[:, None, None, None], 0.0).astype(
        jnp.bfloat16
    )
    hidden = with_halo(hidden, (("rows", 2), ("cols", 3)), 1)
    result = (
        convolve(hidden, weight_two) + bias_two[:, None, None, None] + volume.astype(jnp.float32)
    )
    return result.astype(jnp.bfloat16)


def solution(mesh):
    return jax.shard_map(
        body,
        mesh=mesh,
        in_specs=(P(None, "rows", "cols"), P(None, "rows", "cols"), P("cols"), P(), P(), P(), P()),
        out_specs=P(None, None, "rows", "cols"),
        check_vma=False,
    )
```

profile of v0, /device:TPU:19, one launch (start us, length us, event | category | flops | bytes accessed | tf_op | source)
XLA Modules:
  0.0 194.7 jit_solution(9750672450855762524)
XLA Ops:
  0.0 0.9 copy.111
  0.9 3.5 %collective-permute-start.3 = (bf16[32,2,128]{0,1,2:T(2,128)(2,1)S(1)}, bf16[32,2,128]{0,1,2:T(2,128)(2,1)S(1)}, u32[]{:S(2)}, u32[]{:S(2)}) collective-permute-start(bf16[32,2,128]{0,1,2:T(2,128)(2,1)S(1)} %copy.111), channel_id=1, source_target_pairs={{0,1},{1,2},{2,3},{3,4},{4,5},{5,6},{6,7},{7,8},{8,9},{9,10},{10,1... | collective-permute-start | bytes 49160 | tf_op jit(solution)/shard_map/ppermute | solution.py:13
  4.4 4.9 %collective-permute-start.2 = (bf16[32,2,128]{0,1,2:T(2,128)(2,1)S(1)}, bf16[32,2,128]{0,1,2:T(2,128)(2,1)S(1)}, u32[]{:S(2)}, u32[]{:S(2)}) collective-permute-start(bf16[32,2,128]{0,1,2:T(2,128)(2,1)S(1)} %copy.111), channel_id=1, source_target_pairs={{0,2},{1,3},{2,4},{3,5},{4,6},{5,7},{6,8},{7,9},{8,10},{9,11},{10,... | collective-permute-start | bytes 49160 | tf_op jit(solution)/shard_map/ppermute | solution.py:13
  9.3 5.7 %collective-permute-start.1 = (bf16[32,2,128]{0,1,2:T(2,128)(2,1)S(1)}, bf16[32,2,128]{0,1,2:T(2,128)(2,1)S(1)}, u32[]{:S(2)}, u32[]{:S(2)}) collective-permute-start(bf16[32,2,128]{0,1,2:T(2,128)(2,1)S(1)} %copy.111), channel_id=1, source_target_pairs={{0,3},{1,4},{2,5},{3,6},{4,7},{5,8},{6,9},{7,10},{8,11},{9,12},{10... | collective-permute-start | bytes 49160 | tf_op jit(solution)/shard_map/ppermute | solution.py:13
  15.0 2.9 %collective-permute-start = (bf16[32,2,128]{0,1,2:T(2,128)(2,1)S(1)}, bf16[32,2,128]{0,1,2:T(2,128)(2,1)S(1)}, u32[]{:S(2)}, u32[]{:S(2)}) collective-permute-start(bf16[32,2,128]{0,1,2:T(2,128)(2,1)S(1)} %copy.111), channel_id=1, source_target_pairs={{0,4},{1,5},{2,6},{3,7},{4,8},{5,9},{6,10},{7,11},{8,12},{9,13},{1... | collective-permute-start | bytes 49160 | tf_op jit(solution)/shard_map/ppermute | solution.py:13
  18.6 0.7 convert_element_type.22
  19.3 5.6 %collective-permute-done = bf16[32,2,128]{0,1,2:T(2,128)(2,1)S(1)} collective-permute-done((bf16[32,2,128]{0,1,2:T(2,128)(2,1)S(1)}, bf16[32,2,128]{0,1,2:T(2,128)(2,1)S(1)}, u32[]{:S(2)}, u32[]{:S(2)}) %collective-permute-start) | collective-permute-done | bytes 16416 | tf_op jit(solution)/shard_map/ppermute | solution.py:13
  25.0 0.0 collective-permute-done.1
  25.0 0.1 constant_dynamic-update-slice_fusion.3
  25.0 0.0 collective-permute-done.2
  25.0 0.1 constant_dynamic-update-slice_fusion.2
  25.1 0.0 collective-permute-done.3
  25.1 0.1 constant_dynamic-update-slice_fusion.1
  25.2 0.1 constant_dynamic-update-slice_fusion
  25.2 0.1 constant_dynamic-slice_fusion
  25.3 8.8 %gather_fusion = bf16[48,32,2,128]{1,2,3,0:T(2,128)(2,1)} fusion(bf16[32,2,175]{0,1,2:T(2,128)(2,1)S(1)} %constant_dynamic-slice_fusion, s32[48]{0:T(128)S(1)} %fusion.30), kind=kCustom, calls=%fused_computation | custom fusion | bytes 1573440 | tf_op jit(solution)/shard_map/vmap()/gather | solution.py:37
  34.1 4.7 %copy.116 = bf16[48,32,2,128]{3,0,2,1:T(8,128)(2,1)S(1)} copy(bf16[48,32,2,128]{1,2,3,0:T(2,128)(2,1)} %gather_fusion) | data formatting | bytes 1572864 | tf_op jit(solution)/shard_map/vmap()/gather | solution.py:37
  38.8 0.2 fusion.27
  39.0 0.0 copy-start.2
  39.0 0.1 fusion.39
  39.0 6.3 %collective-permute-start.4 = (bf16[32,48,1,128]{3,1,2,0:T(8,128)(2,1)S(1)}, bf16[32,48,1,128]{3,1,2,0:T(8,128)(2,1)S(1)}, u32[]{:S(2)}, u32[]{:S(2)}) collective-permute-start(bf16[32,48,1,128]{3,1,2,0:T(8,128)(2,1)S(1)} %get-tuple-element.11), channel_id=1, source_target_pairs={{0,32},{32,64},{64,96},{96,128},{128,160},{160,192},{192,224},{1,3... | collective-permute-start | bytes 1179656 | tf_op jit(solution)/shard_map/ppermute | solution.py:21
  45.4 1.9 collective-permute-start.5
  47.3 2.8 %collective-permute-done.4 = bf16[32,48,1,128]{3,1,2,0:T(8,128)(2,1)S(1)} collective-permute-done((bf16[32,48,1,128]{3,1,2,0:T(8,128)(2,1)S(1)}, bf16[32,48,1,128]{3,1,2,0:T(8,128)(2,1)S(1)}, u32[]{:S(2)}, u32[]{:S(2)}) %collective-permute-start.4) | collective-permute-done | bytes 393248 | tf_op jit(solution)/shard_map/ppermute | solution.py:21
  50.1 4.4 %collective-permute-done.5 = bf16[32,48,1,128]{3,1,2,0:T(8,128)(2,1)S(1)} collective-permute-done((bf16[32,48,1,128]{3,1,2,0:T(8,128)(2,1)S(1)}, bf16[32,48,1,128]{3,1,2,0:T(8,128)(2,1)S(1)}, u32[]{:S(2)}, u32[]{:S(2)}) %collective-permute-start.5) | collective-permute-done | bytes 393248 | tf_op jit(solution)/shard_map/ppermute | solution.py:24
  54.5 0.7 copy-done.7
  55.2 0.2 pad_maximum_fusion
  55.4 1.9 fusion.38
  57.3 2.0 %copy.117 = bf16[32,48,4,1]{1,0,3,2:T(8,128)(2,1)S(1)} copy(bf16[32,48,4,1]{3,1,2,0:T(8,128)(2,1)} %get-tuple-element.9) | data formatting | bytes 24576 | tf_op jit(solution)/shard_map/slice | solution.py:22
  59.3 2.3 %collective-permute-start.6 = (bf16[32,48,4,1]{1,0,3,2:T(8,128)(2,1)S(1)}, bf16[32,48,4,1]{1,0,3,2:T(8,128)(2,1)S(1)}, u32[]{:S(2)}, u32[]{:S(2)}) collective-permute-start(bf16[32,48,4,1]{1,0,3,2:T(8,128)(2,1)S(1)} %copy.117), channel_id=1, source_target_pairs={{0,1},{1,2},{2,3},{3,4},{4,5},{5,6},{6,7},{7,8},{8,9},{9,10},{10,1... | collective-permute-start | bytes 36872 | tf_op jit(solution)/shard_map/ppermute | solution.py:21
  61.6 1.0 copy.118
  62.6 5.3 %collective-permute-start.7 = (bf16[32,48,4,1]{1,0,3,2:T(8,128)(2,1)S(1)}, bf16[32,48,4,1]{1,0,3,2:T(8,128)(2,1)S(1)}, u32[]{:S(2)}, u32[]{:S(2)}) collective-permute-start(bf16[32,48,4,1]{1,0,3,2:T(8,128)(2,1)S(1)} %copy.118), channel_id=1, source_target_pairs={{1,0},{2,1},{3,2},{4,3},{5,4},{6,5},{7,6},{8,7},{9,8},{10,9},{11,1... | collective-permute-start | bytes 36872 | tf_op jit(solution)/shard_map/ppermute | solution.py:24
  67.9 1.9 copy.119
  69.8 1.9 copy.120
  71.7 4.3 %maximum_bitcast_fusion.1 = bf16[32,48,4,1,130]{4,1,2,0,3:T(8,128)(2,1)S(1)} fusion(bf16[32,48,4,1]{3,1,2,0:T(8,128)(2,1)} %copy.120, bf16[32,48,1,128]{3,1,2,0:T(8,128)(2,1)} %copy-done.7, bf16[32,48,2,128]{3,1,2,0:T(8,128)(2,1)} %copy-done.2, bf16[32,48,1,128]{3,1,2,0:T(8,128)(2,1)} %copy-done.6, bf16[32,48,4,1]{3,1,2,0:T(8,128)(2,1)} %copy.119), kind=kLoop, calls=%fused_computation.25 | loop fusion | flops 7987200 | bytes 3194880 | tf_op jit(solution)/shard_map/broadcast_in_dim | solution.py:48
  76.0 5.8 %copy.135 = bf16[32,48,4,1,130]{1,0,4,2,3:T(8,128)(2,1)} copy(bf16[32,48,4,1,130]{4,1,2,0,3:T(8,128)(2,1)S(1)} %maximum_bitcast_fusion.1) | data formatting | bytes 3194880
  81.8 5.2 %pad.1.clone = bf16[32,48,4,1,136]{1,0,4,2,3:T(8,128)(2,1)} pad(bf16[32,48,4,1,130]{1,0,4,2,3:T(8,128)(2,1)} %copy.135, bf16[]{:T(256)} %constant.26), padding=0_0x0_0x0_0x0_0x0_6 | pad | bytes 3268610 | tf_op jit(solution)/shard_map/broadcast_in_dim | solution.py:48
  87.0 8.6 %copy.123 = bf16[32,48,4,1,8,17]{0,4,5,2,1,3:T(8,128)(2,1)} copy(bf16[32,48,4,1,8,17]{1,0,5,4,2,3:T(8,128)(2,1)} %bitcast.50) | data formatting | bytes 3342336 | tf_op jit(solution)/shard_map/conv_general_dilated | solution.py:47
  95.7 1.4 slice.43
  97.1 13.4 %broadcast_select_fusion.1 = f32[48,2,8,17,32]{4,2,3,1,0:T(8,128)} fusion(pred[8,17]{0,1:T(8,128)(4,1)S(1)} %copy-done.11, bf16[3,3,3,32,32]{4,3,2,1,0:T(8,128)(2,1)S(1)} %bitcast.48, bf16[32,48,4,1,7,2]{0,4,5,2,1,3:T(8,128)(2,1)S(1)} %slice.43, bf16[32,48,4,1,8,17]{0,4,5,2,1,3:T(8,128)(2,1)} %copy.123), kind=kOutput, calls=%fused_computation.24 | convolution fusion | flops 717938688 | bytes 3569800 | tf_op jit(solution)/shard_map/conv_general_dilated | solution.py:47
  110.5 6.3 %copy.124 = f32[48,2,8,17,32]{0,4,3,2,1:T(8,128)} copy(f32[48,2,8,17,32]{4,2,3,1,0:T(8,128)} %broadcast_select_fusion.1) | data formatting | bytes 3342336 | tf_op jit(solution)/shard_map/conv_general_dilated | solution.py:47
  116.8 2.8 %fusion.18 = bf16[32,48,2,128]{1,0,3,2:T(8,128)(2,1)S(1)} fusion(f32[48,2,1,136,32]{0,4,3,1,2:T(8,128)} %bitcast.51, f32[32]{0:T(128)S(1)} %copy-done.8), kind=kLoop, calls=%fused_computation.20 | loop fusion | flops 1179648 | bytes 2359424 | tf_op jit(solution)/shard_map/convert_element_type | solution.py:67
  119.6 1.4 fusion.37
  121.0 3.0 %copy.125 = bf16[32,48,1,128]{3,1,2,0:T(8,128)(2,1)} copy(bf16[32,48,1,128]{1,0,3,2:T(8,128)(2,1)} %get-tuple-element.7) | data formatting | bytes 786432 | tf_op jit(solution)/shard_map/slice | solution.py:22
  123.9 2.5 %collective-permute-start.8 = (bf16[32,48,1,128]{3,1,2,0:T(8,128)(2,1)}, bf16[32,48,1,128]{3,1,2,0:T(8,128)(2,1)}, u32[]{:S(2)}, u32[]{:S(2)}) collective-permute-start(bf16[32,48,1,128]{3,1,2,0:T(8,128)(2,1)} %copy.125), channel_id=1, source_target_pairs={{0,32},{32,64},{64,96},{96,128},{128,160},{160,192},{192,224},{1,3... | collective-permute-start | bytes 1179656 | tf_op jit(solution)/shard_map/ppermute | solution.py:21
  126.4 1.8 copy.126
  128.3 2.0 %collective-permute-start.9 = (bf16[32,48,1,128]{3,1,2,0:T(8,128)(2,1)}, bf16[32,48,1,128]{3,1,2,0:T(8,128)(2,1)}, u32[]{:S(2)}, u32[]{:S(2)}) collective-permute-start(bf16[32,48,1,128]{3,1,2,0:T(8,128)(2,1)} %copy.126), channel_id=1, source_target_pairs={{32,0},{64,32},{96,64},{128,96},{160,128},{192,160},{224,192},{33,... | collective-permute-start | bytes 1179656 | tf_op jit(solution)/shard_map/ppermute | solution.py:24
  130.3 0.9 collective-permute-done.8
  131.2 2.4 %copy.127 = bf16[32,48,1,128]{1,0,3,2:T(8,128)(2,1)S(1)} copy(bf16[32,48,1,128]{3,1,2,0:T(8,128)(2,1)} %collective-permute-done.8) | data formatting | bytes 786432 | tf_op jit(solution)/shard_map/ppermute | solution.py:21
  133.7 4.0 %collective-permute-done.9 = bf16[32,48,1,128]{3,1,2,0:T(8,128)(2,1)} collective-permute-done((bf16[32,48,1,128]{3,1,2,0:T(8,128)(2,1)}, bf16[32,48,1,128]{3,1,2,0:T(8,128)(2,1)}, u32[]{:S(2)}, u32[]{:S(2)}) %collective-permute-start.9) | collective-permute-done | bytes 393248 | tf_op jit(solution)/shard_map/ppermute | solution.py:24
  137.7 3.3 %copy.128 = bf16[32,48,1,128]{1,0,3,2:T(8,128)(2,1)} copy(bf16[32,48,1,128]{3,1,2,0:T(8,128)(2,1)} %collective-permute-done.9) | data formatting | bytes 786432 | tf_op jit(solution)/shard_map/ppermute | solution.py:24
  141.0 0.8 pad_maximum_fusion.3
  141.8 1.9 collective-permute-start.10
  143.7 5.7 %collective-permute-start.11 = (bf16[32,48,4,1]{1,0,3,2:T(8,128)(2,1)S(1)}, bf16[32,48,4,1]{1,0,3,2:T(8,128)(2,1)S(1)}, u32[]{:S(2)}, u32[]{:S(2)}) collective-permute-start(bf16[32,48,4,1]{1,0,3,2:T(8,128)(2,1)S(1)} %get-tuple-element.6), channel_id=1, source_target_pairs={{1,0},{2,1},{3,2},{4,3},{5,4},{6,5},{7,6},{8,7},{9,8},{10,9},{11,1... | collective-permute-start | bytes 36872 | tf_op jit(solution)/shard_map/ppermute | solution.py:24
  149.5 1.0 collective-permute-done.11
  150.5 1.4 maximum_bitcast_fusion
  151.8 3.0 %pad.3 = bf16[32,48,4,1,136]{1,0,4,2,3:T(8,128)(2,1)} pad(bf16[32,48,4,1,130]{1,0,4,2,3:T(8,128)(2,1)S(1)} %maximum_bitcast_fusion, bf16[]{:T(256)} %constant.26), padding=0_0x0_0x0_0x0_0x0_6 | pad | bytes 3268610 | tf_op jit(solution)/shard_map/broadcast_in_dim | solution.py:48
  154.8 8.7 %copy.130 = bf16[32,48,4,1,8,17]{0,4,5,2,1,3:T(8,128)(2,1)} copy(bf16[32,48,4,1,8,17]{1,0,5,4,2,3:T(8,128)(2,1)} %bitcast.49) | data formatting | bytes 3342336 | tf_op jit(solution)/shard_map/conv_general_dilated | solution.py:47
  163.5 1.4 slice.47
  164.9 13.4 %broadcast_select_fusion = f32[48,2,8,17,32]{4,2,3,1,0:T(8,128)} fusion(pred[8,17]{0,1:T(8,128)(4,1)S(1)} %copy-done.11, bf16[3,3,3,32,32]{4,3,2,1,0:T(8,128)(2,1)S(1)} %bitcast.53, bf16[32,48,4,1,7,2]{0,4,5,2,1,3:T(8,128)(2,1)S(1)} %slice.47, bf16[32,48,4,1,8,17]{0,4,5,2,1,3:T(8,128)(2,1)} %copy.130), kind=kOutput, calls=%fused_computation.23 | convolution fusion | flops 717938688 | bytes 3569800 | tf_op jit(solution)/shard_map/conv_general_dilated | solution.py:47
  178.3 6.3 %copy.131 = f32[48,2,8,17,32]{0,4,3,2,1:T(8,128)} copy(f32[48,2,8,17,32]{4,2,3,1,0:T(8,128)} %broadcast_select_fusion) | data formatting | bytes 3342336 | tf_op jit(solution)/shard_map/conv_general_dilated | solution.py:47
  184.6 4.7 %slice.48 = f32[48,2,1,128,32]{0,4,3,1,2:T(8,128)} slice(f32[48,2,1,136,32]{0,4,3,1,2:T(8,128)} %bitcast.52), slice={[0:48], [0:2], [0:1], [0:128], [0:32]} | slice | bytes 3145728 | tf_op jit(solution)/shard_map/conv_general_dilated | solution.py:47
  189.3 3.6 %copy.134 = f32[48,2,1,128,32]{3,0,1,4,2:T(8,128)S(1)} copy(f32[48,2,1,128,32]{0,4,3,1,2:T(8,128)} %slice.48) | data formatting | bytes 3145728
  192.9 0.3 fusion.26
  193.3 1.5 copy.133
  (27 shorter events, 0.1 us)
Async XLA Ops:
  0.0 97.1 %copy-start = (bf16[27,32,32]{2,1,0:T(8,128)(2,1)S(1)}, bf16[27,32,32]{2,1,0:T(8,128)(2,1)}, u32[]{:S(2)}) copy-start(bf16[27,32,32]{2,1,0:T(8,128)(2,1)} %param.10) | copy-start | bytes 165892
  0.9 24.2 %collective-permute-start.3 = (bf16[32,2,128]{0,1,2:T(2,128)(2,1)S(1)}, bf16[32,2,128]{0,1,2:T(2,128)(2,1)S(1)}, u32[]{:S(2)}, u32[]{:S(2)}) collective-permute-start(bf16[32,2,128]{0,1,2:T(2,128)(2,1)S(1)} %copy.111), channel_id=1, source_target_pairs={{0,1},{1,2},{2,3},{3,4},{4,5},{5,6},{6,7},{7,8},{8,9},{9,10},{10,1... | collective-permute-start | bytes 49160 | tf_op jit(solution)/shard_map/ppermute | solution.py:13
  4.4 20.6 %collective-permute-start.2 = (bf16[32,2,128]{0,1,2:T(2,128)(2,1)S(1)}, bf16[32,2,128]{0,1,2:T(2,128)(2,1)S(1)}, u32[]{:S(2)}, u32[]{:S(2)}) collective-permute-start(bf16[32,2,128]{0,1,2:T(2,128)(2,1)S(1)} %copy.111), channel_id=1, source_target_pairs={{0,2},{1,3},{2,4},{3,5},{4,6},{5,7},{6,8},{7,9},{8,10},{9,11},{10,... | collective-permute-start | bytes 49160 | tf_op jit(solution)/shard_map/ppermute | solution.py:13
  9.3 15.6 %collective-permute-start.1 = (bf16[32,2,128]{0,1,2:T(2,128)(2,1)S(1)}, bf16[32,2,128]{0,1,2:T(2,128)(2,1)S(1)}, u32[]{:S(2)}, u32[]{:S(2)}) collective-permute-start(bf16[32,2,128]{0,1,2:T(2,128)(2,1)S(1)} %copy.111), channel_id=1, source_target_pairs={{0,3},{1,4},{2,5},{3,6},{4,7},{5,8},{6,9},{7,10},{8,11},{9,12},{10... | collective-permute-start | bytes 49160 | tf_op jit(solution)/shard_map/ppermute | solution.py:13
  15.0 9.9 %collective-permute-start = (bf16[32,2,128]{0,1,2:T(2,128)(2,1)S(1)}, bf16[32,2,128]{0,1,2:T(2,128)(2,1)S(1)}, u32[]{:S(2)}, u32[]{:S(2)}) collective-permute-start(bf16[32,2,128]{0,1,2:T(2,128)(2,1)S(1)} %copy.111), channel_id=1, source_target_pairs={{0,4},{1,5},{2,6},{3,7},{4,8},{5,9},{6,10},{7,11},{8,12},{9,13},{1... | collective-permute-start | bytes 49160 | tf_op jit(solution)/shard_map/ppermute | solution.py:13
  38.8 18.5 %copy-start.4 = (bf16[48,32,2,128]{3,0,2,1:T(8,128)(2,1)}, bf16[48,32,2,128]{3,0,2,1:T(8,128)(2,1)S(1)}, u32[]{:S(2)}) copy-start(bf16[48,32,2,128]{3,0,2,1:T(8,128)(2,1)S(1)} %copy.116) | copy-start | bytes 2359300
  39.0 15.5 %copy-start.2 = (bf16[32,48,2,128]{3,1,2,0:T(8,128)(2,1)}, bf16[32,48,2,128]{3,1,2,0:T(8,128)(2,1)S(1)}, u32[]{:S(2)}) copy-start(bf16[32,48,2,128]{3,1,2,0:T(8,128)(2,1)S(1)} %fusion.27) | copy-start | bytes 2359300
  39.0 11.0 %collective-permute-start.4 = (bf16[32,48,1,128]{3,1,2,0:T(8,128)(2,1)S(1)}, bf16[32,48,1,128]{3,1,2,0:T(8,128)(2,1)S(1)}, u32[]{:S(2)}, u32[]{:S(2)}) collective-permute-start(bf16[32,48,1,128]{3,1,2,0:T(8,128)(2,1)S(1)} %get-tuple-element.11), channel_id=1, source_target_pairs={{0,32},{32,64},{64,96},{96,128},{128,160},{160,192},{192,224},{1,3... | collective-permute-start | bytes 1179656 | tf_op jit(solution)/shard_map/ppermute | solution.py:21
  45.4 9.1 %collective-permute-start.5 = (bf16[32,48,1,128]{3,1,2,0:T(8,128)(2,1)S(1)}, bf16[32,48,1,128]{3,1,2,0:T(8,128)(2,1)S(1)}, u32[]{:S(2)}, u32[]{:S(2)}) collective-permute-start(bf16[32,48,1,128]{3,1,2,0:T(8,128)(2,1)S(1)} %get-tuple-element.12), channel_id=1, source_target_pairs={{32,0},{64,32},{96,64},{128,96},{160,128},{192,160},{224,192},{33,... | collective-permute-start | bytes 1179656 | tf_op jit(solution)/shard_map/ppermute | solution.py:24
  50.1 4.4 %copy-start.6 = (bf16[32,48,1,128]{3,1,2,0:T(8,128)(2,1)}, bf16[32,48,1,128]{3,1,2,0:T(8,128)(2,1)S(1)}, u32[]{:S(2)}) copy-start(bf16[32,48,1,128]{3,1,2,0:T(8,128)(2,1)S(1)} %collective-permute-done.4) | copy-start | bytes 1179652
  54.5 0.7 copy-start.7
  59.3 8.6 %collective-permute-start.6 = (bf16[32,48,4,1]{1,0,3,2:T(8,128)(2,1)S(1)}, bf16[32,48,4,1]{1,0,3,2:T(8,128)(2,1)S(1)}, u32[]{:S(2)}, u32[]{:S(2)}) collective-permute-start(bf16[32,48,4,1]{1,0,3,2:T(8,128)(2,1)S(1)} %copy.117), channel_id=1, source_target_pairs={{0,1},{1,2},{2,3},{3,4},{4,5},{5,6},{6,7},{7,8},{8,9},{9,10},{10,1... | collective-permute-start | bytes 36872 | tf_op jit(solution)/shard_map/ppermute | solution.py:21
  62.6 7.2 %collective-permute-start.7 = (bf16[32,48,4,1]{1,0,3,2:T(8,128)(2,1)S(1)}, bf16[32,48,4,1]{1,0,3,2:T(8,128)(2,1)S(1)}, u32[]{:S(2)}, u32[]{:S(2)}) collective-permute-start(bf16[32,48,4,1]{1,0,3,2:T(8,128)(2,1)S(1)} %copy.118), channel_id=1, source_target_pairs={{1,0},{2,1},{3,2},{4,3},{5,4},{6,5},{7,6},{8,7},{9,8},{10,9},{11,1... | collective-permute-start | bytes 36872 | tf_op jit(solution)/shard_map/ppermute | solution.py:24
  87.0 10.1 %copy-start.11 = (pred[8,17]{0,1:T(8,128)(4,1)S(1)}, pred[8,17]{0,1:T(8,128)(4,1)}, u32[]{:S(2)}) copy-start(pred[8,17]{0,1:T(8,128)(4,1)} %constant.34) | copy-start | bytes 412
  110.5 6.3 %copy-start.8 = (f32[32]{0:T(128)S(1)}, f32[32]{0:T(128)}, u32[]{:S(2)}) copy-start(f32[32]{0:T(128)} %param.11) | copy-start | bytes 388
  123.9 7.3 %collective-permute-start.8 = (bf16[32,48,1,128]{3,1,2,0:T(8,128)(2,1)}, bf16[32,48,1,128]{3,1,2,0:T(8,128)(2,1)}, u32[]{:S(2)}, u32[]{:S(2)}) collective-permute-start(bf16[32,48,1,128]{3,1,2,0:T(8,128)(2,1)} %copy.125), channel_id=1, source_target_pairs={{0,32},{32,64},{64,96},{96,128},{128,160},{160,192},{192,224},{1,3... | collective-permute-start | bytes 1179656 | tf_op jit(solution)/shard_map/ppermute | solution.py:21
  128.3 9.4 %collective-permute-start.9 = (bf16[32,48,1,128]{3,1,2,0:T(8,128)(2,1)}, bf16[32,48,1,128]{3,1,2,0:T(8,128)(2,1)}, u32[]{:S(2)}, u32[]{:S(2)}) collective-permute-start(bf16[32,48,1,128]{3,1,2,0:T(8,128)(2,1)} %copy.126), channel_id=1, source_target_pairs={{32,0},{64,32},{96,64},{128,96},{160,128},{192,160},{224,192},{33,... | collective-permute-start | bytes 1179656 | tf_op jit(solution)/shard_map/ppermute | solution.py:24
  141.0 9.5 %copy-start.3 = (bf16[32,48,1,128]{1,0,3,2:T(8,128)(2,1)S(1)}, bf16[32,48,1,128]{1,0,3,2:T(8,128)(2,1)}, u32[]{:S(2)}) copy-start(bf16[32,48,1,128]{1,0,3,2:T(8,128)(2,1)} %copy.128) | copy-start | bytes 1179652
  141.8 7.6 %collective-permute-start.10 = (bf16[32,48,4,1]{1,0,3,2:T(8,128)(2,1)S(1)}, bf16[32,48,4,1]{1,0,3,2:T(8,128)(2,1)S(1)}, u32[]{:S(2)}, u32[]{:S(2)}) collective-permute-start(bf16[32,48,4,1]{1,0,3,2:T(8,128)(2,1)S(1)} %get-tuple-element.5), channel_id=1, source_target_pairs={{0,1},{1,2},{2,3},{3,4},{4,5},{5,6},{6,7},{7,8},{8,9},{9,10},{10,1... | collective-permute-start | bytes 36872 | tf_op jit(solution)/shard_map/ppermute | solution.py:21
  143.7 6.7 %collective-permute-start.11 = (bf16[32,48,4,1]{1,0,3,2:T(8,128)(2,1)S(1)}, bf16[32,48,4,1]{1,0,3,2:T(8,128)(2,1)S(1)}, u32[]{:S(2)}, u32[]{:S(2)}) collective-permute-start(bf16[32,48,4,1]{1,0,3,2:T(8,128)(2,1)S(1)} %get-tuple-element.6), channel_id=1, source_target_pairs={{1,0},{2,1},{3,2},{4,3},{5,4},{6,5},{7,6},{8,7},{9,8},{10,9},{11,1... | collective-permute-start | bytes 36872 | tf_op jit(solution)/shard_map/ppermute | solution.py:24
  154.8 10.1 %copy-start.10 = (bf16[27,32,32]{2,1,0:T(8,128)(2,1)S(1)}, bf16[27,32,32]{2,1,0:T(8,128)(2,1)}, u32[]{:S(2)}) copy-start(bf16[27,32,32]{2,1,0:T(8,128)(2,1)} %param.12) | copy-start | bytes 165892
  184.6 10.1 %copy-start.1 = (bf16[27,32,32]{2,1,0:T(8,128)(2,1)S(1)}, bf16[27,32,32]{2,1,0:T(8,128)(2,1)}, u32[]{:S(2)}) copy-start(bf16[27,32,32]{2,1,0:T(8,128)(2,1)} %param.10) | copy-start | bytes 165892
  189.3 3.6 %copy-start.5 = (bf16[48,32,2,128]{3,0,2,1:T(8,128)(2,1)S(1)}, bf16[48,32,2,128]{3,0,2,1:T(8,128)(2,1)}, u32[]{:S(2)}) copy-start(bf16[48,32,2,128]{3,0,2,1:T(8,128)(2,1)} %copy-done.4) | copy-start | bytes 2359300
  189.3 3.6 %copy-start.9 = (f32[32]{0:T(128)S(1)}, f32[32]{0:T(128)}, u32[]{:S(2)}) copy-start(f32[32]{0:T(128)} %param.13) | copy-start | bytes 388
where the time goes:
time: 196 us; the launch traced here: 195 us
  local copies, waits for them, and re-layouts  92.7 us (47%)
  starting transfers between devices  44.9 us (23%)
  matrix products  26.8 us (14%)
  waiting for transfers between devices  18.7 us (10%)
  other arithmetic  10.7 us (5%)
    conv_general_dilated x7, local copies, waits for them, and re-layouts, convolve(): lax.conv_general_dilated(padded[None], kernel, (1, 1, 1), ((1, 1), (0, 0)...  37.5 us
    conv_general_dilated x2, matrix products, convolve(): lax.conv_general_dilated(padded[None], kernel, (1, 1, 1), ((1, 1), (0, 0)...  26.8 us
    ppermute x4, starting transfers between devices, passed_along(): return lax.ppermute(shard, axis, pairs)  17 us
    ppermute x4, starting transfers between devices, with_halo(): lax.ppermute(lax.slice_in_dim(block, 0, width, axis=dim), axis, backward)  14.9 us
    gather x2, local copies, waits for them, and re-layouts, one_disparity(): lax.dynamic_slice_in_dim(window, disparities - 1 - disparity, width, 2)  13.5 us
    ppermute x4, starting transfers between devices, with_halo(): lax.ppermute(lax.slice_in_dim(block, block.shape[dim] - width, None, axis...  13 us
    unnamed x31, local copies, waits for them, and re-layouts  11.3 us
    ppermute x4, waiting for transfers between devices, with_halo(): lax.ppermute(lax.slice_in_dim(block, 0, width, axis=dim), axis, backward)  9.41 us
  transfers between devices with their start and end apart: 12, of which 6 were waited for; matrix products, arithmetic and copies ran while one was open for 4% of the time, Pallas kernels for 0%

commit v1 on v0

v1 whole, which is shorter than its diff:
```python
import jax
import jax.numpy as jnp
from jax import lax
from jax.experimental import pallas as pl
from jax.experimental.pallas import tpu as pltpu
from jax.sharding import PartitionSpec as P

C = 32
D = 48
RH = 2
CW = 128
VR = RH + 4
HR = RH + 2
VD = VR * C
HD = HR * C
OD = RH * C
KK = 768
F32 = jnp.float32
BF16 = jnp.bfloat16
LIMIT = 50 * 1024 * 1024
VMEM = pl.BlockSpec(memory_space=pltpu.VMEM)
SMEM = pl.BlockSpec(memory_space=pltpu.SMEM)


def iota(shape, dim):
    return lax.broadcasted_iota(jnp.int32, shape, dim)


def prepare(w1_ref, w2_ref, b_ref, t1_ref, t2_ref, c1_ref, c2_ref, sel_ref, idp_ref, tmp):
    zero = jnp.zeros((C, C), F32)
    for e in range(3):
        one = {(a, b): w1_ref[9 * a + 3 * b + e].astype(F32) for a in range(3) for b in range(3)}
        two = {(a, b): w2_ref[9 * a + 3 * b + e].astype(F32) for a in range(3) for b in range(3)}
        for d in range(2):
            for r in range(HR):
                parts = [one.get((dl - d, rl - r), zero) for dl in range(4) for rl in range(VR)]
                row = jnp.concatenate(parts, axis=1)
                t1_ref[e, (d * HR + r) * C : (d * HR + r + 1) * C, :] = row.astype(BF16)
        for d in range(4):
            for h in range(RH):
                parts = [two.get((dl - d, rl - h), zero) for dl in range(6) for rl in range(HR)]
                for q in range(6):
                    tmp[q, pl.ds(d * RH + h, C, stride=8), :] = jnp.concatenate(
                        parts[4 * q : 4 * q + 4], axis=1
                    )
        for q in range(6):
            t2_ref[e, :, q * CW : (q + 1) * CW] = tmp[q].astype(BF16)
    for p in range(8):
        c1_ref[p * C : (p + 1) * C, :] = b_ref[0]
        c2_ref[pl.ds(p, C, stride=8), :] = b_ref[1]
    lane = iota((128, 128), 1)
    src = iota((128, 128), 0)
    d = lane // 2
    used = d < D
    left = (lane % 2 == 1) & used
    right = (lane % 2 == 0) & used
    right_of = (
        ((3, 47 - d), (2, 47 - d)),
        ((3, 48 - d), (3, 111 - d)),
        ((1, 48 - d), (3, 112 - d)),
    )
    left_of = (((3, 50), (0, 127)), ((3, 51), (3, 114)), ((0, 0), (3, 115)))
    for e in range(3):
        for which, table in ((0, right_of), (1, left_of)):
            for t in range(4):
                hit = jnp.zeros((128, 128), jnp.bool_)
                for mask, (tile, place) in zip((left, right), table[e]):
                    if tile == t:
                        hit = hit | (mask & (src == place))
                g = 2 * e + which
                sel_ref[t * 128 : (t + 1) * 128, g * 128 : (g + 1) * 128] = jnp.where(
                    hit, 1.0, 0.0
                ).astype(BF16)
    out = iota((256, 256), 0)
    inn = iota((256, 256), 1)
    idp_ref[...] = jnp.where(inn == (out % 8) * C + out // 8, 1.0, 0.0).astype(BF16)


def prepared(weight_one, weight_two, bias):
    return pl.pallas_call(
        prepare,
        out_shape=(
            jax.ShapeDtypeStruct((3, 256, KK), BF16),
            jax.ShapeDtypeStruct((3, 256, KK), BF16),
            jax.ShapeDtypeStruct((256, CW), F32),
            jax.ShapeDtypeStruct((256, CW), F32),
            jax.ShapeDtypeStruct((512, 768), BF16),
            jax.ShapeDtypeStruct((256, 256), BF16),
        ),
        in_specs=[VMEM] * 3,
        out_specs=[VMEM] * 6,
        scratch_shapes=[pltpu.VMEM((6, 256, CW), F32)],
        compiler_params=pltpu.CompilerParams(vmem_limit_bytes=LIMIT),
        name="prepare",
    )(weight_one, weight_two, bias)


def cut(ids_ref, off_ref, r4, r3, r2, xl, xo, xr, out_ref, tiles):
    col = ids_ref[1]
    last = ids_ref[3] - 1
    o = off_ref[0]

    def scalar_of(ref):
        v = ref[128:144, :].astype(F32)
        return jnp.max(v[0:1] * 8.0 + v[1:2]).astype(jnp.int32)

    o_l = scalar_of(xl)
    o_r = scalar_of(xr)
    dst = iota((64, 64), 0)
    src = iota((64, 64), 1)
    perm = jnp.where(src == (dst % C) * RH + dst // C, 1.0, 0.0).astype(BF16)

    def rows(x):
        return jnp.dot(perm, x, preferred_element_type=F32)

    for t, x in enumerate((r4[...], r3[...], r2[...], xl[64:128, :], xo[64:128, :])):
        keep = (col + (t - 4) >= 0).astype(F32)
        tiles[t] = rows(x) * keep
    tiles[5] = rows(xr[64:128, :])
    lane = iota((64, CW), 1)

    def window(start):
        t = start // CW
        s = start % CW
        back = (CW - s) % CW
        a = tiles[t]
        b = tiles[t + 1]
        return t, s, back, pltpu.roll(jnp.where(lane < s, b, a), back, 1)

    t, s, back, one = window(464 - o)
    two = pltpu.roll(jnp.where(lane < s, tiles[t + 2], tiles[t + 1]), back, 1)
    wl = window(463 - o_l)[3]
    wr = window(529 - o_r)[3]
    near = rows(xl[0:64, :]) * (col > 0).astype(F32)
    far = rows(xr[0:64, :]) * (col < last).astype(F32)
    border = jnp.where(lane < 50, wl, jnp.where(lane < 52, pltpu.roll(near, 52, 1), wr))
    border = jnp.where((lane < 114), border, pltpu.roll(far, 114, 1))
    border = jnp.where((lane < 116) & ((lane < 52) | (lane >= 64)), border, 0.0)
    out_ref[0:64, :] = rows(xo[0:64, :]).astype(BF16)
    out_ref[64:128, :] = one.astype(BF16)
    out_ref[128:192, :] = two.astype(BF16)
    out_ref[192:256, :] = border.astype(BF16)


def windows(ids, offsets, r4, r3, r2, xl, xo, xr):
    return pl.pallas_call(
        cut,
        out_shape=jax.ShapeDtypeStruct((256, CW), BF16),
        in_specs=[SMEM, SMEM] + [VMEM] * 6,
        out_specs=VMEM,
        scratch_shapes=[pltpu.VMEM((6, 64, CW), F32)],
        name="windows",
    )(ids, offsets, r4, r3, r2, xl, xo, xr)


def aggregate(
    ids_ref, own, pair, cross, t1, t2, c1, c2, sel, idp, out_ref, vol, vown, hid, zcol, hcol
):
    row = ids_ref[0]
    col = ids_ref[1]
    rows_last = ids_ref[2] - 1
    cols_last = ids_ref[3] - 1
    odd = row % 2 == 1
    no_up = row == 0
    no_down = row == rows_last

    def tile(t):
        part = slice(t * 64, t * 64 + 64)
        p = pair[part, :]
        x = cross[part, :]
        up = jnp.where(odd, p, x)
        down = jnp.where(odd, x, p)
        up = jnp.where(no_up, jnp.zeros_like(up), up)
        down = jnp.where(no_down, jnp.zeros_like(down), down)
        return jnp.concatenate([up, own[part, :], down], axis=0)

    left, win0, win1, edge = (tile(t) for t in range(4))

    sources = jnp.concatenate([left, win0, win1, edge], axis=1)
    picked = jnp.dot(sources, sel[...], preferred_element_type=F32)
    cells = []
    for e in range(3):
        r = picked[:, (2 * e) * CW : (2 * e + 1) * CW]
        lft = picked[:, (2 * e + 1) * CW : (2 * e + 2) * CW]
        cells.append(r * lft)
    zcol[...] = cells[1]
    acc = jnp.zeros((HD, CW), F32)
    zeros = jnp.zeros((VD, CW), BF16)
    for e in range(3):
        z = cells[e]
        rhs = jnp.concatenate(
            [
                pltpu.roll(z, 2, 1).astype(BF16),
                z.astype(BF16),
                pltpu.roll(z, CW - 2, 1).astype(BF16),
                zeros,
            ],
            axis=0,
        )
        acc += jnp.dot(t1[e, 0:HD, :], rhs, preferred_element_type=F32)
    h = jnp.maximum(acc + c1[0:HD, :], 0.0)
    lane = iota((HD, CW), 1)
    hrow = iota((HD, CW), 0) // C
    gone = (no_up & (hrow == 0)) | (no_down & (hrow == HR - 1))
    gone = gone | ((col == 0) & (lane % 2 == 1)) | ((col == cols_last) & (lane % 2 == 0))
    hcol[...] = jnp.where(gone, 0.0, h)

    vlane = iota((VD, CW), 1)
    first = vlane == 0
    lastl = vlane == CW - 1
    l1 = left.astype(F32)
    l0 = pltpu.roll(l1, 1, 1)
    l2 = pltpu.roll(l1, CW - 1, 1)
    w0 = win0.astype(F32)
    w1 = win1.astype(F32)
    pad = jnp.zeros((VD, CW), BF16)
    for e in range(3):
        vol[e, 0:VD, :] = pad
        vol[e, (D + 1) * VD : (D + 2) * VD, :] = pad
        hid[e, 0:HD, :] = pad[0:HD]
        hid[e, (D + 1) * HD : (D + 2) * HD, :] = pad[0:HD]

    def shifted(k):
        return pltpu.roll(jnp.where(vlane < k, w1, w0), (CW - k) % CW, 1)

    def one_disparity(d, carry):
        s0, s1 = carry
        s2 = s1
        s1 = s0
        s0 = shifted(D - 1 - d)
        border = pltpu.roll(zcol[...], (2 * CW - 1 - 2 * d) % CW, 1)
        base = pl.multiple_of((d + 1) * VD, VD)
        mid = (l1 * s1).astype(BF16)
        vol[0, pl.ds(base, VD), :] = jnp.where(first, border, l0 * s0).astype(BF16)
        vol[1, pl.ds(base, VD), :] = mid
        vol[2, pl.ds(base, VD), :] = jnp.where(lastl, border, l2 * s2).astype(BF16)
        vown[pl.ds(pl.multiple_of(d * OD, OD), OD), :] = mid[2 * C : 4 * C]
        return s0, s1

    lax.fori_loop(0, D, one_disparity, (shifted(D), shifted(D + 1)))

    hl = iota((256, CW), 1)
    hr = (iota((256, CW), 0) // C) % HR
    dead = (no_up & (hr == 0)) | (no_down & (hr == HR - 1))
    hfirst = hl == 0
    hlast = hl == CW - 1

    def conv_one(j, carry):
        d0 = j * 4
        acc = jnp.zeros((256, 256), F32)
        for e in range(3):
            a = vol[e, pl.ds(pl.multiple_of(d0 * VD, VD), KK), :]
            b = vol[e, pl.ds(pl.multiple_of((d0 + 2) * VD, VD), KK), :]
            acc += jnp.dot(t1[e], jnp.concatenate([a, b], axis=1), preferred_element_type=F32)
        for i in range(2):
            h = jnp.maximum(acc[:, i * CW : (i + 1) * CW] + c1[...], 0.0)
            h = jnp.where(dead, 0.0, h)
            d = d0 + 2 * i
            border = jnp.concatenate(
                [
                    pltpu.roll(hcol[...], (2 * CW - 1 - 2 * d) % CW, 1),
                    pltpu.roll(hcol[...], (2 * CW - 3 - 2 * d) % CW, 1),
                ],
                axis=0,
            )
            base = pl.multiple_of((d + 1) * HD, HD)
            hid[0, pl.ds(base, 256), :] = jnp.where(hfirst, border, pltpu.roll(h, 1, 1)).astype(BF16)
            hid[1, pl.ds(base, 256), :] = h.astype(BF16)
            hid[2, pl.ds(base, 256), :] = jnp.where(
                hlast, border, pltpu.roll(h, CW - 1, 1)
            ).astype(BF16)
        return carry

    lax.fori_loop(0, D // 4, conv_one, 0)

    def conv_two(j, carry):
        d0 = j * 8
        va = vown[pl.ds(pl.multiple_of(d0 * OD, OD), 256), :]
        vb = vown[pl.ds(pl.multiple_of((d0 + 4) * OD, OD), 256), :]
        acc = jnp.dot(idp[...], jnp.concatenate([va, vb], axis=1), preferred_element_type=F32)
        for e in range(3):
            a = hid[e, pl.ds(pl.multiple_of(d0 * HD, HD), KK), :]
            b = hid[e, pl.ds(pl.multiple_of((d0 + 4) * HD, HD), KK), :]
            acc += jnp.dot(t2[e], jnp.concatenate([a, b], axis=1), preferred_element_type=F32)
        a = (acc[:, 0:CW] + c2[...]).reshape(C, 8, CW)
        b = (acc[:, CW:] + c2[...]).reshape(C, 8, CW)
        out_ref[:, pl.ds(pl.multiple_of(j * 16, 16), 16), :] = jnp.concatenate(
            [a, b], axis=1
        ).astype(BF16)
        return carry

    lax.fori_loop(0, D // 8, conv_two, 0)


def aggregated(ids, own, pair, cross, t1, t2, c1, c2, sel, idp):
    return pl.pallas_call(
        aggregate,
        out_shape=jax.ShapeDtypeStruct((C, D * RH, CW), BF16),
        in_specs=[SMEM] + [VMEM] * 9,
        out_specs=VMEM,
        scratch_shapes=[
            pltpu.VMEM((3, (D + 2) * VD, CW), BF16),
            pltpu.VMEM((D * OD, CW), BF16),
            pltpu.VMEM((3, (D + 2) * HD, CW), BF16),
            pltpu.VMEM((VD, CW), F32),
            pltpu.VMEM((HD, CW), F32),
        ],
        compiler_params=pltpu.CompilerParams(vmem_limit_bytes=LIMIT),
        name="aggregate",
    )(ids, own, pair, cross, t1, t2, c1, c2, sel, idp)


def ring(x, axis, by):
    n = lax.axis_size(axis)
    return lax.ppermute(x, axis, [(i, (i + by) % n) for i in range(n)])


def swap(x, axis, first):
    n = lax.axis_size(axis)
    pairs = []
    for i in range(first, n + first, 2):
        a, b = i % n, (i + 1) % n
        pairs += [(a, b), (b, a)]
    return lax.ppermute(x, axis, pairs)


def body(left, right, offsets, weight_one, bias_one, weight_two, bias_two):
    ids = jnp.stack(
        [
            lax.axis_index("rows"),
            lax.axis_index("cols"),
            lax.axis_size("rows"),
            lax.axis_size("cols"),
        ]
    ).astype(jnp.int32)
    bias = jnp.broadcast_to(jnp.stack([bias_one, bias_two])[:, :, None], (2, C, CW))
    r = right.reshape(C * RH, CW)
    l = left.reshape(C * RH, CW)
    o = offsets[0]
    place = jnp.arange(16, dtype=jnp.int32)[:, None]
    code = jnp.where(place == 0, o // 8, jnp.where(place == 1, o % 8, 0)).astype(BF16)
    x = jnp.concatenate([l, r, jnp.broadcast_to(code, (16, CW))], axis=0)
    r4 = ring(r, "cols", 4)
    r3 = ring(r, "cols", 3)
    r2 = ring(r, "cols", 2)
    xl = ring(x, "cols", 1)
    xr = ring(x, "cols", -1)
    ready = prepared(weight_one, weight_two, bias)
    own = windows(ids, offsets, r4, r3, r2, xl, x, xr)
    pair = swap(own, "rows", 0)
    cross = swap(own, "rows", 1)
    out = aggregated(ids, own, pair, cross, *ready)
    return out.reshape(C, D, RH, CW)


def solution(mesh):
    return jax.shard_map(
        body,
        mesh=mesh,
        in_specs=(P(None, "rows", "cols"), P(None, "rows", "cols"), P("cols"), P(), P(), P(), P()),
        out_specs=P(None, None, "rows", "cols"),
        check_vma=False,
    )
```

time: 196 us -> 50.6 us (0.26)
  the two profiles are of different devices: /device:TPU:19 before, /device:TPU:1 now
where the time goes in v1:
time: 50.6 us; the launch traced here: 50.3 us
  Pallas kernels  20.6 us (41%)
  starting transfers between devices  17.3 us (34%)
  waiting for transfers between devices  5.5 us (11%)
  local copies, waits for them, and re-layouts  4.03 us (8%)
  other arithmetic  2.12 us (4%)
  between operations  0.79 us (2%)
    pallas_call x1, Pallas kernels, aggregated(): pl.pallas_call(aggregate, out_shape=jax.ShapeDtypeStruct((C, D * RH, CW),...  17.9 us
    ppermute x5, starting transfers between devices, ring(): return lax.ppermute(x, axis, [(i, (i + by) % n) for i in range(n)])  13.5 us
    ppermute x5, waiting for transfers between devices, ring(): return lax.ppermute(x, axis, [(i, (i + by) % n) for i in range(n)])  5.49 us
    unnamed x20, local copies, waits for them, and re-layouts  3.95 us
    ppermute x2, starting transfers between devices, swap(): return lax.ppermute(x, axis, pairs)  3.76 us
    pallas_call x1, Pallas kernels, windows(): pl.pallas_call(cut, out_shape=jax.ShapeDtypeStruct((256, CW), BF16), in_s...  1.76 us
  transfers between devices with their start and end apart: 7, of which 2 were waited for; matrix products, arithmetic and copies ran while one was open for 4% of the time, Pallas kernels for 2%

profile of v1, /device:TPU:1, one launch (start us, length us, event | category | flops | bytes accessed | tf_op | source)
XLA Modules:
  0.0 50.3 jit_solution(11959166752039530450)
XLA Ops:
  0.0 3.8 %collective-permute-start.2 = (bf16[64,128]{1,0:T(8,128)(2,1)}, bf16[64,128]{1,0:T(8,128)(2,1)S(1)}, u32[]{:S(2)}, u32[]{:S(2)}) collective-permute-start(bf16[64,128]{1,0:T(8,128)(2,1)} %bitcast.13), channel_id=1, source_target_pairs={{0,2},{1,3},{2,4},{3,5},{4,6},{5,7},{6,8},{7,9},{8,10},{9,11},{10,... | collective-permute-start | bytes 49160 | tf_op jit(solution)/shard_map/ppermute | solution.py:315
  3.8 4.7 %collective-permute-start.1 = (bf16[64,128]{1,0:T(8,128)(2,1)}, bf16[64,128]{1,0:T(8,128)(2,1)S(1)}, u32[]{:S(2)}, u32[]{:S(2)}) collective-permute-start(bf16[64,128]{1,0:T(8,128)(2,1)} %bitcast.14), channel_id=1, source_target_pairs={{0,3},{1,4},{2,5},{3,6},{4,7},{5,8},{6,9},{7,10},{8,11},{9,12},{10... | collective-permute-start | bytes 49160 | tf_op jit(solution)/shard_map/ppermute | solution.py:315
  8.5 0.9 %collective-permute-start = (bf16[64,128]{1,0:T(8,128)(2,1)}, bf16[64,128]{1,0:T(8,128)(2,1)S(1)}, u32[]{:S(2)}, u32[]{:S(2)}) collective-permute-start(bf16[64,128]{1,0:T(8,128)(2,1)} %bitcast.15), channel_id=1, source_target_pairs={{0,4},{1,5},{2,6},{3,7},{4,8},{5,9},{6,10},{7,11},{8,12},{9,13},{1... | collective-permute-start | bytes 49160 | tf_op jit(solution)/shard_map/ppermute | solution.py:315
  10.1 0.8 %maximum_maximum_fusion.xo = bf16[144,128]{1,0:T(8,128)(2,1)S(1)} fusion(bf16[64,128]{1,0:T(8,128)(2,1)} %bitcast.16, bf16[64,128]{1,0:T(8,128)(2,1)} %bitcast.12, bf16[144]{0:T(256)(128)(2,1)S(1)} %pad.4.clone), kind=kLoop, calls=%fused_computation | loop fusion | flops 110592 | bytes 69920 | tf_op jit(solution)/shard_map/concatenate | solution.py:342
  10.9 0.0 copy-start.4
  10.9 4.1 %collective-permute-start.4 = (bf16[144,128]{1,0:T(8,128)(2,1)S(1)}, bf16[144,128]{1,0:T(8,128)(2,1)S(1)}, u32[]{:S(2)}, u32[]{:S(2)}) collective-permute-start(bf16[144,128]{1,0:T(8,128)(2,1)S(1)} %maximum_maximum_fusion.xo), channel_id=1, source_target_pairs={{0,31},{1,0},{2,1},{3,2},{4,3},{5,4},{6,5},{7,6},{8,7},{9,8},{10,9... | collective-permute-start | bytes 110600 | tf_op jit(solution)/shard_map/ppermute | solution.py:315
  15.1 0.0 collective-permute-start.3
  15.1 0.6 %pad_add_fusion.ids_ref = s32[4]{0:T(128)} fusion(s32[1]{0:T(128)} %constant.35.clone.1, s32[1]{0:T(128)} %constant.34.clone.1, s32[1]{0:T(128)} %bitcast.1, s32[1]{0:T(128)} %bitcast), kind=kLoop, calls=%fused_computation.5 | loop fusion | flops 12 | bytes 32 | tf_op jit(solution)/shard_map/stack | solution.py:328
  15.7 0.0 collective-permute-done.2.r2
  15.7 0.0 copy-start.7
  15.7 0.0 collective-permute-done.1.r3
  15.7 0.0 copy-start.8
  15.7 1.8 %collective-permute-done.r4 = bf16[64,128]{1,0:T(8,128)(2,1)S(1)} collective-permute-done((bf16[64,128]{1,0:T(8,128)(2,1)}, bf16[64,128]{1,0:T(8,128)(2,1)S(1)}, u32[]{:S(2)}, u32[]{:S(2)}) %collective-permute-start) | collective-permute-done | bytes 16416 | tf_op jit(solution)/shard_map/ppermute | solution.py:315
  17.5 0.0 copy-start.9
  17.5 0.0 collective-permute-done.4.xr
  17.5 0.0 copy-start.5
  17.5 3.7 %collective-permute-done.3.xl = bf16[144,128]{1,0:T(8,128)(2,1)S(1)} collective-permute-done((bf16[144,128]{1,0:T(8,128)(2,1)S(1)}, bf16[144,128]{1,0:T(8,128)(2,1)S(1)}, u32[]{:S(2)}, u32[]{:S(2)}) %collective-permute-start.3) | collective-permute-done | bytes 36896 | tf_op jit(solution)/shard_map/ppermute | solution.py:315
  21.2 0.0 copy-done.4
  21.2 0.0 copy-done.7
  21.2 0.0 copy-done.8
  21.2 0.0 copy-done.9
  21.2 0.0 copy-done.5
  21.2 0.0 copy-start.6
  21.2 0.6 %copy-done.6 = bf16[144,128]{1,0:T(8,128)(2,1)} copy-done((bf16[144,128]{1,0:T(8,128)(2,1)}, bf16[144,128]{1,0:T(8,128)(2,1)S(1)}, u32[]{:S(2)}) %copy-start.6) | copy-done | bytes 36888
  21.8 1.8 %windows.1.own = bf16[256,128]{1,0:T(8,128)(2,1)} custom-call(s32[4]{0:T(128)} %pad_add_fusion.ids_ref, s32[1]{0:T(128)} %copy.8.off_ref, bf16[64,128]{1,0:T(8,128)(2,1)} %copy-done.9, bf16[64,128]{1,0:T(8,128)(2,1)} %copy-done.8, bf16[64,128]{1,0:T(8,128)(2,1)} %copy-done.7, bf16[144,128]{1,0:T(8,128)(2,1)} %copy-done.6, bf16[144,128]{1,0:T(8,128)(2,1)} %copy-done.4, ...), custom_call_target="tpu_custom_call" | custom-call | tf_op jit(solution)/shard_map/windows/pallas_call | solution.py:146
  23.6 3.8 %collective-permute-start.6 = (bf16[256,128]{1,0:T(8,128)(2,1)}, bf16[256,128]{1,0:T(8,128)(2,1)S(1)}, u32[]{:S(2)}, u32[]{:S(2)}) collective-permute-start(bf16[256,128]{1,0:T(8,128)(2,1)} %windows.1.own), channel_id=1, source_target_pairs={{32,64},{64,32},{96,128},{128,96},{160,192},{192,160},{224,0},{0,2... | collective-permute-start | bytes 196616 | tf_op jit(solution)/shard_map/ppermute | solution.py:324
  27.4 0.0 collective-permute-start.5
  27.4 0.7 %pad_maximum_fusion = f32[2,32]{1,0:T(2,128)S(1)} fusion(f32[1,32]{1,0:T(1,128)} %bitcast.17, f32[1,32]{1,0:T(1,128)} %bitcast.18), kind=kLoop, calls=%fused_computation.3 | loop fusion | flops 64 | bytes 512 | tf_op jit(solution)/shard_map/stack | solution.py:336
  28.0 0.1 broadcast_in_dim.25.b_ref
  28.1 0.0 copy-start.1
  28.1 0.9 %copy-done.1 = bf16[27,32,32]{2,1,0:T(8,128)(2,1)S(1)} copy-done((bf16[27,32,32]{2,1,0:T(8,128)(2,1)S(1)}, bf16[27,32,32]{2,1,0:T(8,128)(2,1)}, u32[]{:S(2)}) %copy-start.1) | copy-done | bytes 55320
  29.1 0.0 copy-start.2
  29.1 0.9 %copy-done.2 = bf16[27,32,32]{2,1,0:T(8,128)(2,1)S(1)} copy-done((bf16[27,32,32]{2,1,0:T(8,128)(2,1)S(1)}, bf16[27,32,32]{2,1,0:T(8,128)(2,1)}, u32[]{:S(2)}) %copy-start.2) | copy-done | bytes 55320
  30.0 1.0 %prepare.1 = (bf16[3,256,768]{2,1,0:T(8,128)(2,1)S(1)}, bf16[3,256,768]{2,1,0:T(8,128)(2,1)S(1)}, f32[256,128]{1,0:T(8,128)S(1)}, f32[256,128]{1,0:T(8,128)S(1)}...) custom-call(bf16[27,32,32]{2,1,0:T(8,128)(2,1)S(1)} %copy-done.1, bf16[27,32,32]{2,1,0:T(8,128)(2,1)S(1)} %copy-done.2, ...), custom_call_target="tpu_custom_call" | custom-call | tf_op jit(solution)/shard_map/prepare/pallas_call | solution.py:80
  31.0 0.0 collective-permute-done.6.cross
  31.0 0.0 collective-permute-done.5.pair
  31.0 0.0 copy-start
  31.0 0.8 %copy-done = bf16[256,128]{1,0:T(8,128)(2,1)S(1)} copy-done((bf16[256,128]{1,0:T(8,128)(2,1)S(1)}, bf16[256,128]{1,0:T(8,128)(2,1)}, u32[]{:S(2)}) %copy-start) | copy-done | bytes 65560
  31.8 0.0 copy-start.3
  31.8 0.6 %copy-done.3 = s32[4]{0:T(128)S(1)} copy-done((s32[4]{0:T(128)S(1)}, s32[4]{0:T(128)}, u32[]{:S(2)}) %copy-start.3) | copy-done | bytes 40
  32.4 17.9 %aggregate.1 = bf16[32,96,128]{2,1,0:T(8,128)(2,1)} custom-call(s32[4]{0:T(128)S(1)} %copy-done.3, bf16[256,128]{1,0:T(8,128)(2,1)S(1)} %copy-done, bf16[256,128]{1,0:T(8,128)(2,1)S(1)} %collective-permute-done.5.pair, bf16[256,128]{1,0:T(8,128)(2,1)S(1)} %collective-permute-done.6.cross, bf16[3,256,768]{2,1,0:T(8,128)(2,1)S(1)} %get-tuple-element.11.t1, ...), custom_call_target="tpu_custom_call" | custom-call | tf_op jit(solution)/shard_map/aggregate/pallas_call | solution.py:296
  (2 shorter events, 0.0 us)
Async XLA Ops:
  0.0 15.7 %collective-permute-start.2 = (bf16[64,128]{1,0:T(8,128)(2,1)}, bf16[64,128]{1,0:T(8,128)(2,1)S(1)}, u32[]{:S(2)}, u32[]{:S(2)}) collective-permute-start(bf16[64,128]{1,0:T(8,128)(2,1)} %bitcast.13), channel_id=1, source_target_pairs={{0,2},{1,3},{2,4},{3,5},{4,6},{5,7},{6,8},{7,9},{8,10},{9,11},{10,... | collective-permute-start | bytes 49160 | tf_op jit(solution)/shard_map/ppermute | solution.py:315
  3.8 11.9 %collective-permute-start.1 = (bf16[64,128]{1,0:T(8,128)(2,1)}, bf16[64,128]{1,0:T(8,128)(2,1)S(1)}, u32[]{:S(2)}, u32[]{:S(2)}) collective-permute-start(bf16[64,128]{1,0:T(8,128)(2,1)} %bitcast.14), channel_id=1, source_target_pairs={{0,3},{1,4},{2,5},{3,6},{4,7},{5,8},{6,9},{7,10},{8,11},{9,12},{10... | collective-permute-start | bytes 49160 | tf_op jit(solution)/shard_map/ppermute | solution.py:315
  8.5 9.0 %collective-permute-start = (bf16[64,128]{1,0:T(8,128)(2,1)}, bf16[64,128]{1,0:T(8,128)(2,1)S(1)}, u32[]{:S(2)}, u32[]{:S(2)}) collective-permute-start(bf16[64,128]{1,0:T(8,128)(2,1)} %bitcast.15), channel_id=1, source_target_pairs={{0,4},{1,5},{2,6},{3,7},{4,8},{5,9},{6,10},{7,11},{8,12},{9,13},{1... | collective-permute-start | bytes 49160 | tf_op jit(solution)/shard_map/ppermute | solution.py:315
  10.9 10.3 %copy-start.4 = (bf16[144,128]{1,0:T(8,128)(2,1)}, bf16[144,128]{1,0:T(8,128)(2,1)S(1)}, u32[]{:S(2)}) copy-start(bf16[144,128]{1,0:T(8,128)(2,1)S(1)} %maximum_maximum_fusion.xo) | copy-start | bytes 110596
  10.9 6.5 %collective-permute-start.4 = (bf16[144,128]{1,0:T(8,128)(2,1)S(1)}, bf16[144,128]{1,0:T(8,128)(2,1)S(1)}, u32[]{:S(2)}, u32[]{:S(2)}) collective-permute-start(bf16[144,128]{1,0:T(8,128)(2,1)S(1)} %maximum_maximum_fusion.xo), channel_id=1, source_target_pairs={{0,31},{1,0},{2,1},{3,2},{4,3},{5,4},{6,5},{7,6},{8,7},{9,8},{10,9... | collective-permute-start | bytes 110600 | tf_op jit(solution)/shard_map/ppermute | solution.py:315
  15.1 6.1 %collective-permute-start.3 = (bf16[144,128]{1,0:T(8,128)(2,1)S(1)}, bf16[144,128]{1,0:T(8,128)(2,1)S(1)}, u32[]{:S(2)}, u32[]{:S(2)}) collective-permute-start(bf16[144,128]{1,0:T(8,128)(2,1)S(1)} %maximum_maximum_fusion.xo), channel_id=1, source_target_pairs={{0,1},{1,2},{2,3},{3,4},{4,5},{5,6},{6,7},{7,8},{8,9},{9,10},{10,1... | collective-permute-start | bytes 110600 | tf_op jit(solution)/shard_map/ppermute | solution.py:315
  15.7 5.5 %copy-start.7 = (bf16[64,128]{1,0:T(8,128)(2,1)}, bf16[64,128]{1,0:T(8,128)(2,1)S(1)}, u32[]{:S(2)}) copy-start(bf16[64,128]{1,0:T(8,128)(2,1)S(1)} %collective-permute-done.2.r2) | copy-start | bytes 49156
  15.7 5.5 %copy-start.8 = (bf16[64,128]{1,0:T(8,128)(2,1)}, bf16[64,128]{1,0:T(8,128)(2,1)S(1)}, u32[]{:S(2)}) copy-start(bf16[64,128]{1,0:T(8,128)(2,1)S(1)} %collective-permute-done.1.r3) | copy-start | bytes 49156
  17.5 3.7 %copy-start.9 = (bf16[64,128]{1,0:T(8,128)(2,1)}, bf16[64,128]{1,0:T(8,128)(2,1)S(1)}, u32[]{:S(2)}) copy-start(bf16[64,128]{1,0:T(8,128)(2,1)S(1)} %collective-permute-done.r4) | copy-start | bytes 49156
  17.5 3.7 %copy-start.5 = (bf16[144,128]{1,0:T(8,128)(2,1)}, bf16[144,128]{1,0:T(8,128)(2,1)S(1)}, u32[]{:S(2)}) copy-start(bf16[144,128]{1,0:T(8,128)(2,1)S(1)} %collective-permute-done.4.xr) | copy-start | bytes 110596
  21.2 0.6 %copy-start.6 = (bf16[144,128]{1,0:T(8,128)(2,1)}, bf16[144,128]{1,0:T(8,128)(2,1)S(1)}, u32[]{:S(2)}) copy-start(bf16[144,128]{1,0:T(8,128)(2,1)S(1)} %collective-permute-done.3.xl) | copy-start | bytes 110596
  23.6 7.4 %collective-permute-start.6 = (bf16[256,128]{1,0:T(8,128)(2,1)}, bf16[256,128]{1,0:T(8,128)(2,1)S(1)}, u32[]{:S(2)}, u32[]{:S(2)}) collective-permute-start(bf16[256,128]{1,0:T(8,128)(2,1)} %windows.1.own), channel_id=1, source_target_pairs={{32,64},{64,32},{96,128},{128,96},{160,192},{192,160},{224,0},{0,2... | collective-permute-start | bytes 196616 | tf_op jit(solution)/shard_map/ppermute | solution.py:324
  27.4 3.6 %collective-permute-start.5 = (bf16[256,128]{1,0:T(8,128)(2,1)}, bf16[256,128]{1,0:T(8,128)(2,1)S(1)}, u32[]{:S(2)}, u32[]{:S(2)}) collective-permute-start(bf16[256,128]{1,0:T(8,128)(2,1)} %windows.1.own), channel_id=1, source_target_pairs={{0,32},{32,0},{64,96},{96,64},{128,160},{160,128},{192,224},{224,1... | collective-permute-start | bytes 196616 | tf_op jit(solution)/shard_map/ppermute | solution.py:324
  28.1 0.9 %copy-start.1 = (bf16[27,32,32]{2,1,0:T(8,128)(2,1)S(1)}, bf16[27,32,32]{2,1,0:T(8,128)(2,1)}, u32[]{:S(2)}) copy-start(bf16[27,32,32]{2,1,0:T(8,128)(2,1)} %w1_ref.1) | copy-start | bytes 165892
  29.1 0.9 %copy-start.2 = (bf16[27,32,32]{2,1,0:T(8,128)(2,1)S(1)}, bf16[27,32,32]{2,1,0:T(8,128)(2,1)}, u32[]{:S(2)}) copy-start(bf16[27,32,32]{2,1,0:T(8,128)(2,1)} %w2_ref.1) | copy-start | bytes 165892
  31.0 0.8 %copy-start = (bf16[256,128]{1,0:T(8,128)(2,1)S(1)}, bf16[256,128]{1,0:T(8,128)(2,1)}, u32[]{:S(2)}) copy-start(bf16[256,128]{1,0:T(8,128)(2,1)} %windows.1.own) | copy-start | bytes 196612
  31.8 0.6 %copy-start.3 = (s32[4]{0:T(128)S(1)}, s32[4]{0:T(128)}, u32[]{:S(2)}) copy-start(s32[4]{0:T(128)} %pad_add_fusion.ids_ref) | copy-start | bytes 52

commit v2 on v1

--- a/solution.py
+++ b/solution.py
@@ -17,7 +17,7 @@
 KK = 768
 F32 = jnp.float32
 BF16 = jnp.bfloat16
-LIMIT = 50 * 1024 * 1024
+MIB = 1024 * 1024
 VMEM = pl.BlockSpec(memory_space=pltpu.VMEM)
 SMEM = pl.BlockSpec(memory_space=pltpu.SMEM)
 
@@ -26,7 +26,7 @@
     return lax.broadcasted_iota(jnp.int32, shape, dim)
 
 
-def prepare(w1_ref, w2_ref, b_ref, t1_ref, t2_ref, c1_ref, c2_ref, sel_ref, idp_ref, tmp):
+def prepare(w1_ref, w2_ref, b1_ref, b2_ref, t1_ref, t2_ref, c1_ref, c2_ref, sel_ref, idp_ref, tmp):
     zero = jnp.zeros((C, C), F32)
     for e in range(3):
         one = {(a, b): w1_ref[9 * a + 3 * b + e].astype(F32) for a in range(3) for b in range(3)}
@@ -45,9 +45,16 @@
                     )
         for q in range(6):
             t2_ref[e, :, q * CW : (q + 1) * CW] = tmp[q].astype(BF16)
+    eye = iota((C, C), 0) == iota((C, C), 1)
+
+    def column(b):
+        b = jnp.sum(jnp.where(eye, jnp.broadcast_to(b, (C, C)), 0.0), axis=1, keepdims=True)
+        return jnp.broadcast_to(b, (C, CW))
+
+    one, two = column(b1_ref[...]), column(b2_ref[...])
     for p in range(8):
-        c1_ref[p * C : (p + 1) * C, :] = b_ref[0]
-        c2_ref[pl.ds(p, C, stride=8), :] = b_ref[1]
+        c1_ref[p * C : (p + 1) * C, :] = one
+        c2_ref[pl.ds(p, C, stride=8), :] = two
     lane = iota((128, 128), 1)
     src = iota((128, 128), 0)
     d = lane // 2
@@ -76,7 +83,7 @@
     idp_ref[...] = jnp.where(inn == (out % 8) * C + out // 8, 1.0, 0.0).astype(BF16)
 
 
-def prepared(weight_one, weight_two, bias):
+def prepared(weight_one, weight_two, bias_one, bias_two):
     return pl.pallas_call(
         prepare,
         out_shape=(
@@ -87,17 +94,18 @@
             jax.ShapeDtypeStruct((512, 768), BF16),
             jax.ShapeDtypeStruct((256, 256), BF16),
         ),
-        in_specs=[VMEM] * 3,
+        in_specs=[VMEM] * 4,
         out_specs=[VMEM] * 6,
         scratch_shapes=[pltpu.VMEM((6, 256, CW), F32)],
-        compiler_params=pltpu.CompilerParams(vmem_limit_bytes=LIMIT),
+        cost_estimate=pl.CostEstimate(flops=1000000, bytes_accessed=4000000, transcendentals=0),
+        compiler_params=pltpu.CompilerParams(vmem_limit_bytes=12 * MIB),
         name="prepare",
-    )(weight_one, weight_two, bias)
-
-
-def cut(ids_ref, off_ref, r4, r3, r2, xl, xo, xr, out_ref, tiles):
-    col = ids_ref[1]
-    last = ids_ref[3] - 1
+    )(weight_one, weight_two, bias_one.reshape(1, C), bias_two.reshape(1, C))
+
+
+def cut(off_ref, r4, r3, r2, xl, xo, xr, after_ref, out_ref, tiles):
+    col = lax.axis_index("cols")
+    last = lax.axis_size("cols") - 1
     o = off_ref[0]
 
     def scalar_of(ref):
@@ -142,24 +150,25 @@
     out_ref[192:256, :] = border.astype(BF16)
 
 
-def windows(ids, offsets, r4, r3, r2, xl, xo, xr):
+def windows(offsets, r4, r3, r2, xl, xo, xr, after):
     return pl.pallas_call(
         cut,
         out_shape=jax.ShapeDtypeStruct((256, CW), BF16),
-        in_specs=[SMEM, SMEM] + [VMEM] * 6,
+        in_specs=[SMEM] + [VMEM] * 6 + [pl.BlockSpec(memory_space=pl.ANY)],
         out_specs=VMEM,
         scratch_shapes=[pltpu.VMEM((6, 64, CW), F32)],
+        compiler_params=pltpu.CompilerParams(vmem_limit_bytes=4 * MIB),
         name="windows",
-    )(ids, offsets, r4, r3, r2, xl, xo, xr)
+    )(offsets, r4, r3, r2, xl, xo, xr, after)
 
 
 def aggregate(
-    ids_ref, own, pair, cross, t1, t2, c1, c2, sel, idp, out_ref, vol, vown, hid, zcol, hcol
+    own, pair, cross, t1, t2, c1, c2, sel, idp, out_ref, vol, vown, hid, zcol, hcol
 ):
-    row = ids_ref[0]
-    col = ids_ref[1]
-    rows_last = ids_ref[2] - 1
-    cols_last = ids_ref[3] - 1
+    row = lax.axis_index("rows")
+    col = lax.axis_index("cols")
+    rows_last = lax.axis_size("rows") - 1
+    cols_last = lax.axis_size("cols") - 1
     odd = row % 2 == 1
     no_up = row == 0
     no_down = row == rows_last
@@ -237,7 +246,7 @@
         vown[pl.ds(pl.multiple_of(d * OD, OD), OD), :] = mid[2 * C : 4 * C]
         return s0, s1
 
-    lax.fori_loop(0, D, one_disparity, (shifted(D), shifted(D + 1)))
+    lax.fori_loop(0, D, one_disparity, (shifted(D), shifted(D + 1)), unroll=True)
 
     hl = iota((256, CW), 1)
     hr = (iota((256, CW), 0) // C) % HR
@@ -271,7 +280,7 @@
             ).astype(BF16)
         return carry
 
-    lax.fori_loop(0, D // 4, conv_one, 0)
+    lax.fori_loop(0, D // 4, conv_one, 0, unroll=True)
 
     def conv_two(j, carry):
         d0 = j * 8
@@ -289,14 +298,14 @@
         ).astype(BF16)
         return carry
 
-    lax.fori_loop(0, D // 8, conv_two, 0)
-
-
-def aggregated(ids, own, pair, cross, t1, t2, c1, c2, sel, idp):
+    lax.fori_loop(0, D // 8, conv_two, 0, unroll=True)
+
+
+def aggregated(own, pair, cross, t1, t2, c1, c2, sel, idp):
     return pl.pallas_call(
         aggregate,
         out_shape=jax.ShapeDtypeStruct((C, D * RH, CW), BF16),
-        in_specs=[SMEM] + [VMEM] * 9,
+        in_specs=[VMEM] * 9,
         out_specs=VMEM,
         scratch_shapes=[
             pltpu.VMEM((3, (D + 2) * VD, CW), BF16),
@@ -305,9 +314,9 @@
             pltpu.VMEM((VD, CW), F32),
             pltpu.VMEM((HD, CW), F32),
         ],
-        compiler_params=pltpu.CompilerParams(vmem_limit_bytes=LIMIT),
+        compiler_params=pltpu.CompilerParams(vmem_limit_bytes=32 * MIB),
         name="aggregate",
-    )(ids, own, pair, cross, t1, t2, c1, c2, sel, idp)
+    )(own, pair, cross, t1, t2, c1, c2, sel, idp)
 
 
 def ring(x, axis, by):
@@ -325,15 +334,6 @@
 
 
 def body(left, right, offsets, weight_one, bias_one, weight_two, bias_two):
-    ids = jnp.stack(
-        [
-            lax.axis_index("rows"),
-            lax.axis_index("cols"),
-            lax.axis_size("rows"),
-            lax.axis_size("cols"),
-        ]
-    ).astype(jnp.int32)
-    bias = jnp.broadcast_to(jnp.stack([bias_one, bias_two])[:, :, None], (2, C, CW))
     r = right.reshape(C * RH, CW)
     l = left.reshape(C * RH, CW)
     o = offsets[0]
@@ -345,11 +345,11 @@
     r2 = ring(r, "cols", 2)
     xl = ring(x, "cols", 1)
     xr = ring(x, "cols", -1)
-    ready = prepared(weight_one, weight_two, bias)
-    own = windows(ids, offsets, r4, r3, r2, xl, x, xr)
+    ready = prepared(weight_one, weight_two, bias_one, bias_two)
+    own = windows(offsets, r4, r3, r2, xl, x, xr, ready[2])
     pair = swap(own, "rows", 0)
     cross = swap(own, "rows", 1)
-    out = aggregated(ids, own, pair, cross, *ready)
+    out = aggregated(own, pair, cross, *ready)
     return out.reshape(C, D, RH, CW)
 
 

time: 50.6 us -> 35.7 us (0.71)
  the two profiles are of different devices: /device:TPU:1 before, /device:TPU:64 now
where the time goes in v2:
time: 35.7 us; the launch traced here: 35.4 us
  starting transfers between devices  13.9 us (39%)
  Pallas kernels  9.32 us (26%)
  waiting for transfers between devices  7.49 us (21%)
  local copies, waits for them, and re-layouts  3.19 us (9%)
  other arithmetic  0.83 us (2%)
  between operations  0.75 us (2%)
    ppermute x5, starting transfers between devices, ring(): return lax.ppermute(x, axis, [(i, (i + by) % n) for i in range(n)])  12.2 us
    pallas_call x1, Pallas kernels, aggregated(): pl.pallas_call(aggregate, out_shape=jax.ShapeDtypeStruct((C, D * RH, CW),...  8.03 us
    ppermute x5, waiting for transfers between devices, ring(): return lax.ppermute(x, axis, [(i, (i + by) % n) for i in range(n)])  4.2 us
    ppermute x2, waiting for transfers between devices, swap(): return lax.ppermute(x, axis, pairs)  3.3 us
    unnamed x8, local copies, waits for them, and re-layouts  3.18 us
    ppermute x2, starting transfers between devices, swap(): return lax.ppermute(x, axis, pairs)  1.69 us
    pallas_call x1, Pallas kernels, prepared(): pl.pallas_call(prepare, out_shape=(jax.ShapeDtypeStruct((3, 256, KK), BF1...  1.01 us
    concatenate x1, other arithmetic, body(): x = jnp.concatenate([l, r, jnp.broadcast_to(code, (16, CW))], axis=0)  0.82 us
  transfers between devices with their start and end apart: 7, of which 2 were waited for; matrix products, arithmetic and copies ran while one was open for 0% of the time, Pallas kernels for 3%

profile of v2, /device:TPU:64, one launch (start us, length us, event | category | flops | bytes accessed | tf_op | source)
XLA Modules:
  0.0 35.4 jit_solution(14940294436810792339)
XLA Ops:
  0.7 0.8 %maximum_maximum_fusion.xo = bf16[144,128]{1,0:T(8,128)(2,1)S(1)} fusion(bf16[64,128]{1,0:T(8,128)(2,1)} %bitcast.13, bf16[64,128]{1,0:T(8,128)(2,1)} %bitcast.12, bf16[144]{0:T(256)(128)(2,1)S(1)} %pad.2.clone), kind=kLoop, calls=%fused_computation | loop fusion | flops 110592 | bytes 69920 | tf_op jit(solution)/shard_map/concatenate | solution.py:342
  1.5 0.2 collective-permute-start.4
  1.7 1.9 %collective-permute-start.3 = (bf16[144,128]{1,0:T(8,128)(2,1)S(1)}, bf16[144,128]{1,0:T(8,128)(2,1)S(1)}, u32[]{:S(2)}, u32[]{:S(2)}) collective-permute-start(bf16[144,128]{1,0:T(8,128)(2,1)S(1)} %maximum_maximum_fusion.xo), channel_id=1, source_target_pairs={{0,1},{1,2},{2,3},{3,4},{4,5},{5,6},{6,7},{7,8},{8,9},{9,10},{10,1... | collective-permute-start | bytes 110600 | tf_op jit(solution)/shard_map/ppermute | solution.py:324
  3.6 4.5 %collective-permute-start.2 = (bf16[64,128]{1,0:T(8,128)(2,1)}, bf16[64,128]{1,0:T(8,128)(2,1)S(1)}, u32[]{:S(2)}, u32[]{:S(2)}) collective-permute-start(bf16[64,128]{1,0:T(8,128)(2,1)} %bitcast.14), channel_id=1, source_target_pairs={{0,2},{1,3},{2,4},{3,5},{4,6},{5,7},{6,8},{7,9},{8,10},{9,11},{10,... | collective-permute-start | bytes 49160 | tf_op jit(solution)/shard_map/ppermute | solution.py:324
  8.1 4.0 %collective-permute-start.1 = (bf16[64,128]{1,0:T(8,128)(2,1)}, bf16[64,128]{1,0:T(8,128)(2,1)S(1)}, u32[]{:S(2)}, u32[]{:S(2)}) collective-permute-start(bf16[64,128]{1,0:T(8,128)(2,1)} %bitcast.15), channel_id=1, source_target_pairs={{0,3},{1,4},{2,5},{3,6},{4,7},{5,8},{6,9},{7,10},{8,11},{9,12},{10... | collective-permute-start | bytes 49160 | tf_op jit(solution)/shard_map/ppermute | solution.py:324
  12.2 1.6 %collective-permute-start = (bf16[64,128]{1,0:T(8,128)(2,1)}, bf16[64,128]{1,0:T(8,128)(2,1)S(1)}, u32[]{:S(2)}, u32[]{:S(2)}) collective-permute-start(bf16[64,128]{1,0:T(8,128)(2,1)} %bitcast.16), channel_id=1, source_target_pairs={{0,4},{1,5},{2,6},{3,7},{4,8},{5,9},{6,10},{7,11},{8,12},{9,13},{1... | collective-permute-start | bytes 49160 | tf_op jit(solution)/shard_map/ppermute | solution.py:324
  13.7 0.0 copy-start
  13.7 0.9 %copy-done = bf16[27,32,32]{2,1,0:T(8,128)(2,1)S(1)} copy-done((bf16[27,32,32]{2,1,0:T(8,128)(2,1)S(1)}, bf16[27,32,32]{2,1,0:T(8,128)(2,1)}, u32[]{:S(2)}) %copy-start) | copy-done | bytes 55320
  14.6 0.0 copy-start.1
  14.7 0.9 %copy-done.1 = bf16[27,32,32]{2,1,0:T(8,128)(2,1)S(1)} copy-done((bf16[27,32,32]{2,1,0:T(8,128)(2,1)S(1)}, bf16[27,32,32]{2,1,0:T(8,128)(2,1)}, u32[]{:S(2)}) %copy-start.1) | copy-done | bytes 55320
  15.6 0.0 copy-start.2
  15.6 0.7 %copy-done.2 = f32[32]{0:T(128)S(1)} copy-done((f32[32]{0:T(128)S(1)}, f32[32]{0:T(128)}, u32[]{:S(2)}) %copy-start.2) | copy-done | bytes 152
  16.2 0.0 copy-start.3
  16.2 0.7 %copy-done.3 = f32[32]{0:T(128)S(1)} copy-done((f32[32]{0:T(128)S(1)}, f32[32]{0:T(128)}, u32[]{:S(2)}) %copy-start.3) | copy-done | bytes 152
  16.9 1.0 %prepare.1 = (bf16[3,256,768]{2,1,0:T(8,128)(2,1)S(1)}, bf16[3,256,768]{2,1,0:T(8,128)(2,1)S(1)}, f32[256,128]{1,0:T(8,128)S(1)}, f32[256,128]{1,0:T(8,128)S(1)}...) custom-call(bf16[27,32,32]{2,1,0:T(8,128)(2,1)S(1)} %copy-done, bf16[27,32,32]{2,1,0:T(8,128)(2,1)S(1)} %copy-done.1, ...), custom_call_target="tpu_custom_call" | custom-call | flops 1000000 | bytes 4000000 | tf_op jit(solution)/shard_map/prepare/pallas_call | solution.py:87
  17.9 0.0 collective-permute-done.2.r2
  17.9 0.0 collective-permute-done.1.r3
  17.9 4.2 %collective-permute-done.r4 = bf16[64,128]{1,0:T(8,128)(2,1)S(1)} collective-permute-done((bf16[64,128]{1,0:T(8,128)(2,1)}, bf16[64,128]{1,0:T(8,128)(2,1)S(1)}, u32[]{:S(2)}, u32[]{:S(2)}) %collective-permute-start) | collective-permute-done | bytes 16416 | tf_op jit(solution)/shard_map/ppermute | solution.py:324
  22.1 0.0 collective-permute-done.4.xr
  22.1 0.0 collective-permute-done.3.xl
  22.1 0.3 windows.1.own
  22.4 0.1 collective-permute-start.6
  22.5 1.6 %collective-permute-start.5 = (bf16[256,128]{1,0:T(8,128)(2,1)S(1)}, bf16[256,128]{1,0:T(8,128)(2,1)S(1)}, u32[]{:S(2)}, u32[]{:S(2)}) collective-permute-start(bf16[256,128]{1,0:T(8,128)(2,1)S(1)} %windows.1.own), channel_id=1, source_target_pairs={{0,32},{32,0},{64,96},{96,64},{128,160},{160,128},{192,224},{224,1... | collective-permute-start | bytes 196616 | tf_op jit(solution)/shard_map/ppermute | solution.py:333
  24.1 3.3 %collective-permute-done.6.cross = bf16[256,128]{1,0:T(8,128)(2,1)S(1)} collective-permute-done((bf16[256,128]{1,0:T(8,128)(2,1)S(1)}, bf16[256,128]{1,0:T(8,128)(2,1)S(1)}, u32[]{:S(2)}, u32[]{:S(2)}) %collective-permute-start.6) | collective-permute-done | bytes 65568 | tf_op jit(solution)/shard_map/ppermute | solution.py:333
  27.4 0.0 collective-permute-done.5.pair
  27.4 8.0 %aggregate.1 = bf16[32,96,128]{2,1,0:T(8,128)(2,1)} custom-call(bf16[256,128]{1,0:T(8,128)(2,1)S(1)} %windows.1.own, bf16[256,128]{1,0:T(8,128)(2,1)S(1)} %collective-permute-done.5.pair, bf16[256,128]{1,0:T(8,128)(2,1)S(1)} %collective-permute-done.6.cross, bf16[3,256,768]{2,1,0:T(8,128)(2,1)S(1)} %get-tuple-element.12.t1, ...), custom_call_target="tpu_custom_call" | custom-call | tf_op jit(solution)/shard_map/aggregate/pallas_call | solution.py:305
  (2 shorter events, 0.0 us)
Async XLA Ops:
  1.5 20.6 %collective-permute-start.4 = (bf16[144,128]{1,0:T(8,128)(2,1)S(1)}, bf16[144,128]{1,0:T(8,128)(2,1)S(1)}, u32[]{:S(2)}, u32[]{:S(2)}) collective-permute-start(bf16[144,128]{1,0:T(8,128)(2,1)S(1)} %maximum_maximum_fusion.xo), channel_id=1, source_target_pairs={{0,31},{1,0},{2,1},{3,2},{4,3},{5,4},{6,5},{7,6},{8,7},{9,8},{10,9... | collective-permute-start | bytes 110600 | tf_op jit(solution)/shard_map/ppermute | solution.py:324
  1.7 20.4 %collective-permute-start.3 = (bf16[144,128]{1,0:T(8,128)(2,1)S(1)}, bf16[144,128]{1,0:T(8,128)(2,1)S(1)}, u32[]{:S(2)}, u32[]{:S(2)}) collective-permute-start(bf16[144,128]{1,0:T(8,128)(2,1)S(1)} %maximum_maximum_fusion.xo), channel_id=1, source_target_pairs={{0,1},{1,2},{2,3},{3,4},{4,5},{5,6},{6,7},{7,8},{8,9},{9,10},{10,1... | collective-permute-start | bytes 110600 | tf_op jit(solution)/shard_map/ppermute | solution.py:324
  3.6 14.3 %collective-permute-start.2 = (bf16[64,128]{1,0:T(8,128)(2,1)}, bf16[64,128]{1,0:T(8,128)(2,1)S(1)}, u32[]{:S(2)}, u32[]{:S(2)}) collective-permute-start(bf16[64,128]{1,0:T(8,128)(2,1)} %bitcast.14), channel_id=1, source_target_pairs={{0,2},{1,3},{2,4},{3,5},{4,6},{5,7},{6,8},{7,9},{8,10},{9,11},{10,... | collective-permute-start | bytes 49160 | tf_op jit(solution)/shard_map/ppermute | solution.py:324
  8.1 9.8 %collective-permute-start.1 = (bf16[64,128]{1,0:T(8,128)(2,1)}, bf16[64,128]{1,0:T(8,128)(2,1)S(1)}, u32[]{:S(2)}, u32[]{:S(2)}) collective-permute-start(bf16[64,128]{1,0:T(8,128)(2,1)} %bitcast.15), channel_id=1, source_target_pairs={{0,3},{1,4},{2,5},{3,6},{4,7},{5,8},{6,9},{7,10},{8,11},{9,12},{10... | collective-permute-start | bytes 49160 | tf_op jit(solution)/shard_map/ppermute | solution.py:324
  12.2 10.0 %collective-permute-start = (bf16[64,128]{1,0:T(8,128)(2,1)}, bf16[64,128]{1,0:T(8,128)(2,1)S(1)}, u32[]{:S(2)}, u32[]{:S(2)}) collective-permute-start(bf16[64,128]{1,0:T(8,128)(2,1)} %bitcast.16), channel_id=1, source_target_pairs={{0,4},{1,5},{2,6},{3,7},{4,8},{5,9},{6,10},{7,11},{8,12},{9,13},{1... | collective-permute-start | bytes 49160 | tf_op jit(solution)/shard_map/ppermute | solution.py:324
  13.7 0.9 %copy-start = (bf16[27,32,32]{2,1,0:T(8,128)(2,1)S(1)}, bf16[27,32,32]{2,1,0:T(8,128)(2,1)}, u32[]{:S(2)}) copy-start(bf16[27,32,32]{2,1,0:T(8,128)(2,1)} %w1_ref.1) | copy-start | bytes 165892
  14.6 0.9 %copy-start.1 = (bf16[27,32,32]{2,1,0:T(8,128)(2,1)S(1)}, bf16[27,32,32]{2,1,0:T(8,128)(2,1)}, u32[]{:S(2)}) copy-start(bf16[27,32,32]{2,1,0:T(8,128)(2,1)} %w2_ref.1) | copy-start | bytes 165892
  15.6 0.7 %copy-start.2 = (f32[32]{0:T(128)S(1)}, f32[32]{0:T(128)}, u32[]{:S(2)}) copy-start(f32[32]{0:T(128)} %param.11) | copy-start | bytes 388
  16.2 0.7 %copy-start.3 = (f32[32]{0:T(128)S(1)}, f32[32]{0:T(128)}, u32[]{:S(2)}) copy-start(f32[32]{0:T(128)} %param.13) | copy-start | bytes 388
  22.4 5.0 %collective-permute-start.6 = (bf16[256,128]{1,0:T(8,128)(2,1)S(1)}, bf16[256,128]{1,0:T(8,128)(2,1)S(1)}, u32[]{:S(2)}, u32[]{:S(2)}) collective-permute-start(bf16[256,128]{1,0:T(8,128)(2,1)S(1)} %windows.1.own), channel_id=1, source_target_pairs={{32,64},{64,32},{96,128},{128,96},{160,192},{192,160},{224,0},{0,2... | collective-permute-start | bytes 196616 | tf_op jit(solution)/shard_map/ppermute | solution.py:333
  22.5 4.9 %collective-permute-start.5 = (bf16[256,128]{1,0:T(8,128)(2,1)S(1)}, bf16[256,128]{1,0:T(8,128)(2,1)S(1)}, u32[]{:S(2)}, u32[]{:S(2)}) collective-permute-start(bf16[256,128]{1,0:T(8,128)(2,1)S(1)} %windows.1.own), channel_id=1, source_target_pairs={{0,32},{32,0},{64,96},{96,64},{128,160},{160,128},{192,224},{224,1... | collective-permute-start | bytes 196616 | tf_op jit(solution)/shard_map/ppermute | solution.py:333

commit v3 on v2

v3 whole, which is shorter than its diff:
```python
import jax
import jax.numpy as jnp
from jax import lax
from jax.experimental import pallas as pl
from jax.experimental.pallas import tpu as pltpu
from jax.sharding import PartitionSpec as P

C = 32
D = 48
RH = 2
CW = 128
VR = RH + 4
HR = RH + 2
VD = VR * C
HD = HR * C
OD = RH * C
KK = 768
KE = 1792
F32 = jnp.float32
BF16 = jnp.bfloat16
MIB = 1024 * 1024
VMEM = pl.BlockSpec(memory_space=pltpu.VMEM)
SMEM = pl.BlockSpec(memory_space=pltpu.SMEM)


def iota(shape, dim):
    return lax.broadcasted_iota(jnp.int32, shape, dim)


def prepare(
    w1_ref, w2_ref, b1_ref, b2_ref, own_ref, halo_ref, edge_ref, mid_ref, ends_ref, c1_ref, c2_ref, sel_ref
):
    zero = jnp.zeros((C, C), F32)

    def taps(ref):
        return {
            (a, b, e): ref[9 * a + 3 * b + e].astype(F32)
            for a in range(3)
            for b in range(3)
            for e in range(3)
        }

    def fill(ref, row, parts):
        for q in range(0, len(parts), 4):
            ref[row : row + C, q * C : (q + 4) * C] = jnp.concatenate(
                parts[q : q + 4], axis=1
            ).astype(BF16)

    one = taps(w1_ref)
    for r in range(HR):
        for d in range(2):
            row = (r * 2 + d) * C

            def band(rows):
                return [
                    one.get((dl - d, rl - r, e), zero)
                    for e in range(3)
                    for dl in range(4)
                    for rl in rows
                ]

            fill(own_ref, row, band((2, 3)))
            fill(halo_ref, row, band((0, 1) if r < 2 else (4, 5)))
        fill(
            edge_ref,
            r * C,
            [
                one.get((a, rl - r, e), zero)
                for e in range(3)
                for a in range(3)
                for rl in range(VR)
            ]
            + [zero] * 2,
        )
    two = taps(w2_ref)
    for d in range(4):
        for h in range(RH):
            row = (d * RH + h) * C

            def band2(deep):
                return [
                    two.get((dl - d, rl - h, e), zero)
                    for e in range(3)
                    for dl in deep
                    for rl in range(HR)
                ]

            fill(mid_ref, row, band2((2, 3)))
            fill(ends_ref, row, band2((0, 1) if d < 2 else (4, 5)))
    eye = iota((C, C), 0) == iota((C, C), 1)

    def column(b):
        b = jnp.sum(jnp.where(eye, jnp.broadcast_to(b, (C, C)), 0.0), axis=1, keepdims=True)
        return jnp.broadcast_to(b, (C, CW))

    one, two = column(b1_ref[...]), column(b2_ref[...])
    for p in range(8):
        c1_ref[p * C : (p + 1) * C, :] = one
        c2_ref[p * C : (p + 1) * C, :] = two
    lane = iota((128, 128), 1)
    src = iota((128, 128), 0)
    d = lane // 2
    used = d < D
    left = (lane % 2 == 1) & used
    right = (lane % 2 == 0) & used
    right_of = (
        ((3, 47 - d), (2, 47 - d)),
        ((3, 48 - d), (3, 111 - d)),
        ((1, 48 - d), (3, 112 - d)),
    )
    left_of = (((3, 50), (0, 127)), ((3, 51), (3, 114)), ((0, 0), (3, 115)))
    for e in range(3):
        for which, table in ((0, right_of), (1, left_of)):
            for t in range(4):
                hit = jnp.zeros((128, 128), jnp.bool_)
                for mask, (tile, place) in zip((left, right), table[e]):
                    if tile == t:
                        hit = hit | (mask & (src == place))
                g = 2 * e + which
                sel_ref[t * 128 : (t + 1) * 128, g * 128 : (g + 1) * 128] = jnp.where(
                    hit, 1.0, 0.0
                ).astype(BF16)


def prepared(weight_one, weight_two, bias_one, bias_two):
    return pl.pallas_call(
        prepare,
        out_shape=(
            jax.ShapeDtypeStruct((256, KK), BF16),
            jax.ShapeDtypeStruct((256, KK), BF16),
            jax.ShapeDtypeStruct((HD, KE), BF16),
            jax.ShapeDtypeStruct((256, KK), BF16),
            jax.ShapeDtypeStruct((256, KK), BF16),
            jax.ShapeDtypeStruct((256, CW), F32),
            jax.ShapeDtypeStruct((256, CW), F32),
            jax.ShapeDtypeStruct((512, 768), BF16),
        ),
        in_specs=[VMEM] * 4,
        out_specs=[VMEM] * 8,
        cost_estimate=pl.CostEstimate(flops=1000000, bytes_accessed=4000000, transcendentals=0),
        compiler_params=pltpu.CompilerParams(vmem_limit_bytes=12 * MIB),
        name="prepare",
    )(weight_one, weight_two, bias_one.reshape(1, C), bias_two.reshape(1, C))


def cut(off_ref, xr, xl, r2, r3, r4, xo, after_ref, out_ref, tiles):
    col = lax.axis_index("cols")
    last = lax.axis_size("cols") - 1
    o = off_ref[0]

    def scalar_of(ref):
        v = ref[128:144, :].astype(F32)
        return jnp.max(v[0:1] * 8.0 + v[1:2]).astype(jnp.int32)

    o_l = scalar_of(xl)
    o_r = scalar_of(xr)
    dst = iota((64, 64), 0)
    src = iota((64, 64), 1)
    perm = jnp.where(src == (dst % C) * RH + dst // C, 1.0, 0.0).astype(BF16)

    def rows(x):
        return jnp.dot(perm, x, preferred_element_type=F32)

    for t, x in enumerate((r4[...], r3[...], r2[...], xl[64:128, :], xo[64:128, :])):
        keep = (col + (t - 4) >= 0).astype(F32)
        tiles[t] = rows(x) * keep
    tiles[5] = rows(xr[64:128, :])
    lane = iota((64, CW), 1)

    def window(start):
        t = start // CW
        s = start % CW
        back = (CW - s) % CW
        a = tiles[t]
        b = tiles[t + 1]
        return t, s, back, pltpu.roll(jnp.where(lane < s, b, a), back, 1)

    t, s, back, one = window(464 - o)
    two = pltpu.roll(jnp.where(lane < s, tiles[t + 2], tiles[t + 1]), back, 1)
    wl = window(463 - o_l)[3]
    wr = window(529 - o_r)[3]
    near = rows(xl[0:64, :]) * (col > 0).astype(F32)
    far = rows(xr[0:64, :]) * (col < last).astype(F32)
    border = jnp.where(lane < 50, wl, jnp.where(lane < 52, pltpu.roll(near, 52, 1), wr))
    border = jnp.where((lane < 114), border, pltpu.roll(far, 114, 1))
    border = jnp.where((lane < 116) & ((lane < 52) | (lane >= 64)), border, 0.0)
    out_ref[0:64, :] = rows(xo[0:64, :]).astype(BF16)
    out_ref[64:128, :] = one.astype(BF16)
    out_ref[128:192, :] = two.astype(BF16)
    out_ref[192:256, :] = border.astype(BF16)


def windows(offsets, xr, xl, r2, r3, r4, xo, after):
    return pl.pallas_call(
        cut,
        out_shape=jax.ShapeDtypeStruct((256, CW), BF16),
        in_specs=[SMEM] + [VMEM] * 6 + [pl.BlockSpec(memory_space=pl.ANY)],
        out_specs=VMEM,
        scratch_shapes=[pltpu.VMEM((6, 64, CW), F32)],
        compiler_params=pltpu.CompilerParams(vmem_limit_bytes=4 * MIB),
        name="windows",
    )(offsets, xr, xl, r2, r3, r4, xo, after)


def aggregate(
    own, pair, cross, t_own, t_halo, t_edge, t_mid, t_ends, c1, c2, sel, out_ref, vol, hid, stage
):
    row = lax.axis_index("rows")
    col = lax.axis_index("cols")
    rows_last = lax.axis_size("rows") - 1
    cols_last = lax.axis_size("cols") - 1
    odd = row % 2 == 1
    no_up = row == 0
    no_down = row == rows_last

    def tile(t):
        part = slice(t * 64, t * 64 + 64)
        p = pair[part, :]
        x = cross[part, :]
        up = jnp.where(odd, p, x)
        down = jnp.where(odd, x, p)
        up = jnp.where(no_up, jnp.zeros_like(up), up)
        down = jnp.where(no_down, jnp.zeros_like(down), down)
        return jnp.concatenate([up, own[part, :], down], axis=0)

    left, win0, win1, edge = (tile(t) for t in range(4))

    sources = jnp.concatenate([left, win0, win1, edge], axis=1)
    picked = jnp.dot(sources, sel[...], preferred_element_type=F32)
    cells = []
    for e in range(3):
        r = picked[:, (2 * e) * CW : (2 * e + 1) * CW]
        lft = picked[:, (2 * e + 1) * CW : (2 * e + 2) * CW]
        cells.append((r * lft).astype(BF16))
    around = []
    for z in cells:
        around += [pltpu.roll(z, 2, 1), z, pltpu.roll(z, CW - 2, 1)]
    around.append(jnp.zeros((KE - 9 * VD, CW), BF16))
    h = jnp.dot(t_edge[...], jnp.concatenate(around, axis=0), preferred_element_type=F32)
    h = jnp.maximum(h + c1[0:HD, :], 0.0)
    lane = iota((HD, CW), 1)
    hrow = iota((HD, CW), 0) // C
    gone = (no_up & (hrow == 0)) | (no_down & (hrow == HR - 1))
    gone = gone | ((col == 0) & (lane % 2 == 1)) | ((col == cols_last) & (lane % 2 == 0))
    hcol = jnp.where(gone, 0.0, h).astype(BF16)
    zcol = cells[1]

    vlane = iota((OD, CW), 1)
    first = vlane == 0
    last = vlane == CW - 1
    pad = jnp.zeros((HD, CW), BF16)
    for e in range(3):
        for g in range(3):
            vol[g, e, 0:OD, :] = pad[0:OD]
            vol[g, e, (D + 1) * OD : (D + 2) * OD, :] = pad[0:OD]
        hid[e, 0:HD, :] = pad
        hid[e, (D + 1) * HD : (D + 2) * HD, :] = pad
    groups = []
    for g in range(3):
        part = slice(g * OD, (g + 1) * OD)
        l1 = left[part]
        groups.append(
            (pltpu.roll(l1, 1, 1), l1, pltpu.roll(l1, CW - 1, 1), win0[part], win1[part], zcol[part])
        )

    def shifted(g, k):
        w0, w1 = groups[g][3:5]
        if k == 0:
            return w0
        return pltpu.roll(jnp.where(vlane < k, w1, w0), CW - k, 1)

    held = {(g, k): shifted(g, k) for g in range(3) for k in (D, D + 1)}

    def disparity(d):
        k = D - 1 - d
        base = (d + 1) * OD
        for g in range(3):
            l0, l1, l2, _, _, z = groups[g]
            held[g, k] = shifted(g, k)
            border = pltpu.roll(z, (2 * CW - 1 - 2 * d) % CW, 1)
            vol[g, 0, base : base + OD, :] = jnp.where(first, border, l0 * held[g, k])
            vol[g, 1, base : base + OD, :] = l1 * held[g, k + 1]
            vol[g, 2, base : base + OD, :] = jnp.where(last, border, l2 * held.pop((g, k + 2)))

    hl = iota((C, CW), 1)
    hfirst = hl == 0
    hlast = hl == CW - 1

    def conv_one(j):
        d0 = j * 4

        def rhs(g):
            return jnp.concatenate(
                [
                    jnp.concatenate(
                        [
                            vol[g, e, d0 * OD : d0 * OD + 256, :],
                            vol[g, e, (d0 + 2) * OD : (d0 + 2) * OD + 256, :],
                        ],
                        axis=1,
                    )
                    for e in range(3)
                ],
                axis=0,
            )

        mine = jnp.dot(t_own[...], rhs(1), preferred_element_type=F32)
        top = jnp.dot(t_halo[0:128, :], rhs(0), preferred_element_type=F32)
        bottom = jnp.dot(t_halo[128:256, :], rhs(2), preferred_element_type=F32)
        for i in range(2):
            cut = slice(i * CW, (i + 1) * CW)
            for dd in range(2):
                d = d0 + 2 * i + dd
                border = pltpu.roll(hcol, (2 * CW - 1 - 2 * d) % CW, 1)
                for r in range(HR):
                    at = (r * 2 + dd) * C
                    halo = top if r < 2 else bottom
                    ha = at % 128
                    h = mine[at : at + C, cut] + halo[ha : ha + C, cut] + c1[0:C, :]
                    h = jnp.maximum(h, 0.0)
                    if r == 0:
                        h = jnp.where(no_up, 0.0, h)
                    if r == HR - 1:
                        h = jnp.where(no_down, 0.0, h)
                    h = h.astype(BF16)
                    b = border[r * C : (r + 1) * C]
                    base = (d + 1) * HD + r * C
                    hid[0, base : base + C, :] = jnp.where(hfirst, b, pltpu.roll(h, 1, 1))
                    hid[1, base : base + C, :] = h
                    hid[2, base : base + C, :] = jnp.where(hlast, b, pltpu.roll(h, CW - 1, 1))

    def conv_two(j):
        d0 = j * 8

        def rhs(i):
            at = (d0 + 2 * i) * HD
            return jnp.concatenate(
                [
                    jnp.concatenate(
                        [hid[e, at : at + 256, :], hid[e, at + 4 * HD : at + 4 * HD + 256, :]], axis=1
                    )
                    for e in range(3)
                ],
                axis=0,
            )

        mid = jnp.dot(t_mid[...], rhs(1), preferred_element_type=F32)
        low = jnp.dot(t_ends[0:128, :], rhs(0), preferred_element_type=F32)
        high = jnp.dot(t_ends[128:256, :], rhs(2), preferred_element_type=F32)
        for i in range(2):
            cut = slice(i * CW, (i + 1) * CW)
            for p in range(8):
                end = low if p < 4 else high
                at = p * C
                ea = at % 128
                v = vol[1, 1, (d0 + 4 * i + 1) * OD + at : (d0 + 4 * i + 1) * OD + at + C, :]
                a = mid[at : at + C, cut] + end[ea : ea + C, cut] + c2[0:C, :] + v.astype(F32)
                stage[j % 2, pl.ds(8 * i + p, C, stride=16), :] = a
        out_ref[:, j * 16 : j * 16 + 16, :] = stage[j % 2].reshape(C, 16, CW).astype(BF16)

    done = 0
    for j in range(D // 4):
        upto = min(D, 4 * j + 5)
        for d in range(done, upto):
            disparity(d)
        done = upto
        conv_one(j)
    for j in range(D // 8):
        conv_two(j)


def aggregated(own, pair, cross, *ready):
    return pl.pallas_call(
        aggregate,
        out_shape=jax.ShapeDtypeStruct((C, D * RH, CW), BF16),
        in_specs=[VMEM] * 11,
        out_specs=VMEM,
        scratch_shapes=[
            pltpu.VMEM((3, 3, (D + 2) * OD, CW), BF16),
            pltpu.VMEM((3, (D + 2) * HD, CW), BF16),
            pltpu.VMEM((2, 512, CW), F32),
        ],
        compiler_params=pltpu.CompilerParams(vmem_limit_bytes=32 * MIB),
        name="aggregate",
    )(own, pair, cross, *ready)


def ring(x, axis, by):
    n = lax.axis_size(axis)
    return lax.ppermute(x, axis, [(i, (i + by) % n) for i in range(n)])


def swap(x, axis, first):
    n = lax.axis_size(axis)
    pairs = []
    for i in range(first, n + first, 2):
        a, b = i % n, (i + 1) % n
        pairs += [(a, b), (b, a)]
    return lax.ppermute(x, axis, pairs)


def body(left, right, offsets, weight_one, bias_one, weight_two, bias_two):
    r = right.reshape(C * RH, CW)
    l = left.reshape(C * RH, CW)
    o = offsets[0]
    place = jnp.arange(16, dtype=jnp.int32)[:, None]
    code = jnp.where(place == 0, o // 8, jnp.where(place == 1, o % 8, 0)).astype(BF16)
    x = jnp.concatenate([l, r, jnp.broadcast_to(code, (16, CW))], axis=0)
    r4 = ring(r, "cols", 4)
    r3 = ring(r, "cols", 3)
    r2 = ring(r, "cols", 2)
    xl = ring(x, "cols", 1)
    xr = ring(x, "cols", -1)
    ready = prepared(weight_one, weight_two, bias_one, bias_two)
    own = windows(offsets, xr, xl, r2, r3, r4, x, ready[5])
    pair = swap(own, "rows", 0)
    cross = swap(own, "rows", 1)
    out = aggregated(own, pair, cross, *ready)
    return out.reshape(C, D, RH, CW)


def solution(mesh):
    return jax.shard_map(
        body,
        mesh=mesh,
        in_specs=(P(None, "rows", "cols"), P(None, "rows", "cols"), P("cols"), P(), P(), P(), P()),
        out_specs=P(None, None, "rows", "cols"),
        check_vma=False,
    )
```

time: 35.7 us -> 32.3 us (0.905)
  the two profiles are of different devices: /device:TPU:64 before, /device:TPU:56 now
where the time goes in v3:
time: 32.3 us; the launch traced here: 32 us
  starting transfers between devices  14.4 us (45%)
  waiting for transfers between devices  6.87 us (21%)
  Pallas kernels  6.63 us (21%)
  local copies, waits for them, and re-layouts  3.22 us (10%)
  between operations  0.75 us (2%)
    ppermute x5, starting transfers between devices, ring(): return lax.ppermute(x, axis, [(i, (i + by) % n) for i in range(n)])  12.7 us
    pallas_call x1, Pallas kernels, aggregated(): pl.pallas_call(aggregate, out_shape=jax.ShapeDtypeStruct((C, D * RH, CW),...  5.74 us
    ppermute x5, waiting for transfers between devices, ring(): return lax.ppermute(x, axis, [(i, (i + by) % n) for i in range(n)])  3.58 us
    ppermute x2, waiting for transfers between devices, swap(): return lax.ppermute(x, axis, pairs)  3.3 us
    unnamed x12, local copies, waits for them, and re-layouts  3.21 us
    ppermute x2, starting transfers between devices, swap(): return lax.ppermute(x, axis, pairs)  1.69 us
  transfers between devices with their start and end apart: 7, of which 3 were waited for; matrix products, arithmetic and copies ran while one was open for 0% of the time, Pallas kernels for 2%

profile of v3, /device:TPU:56, one launch (start us, length us, event | category | flops | bytes accessed | tf_op | source)
XLA Modules:
  0.0 32.0 jit_solution(7876822281109876761)
XLA Ops:
  0.7 0.0 copy-start.4
  0.7 0.0 copy-start.5
  0.7 0.7 %copy-done.4 = bf16[32,2,128]{2,1,0:T(2,128)(2,1)S(1)} copy-done((bf16[32,2,128]{2,1,0:T(2,128)(2,1)S(1)}, bf16[32,2,128]{2,1,0:T(2,128)(2,1)}, u32[]{:S(2)}) %copy-start.4) | copy-done | bytes 16408
  1.4 0.0 copy-done.5
  1.4 0.1 maximum_maximum_fusion.xo
  1.5 2.0 %collective-permute-start.1 = (bf16[144,128]{1,0:T(8,128)(2,1)S(1)}, bf16[144,128]{1,0:T(8,128)(2,1)S(1)}, u32[]{:S(2)}, u32[]{:S(2)}) collective-permute-start(bf16[144,128]{1,0:T(8,128)(2,1)S(1)} %maximum_maximum_fusion.xo), channel_id=1, source_target_pairs={{0,1},{1,2},{2,3},{3,4},{4,5},{5,6},{6,7},{7,8},{8,9},{9,10},{10,1... | collective-permute-start | bytes 110600 | tf_op jit(solution)/shard_map/ppermute | solution.py:390
  3.5 0.1 collective-permute-start
  3.6 6.3 %collective-permute-start.4 = (bf16[64,128]{1,0:T(8,128)(2,1)S(1)}, bf16[64,128]{1,0:T(8,128)(2,1)S(1)}, u32[]{:S(2)}, u32[]{:S(2)}) collective-permute-start(bf16[64,128]{1,0:T(8,128)(2,1)S(1)} %bitcast.14), channel_id=1, source_target_pairs={{0,4},{1,5},{2,6},{3,7},{4,8},{5,9},{6,10},{7,11},{8,12},{9,13},{1... | collective-permute-start | bytes 49160 | tf_op jit(solution)/shard_map/ppermute | solution.py:390
  9.9 4.3 %collective-permute-start.3 = (bf16[64,128]{1,0:T(8,128)(2,1)S(1)}, bf16[64,128]{1,0:T(8,128)(2,1)S(1)}, u32[]{:S(2)}, u32[]{:S(2)}) collective-permute-start(bf16[64,128]{1,0:T(8,128)(2,1)S(1)} %bitcast.15), channel_id=1, source_target_pairs={{0,3},{1,4},{2,5},{3,6},{4,7},{5,8},{6,9},{7,10},{8,11},{9,12},{10... | collective-permute-start | bytes 49160 | tf_op jit(solution)/shard_map/ppermute | solution.py:390
  14.2 0.0 collective-permute-start.2
  14.2 0.0 copy-start.2
  14.2 0.0 copy-start.3
  14.2 0.7 %copy-done.2 = f32[32]{0:T(128)S(1)} copy-done((f32[32]{0:T(128)S(1)}, f32[32]{0:T(128)}, u32[]{:S(2)}) %copy-start.2) | copy-done | bytes 152
  14.9 0.0 copy-done.3
  14.9 0.0 copy-start
  14.9 0.9 %copy-done = bf16[27,32,32]{2,1,0:T(8,128)(2,1)S(1)} copy-done((bf16[27,32,32]{2,1,0:T(8,128)(2,1)S(1)}, bf16[27,32,32]{2,1,0:T(8,128)(2,1)}, u32[]{:S(2)}) %copy-start) | copy-done | bytes 55320
  15.8 0.0 copy-start.1
  15.8 0.9 %copy-done.1 = bf16[27,32,32]{2,1,0:T(8,128)(2,1)S(1)} copy-done((bf16[27,32,32]{2,1,0:T(8,128)(2,1)S(1)}, bf16[27,32,32]{2,1,0:T(8,128)(2,1)}, u32[]{:S(2)}) %copy-start.1) | copy-done | bytes 55320
  16.7 0.6 %prepare.1 = (bf16[256,768]{1,0:T(8,128)(2,1)S(1)}, bf16[256,768]{1,0:T(8,128)(2,1)S(1)}, bf16[128,1792]{1,0:T(8,128)(2,1)S(1)}, bf16[256,768]{1,0:T(8,128)(2,1)...) custom-call(bf16[27,32,32]{2,1,0:T(8,128)(2,1)S(1)} %copy-done, ...), custom_call_target="tpu_custom_call" | custom-call | flops 1000000 | bytes 4000000 | tf_op jit(solution)/shard_map/prepare/pallas_call | solution.py:126
  17.4 0.0 collective-permute-done.4.r4
  17.4 0.3 collective-permute-done.3.r3
  17.7 3.3 %collective-permute-done.2.r2 = bf16[64,128]{1,0:T(8,128)(2,1)S(1)} collective-permute-done((bf16[64,128]{1,0:T(8,128)(2,1)S(1)}, bf16[64,128]{1,0:T(8,128)(2,1)S(1)}, u32[]{:S(2)}, u32[]{:S(2)}) %collective-permute-start.2) | collective-permute-done | bytes 16416 | tf_op jit(solution)/shard_map/ppermute | solution.py:390
  20.9 0.0 collective-permute-done.1.xl
  21.0 0.0 collective-permute-done.xr
  21.0 0.3 windows.1.own
  21.2 0.6 %collective-permute-start.6 = (bf16[256,128]{1,0:T(8,128)(2,1)S(1)}, bf16[256,128]{1,0:T(8,128)(2,1)S(1)}, u32[]{:S(2)}, u32[]{:S(2)}) collective-permute-start(bf16[256,128]{1,0:T(8,128)(2,1)S(1)} %windows.1.own), channel_id=1, source_target_pairs={{32,64},{64,32},{96,128},{128,96},{160,192},{192,160},{224,0},{0,2... | collective-permute-start | bytes 196616 | tf_op jit(solution)/shard_map/ppermute | solution.py:399
  21.9 1.0 %collective-permute-start.5 = (bf16[256,128]{1,0:T(8,128)(2,1)S(1)}, bf16[256,128]{1,0:T(8,128)(2,1)S(1)}, u32[]{:S(2)}, u32[]{:S(2)}) collective-permute-start(bf16[256,128]{1,0:T(8,128)(2,1)S(1)} %windows.1.own), channel_id=1, source_target_pairs={{0,32},{32,0},{64,96},{96,64},{128,160},{160,128},{192,224},{224,1... | collective-permute-start | bytes 196616 | tf_op jit(solution)/shard_map/ppermute | solution.py:399
  22.9 3.3 %collective-permute-done.6.cross = bf16[256,128]{1,0:T(8,128)(2,1)S(1)} collective-permute-done((bf16[256,128]{1,0:T(8,128)(2,1)S(1)}, bf16[256,128]{1,0:T(8,128)(2,1)S(1)}, u32[]{:S(2)}, u32[]{:S(2)}) %collective-permute-start.6) | collective-permute-done | bytes 65568 | tf_op jit(solution)/shard_map/ppermute | solution.py:399
  26.2 0.0 collective-permute-done.5.pair
  26.2 5.7 %aggregate.1 = bf16[32,96,128]{2,1,0:T(8,128)(2,1)} custom-call(bf16[256,128]{1,0:T(8,128)(2,1)S(1)} %windows.1.own, bf16[256,128]{1,0:T(8,128)(2,1)S(1)} %collective-permute-done.5.pair, bf16[256,128]{1,0:T(8,128)(2,1)S(1)} %collective-permute-done.6.cross, bf16[256,768]{1,0:T(8,128)(2,1)S(1)} %get-tuple-element.14.t_own, ...), custom_call_target="tpu_custom_call" | custom-call | tf_op jit(solution)/shard_map/aggregate/pallas_call | solution.py:373
  (2 shorter events, 0.0 us)
Async XLA Ops:
  0.7 0.7 %copy-start.4 = (bf16[32,2,128]{2,1,0:T(2,128)(2,1)S(1)}, bf16[32,2,128]{2,1,0:T(2,128)(2,1)}, u32[]{:S(2)}) copy-start(bf16[32,2,128]{2,1,0:T(2,128)(2,1)} %param.7) | copy-start | bytes 49156
  0.7 0.7 %copy-start.5 = (bf16[32,2,128]{2,1,0:T(2,128)(2,1)S(1)}, bf16[32,2,128]{2,1,0:T(2,128)(2,1)}, u32[]{:S(2)}) copy-start(bf16[32,2,128]{2,1,0:T(2,128)(2,1)} %param.8) | copy-start | bytes 49156
  1.5 19.5 %collective-permute-start.1 = (bf16[144,128]{1,0:T(8,128)(2,1)S(1)}, bf16[144,128]{1,0:T(8,128)(2,1)S(1)}, u32[]{:S(2)}, u32[]{:S(2)}) collective-permute-start(bf16[144,128]{1,0:T(8,128)(2,1)S(1)} %maximum_maximum_fusion.xo), channel_id=1, source_target_pairs={{0,1},{1,2},{2,3},{3,4},{4,5},{5,6},{6,7},{7,8},{8,9},{9,10},{10,1... | collective-permute-start | bytes 110600 | tf_op jit(solution)/shard_map/ppermute | solution.py:390
  3.5 17.5 %collective-permute-start = (bf16[144,128]{1,0:T(8,128)(2,1)S(1)}, bf16[144,128]{1,0:T(8,128)(2,1)S(1)}, u32[]{:S(2)}, u32[]{:S(2)}) collective-permute-start(bf16[144,128]{1,0:T(8,128)(2,1)S(1)} %maximum_maximum_fusion.xo), channel_id=1, source_target_pairs={{0,31},{1,0},{2,1},{3,2},{4,3},{5,4},{6,5},{7,6},{8,7},{9,8},{10,9... | collective-permute-start | bytes 110600 | tf_op jit(solution)/shard_map/ppermute | solution.py:390
  3.6 13.8 %collective-permute-start.4 = (bf16[64,128]{1,0:T(8,128)(2,1)S(1)}, bf16[64,128]{1,0:T(8,128)(2,1)S(1)}, u32[]{:S(2)}, u32[]{:S(2)}) collective-permute-start(bf16[64,128]{1,0:T(8,128)(2,1)S(1)} %bitcast.14), channel_id=1, source_target_pairs={{0,4},{1,5},{2,6},{3,7},{4,8},{5,9},{6,10},{7,11},{8,12},{9,13},{1... | collective-permute-start | bytes 49160 | tf_op jit(solution)/shard_map/ppermute | solution.py:390
  9.9 7.8 %collective-permute-start.3 = (bf16[64,128]{1,0:T(8,128)(2,1)S(1)}, bf16[64,128]{1,0:T(8,128)(2,1)S(1)}, u32[]{:S(2)}, u32[]{:S(2)}) collective-permute-start(bf16[64,128]{1,0:T(8,128)(2,1)S(1)} %bitcast.15), channel_id=1, source_target_pairs={{0,3},{1,4},{2,5},{3,6},{4,7},{5,8},{6,9},{7,10},{8,11},{9,12},{10... | collective-permute-start | bytes 49160 | tf_op jit(solution)/shard_map/ppermute | solution.py:390
  14.2 6.7 %collective-permute-start.2 = (bf16[64,128]{1,0:T(8,128)(2,1)S(1)}, bf16[64,128]{1,0:T(8,128)(2,1)S(1)}, u32[]{:S(2)}, u32[]{:S(2)}) collective-permute-start(bf16[64,128]{1,0:T(8,128)(2,1)S(1)} %bitcast.16), channel_id=1, source_target_pairs={{0,2},{1,3},{2,4},{3,5},{4,6},{5,7},{6,8},{7,9},{8,10},{9,11},{10,... | collective-permute-start | bytes 49160 | tf_op jit(solution)/shard_map/ppermute | solution.py:390
  14.2 0.7 %copy-start.2 = (f32[32]{0:T(128)S(1)}, f32[32]{0:T(128)}, u32[]{:S(2)}) copy-start(f32[32]{0:T(128)} %param.11) | copy-start | bytes 388
  14.2 0.7 %copy-start.3 = (f32[32]{0:T(128)S(1)}, f32[32]{0:T(128)}, u32[]{:S(2)}) copy-start(f32[32]{0:T(128)} %param.13) | copy-start | bytes 388
  14.9 0.9 %copy-start = (bf16[27,32,32]{2,1,0:T(8,128)(2,1)S(1)}, bf16[27,32,32]{2,1,0:T(8,128)(2,1)}, u32[]{:S(2)}) copy-start(bf16[27,32,32]{2,1,0:T(8,128)(2,1)} %w1_ref.1) | copy-start | bytes 165892
  15.8 0.9 %copy-start.1 = (bf16[27,32,32]{2,1,0:T(8,128)(2,1)S(1)}, bf16[27,32,32]{2,1,0:T(8,128)(2,1)}, u32[]{:S(2)}) copy-start(bf16[27,32,32]{2,1,0:T(8,128)(2,1)} %w2_ref.1) | copy-start | bytes 165892
  21.2 5.0 %collective-permute-start.6 = (bf16[256,128]{1,0:T(8,128)(2,1)S(1)}, bf16[256,128]{1,0:T(8,128)(2,1)S(1)}, u32[]{:S(2)}, u32[]{:S(2)}) collective-permute-start(bf16[256,128]{1,0:T(8,128)(2,1)S(1)} %windows.1.own), channel_id=1, source_target_pairs={{32,64},{64,32},{96,128},{128,96},{160,192},{192,160},{224,0},{0,2... | collective-permute-start | bytes 196616 | tf_op jit(solution)/shard_map/ppermute | solution.py:399
  21.9 4.3 %collective-permute-start.5 = (bf16[256,128]{1,0:T(8,128)(2,1)S(1)}, bf16[256,128]{1,0:T(8,128)(2,1)S(1)}, u32[]{:S(2)}, u32[]{:S(2)}) collective-permute-start(bf16[256,128]{1,0:T(8,128)(2,1)S(1)} %windows.1.own), channel_id=1, source_target_pairs={{0,32},{32,0},{64,96},{96,64},{128,160},{160,128},{192,224},{224,1... | collective-permute-start | bytes 196616 | tf_op jit(solution)/shard_map/ppermute | solution.py:399

commit v4 on v3

--- a/solution.py
+++ b/solution.py
@@ -28,13 +28,13 @@
 
 
 def prepare(
-    w1_ref, w2_ref, b1_ref, b2_ref, own_ref, halo_ref, edge_ref, mid_ref, ends_ref, c1_ref, c2_ref, sel_ref
+    w_ref, b_ref, own_ref, halo_ref, edge_ref, mid_ref, ends_ref, c1_ref, c2_ref, sel_ref
 ):
     zero = jnp.zeros((C, C), F32)
 
-    def taps(ref):
+    def taps(base):
         return {
-            (a, b, e): ref[9 * a + 3 * b + e].astype(F32)
+            (a, b, e): w_ref[base + 9 * a + 3 * b + e].astype(F32)
             for a in range(3)
             for b in range(3)
             for e in range(3)
@@ -46,7 +46,7 @@
                 parts[q : q + 4], axis=1
             ).astype(BF16)
 
-    one = taps(w1_ref)
+    one = taps(0)
     for r in range(HR):
         for d in range(2):
             row = (r * 2 + d) * C
@@ -72,7 +72,7 @@
             ]
             + [zero] * 2,
         )
-    two = taps(w2_ref)
+    two = taps(27)
     for d in range(4):
         for h in range(RH):
             row = (d * RH + h) * C
@@ -93,7 +93,7 @@
         b = jnp.sum(jnp.where(eye, jnp.broadcast_to(b, (C, C)), 0.0), axis=1, keepdims=True)
         return jnp.broadcast_to(b, (C, CW))
 
-    one, two = column(b1_ref[...]), column(b2_ref[...])
+    one, two = column(b_ref[0:1, :]), column(b_ref[1:2, :])
     for p in range(8):
         c1_ref[p * C : (p + 1) * C, :] = one
         c2_ref[p * C : (p + 1) * C, :] = two
@@ -135,36 +135,80 @@
             jax.ShapeDtypeStruct((256, CW), F32),
             jax.ShapeDtypeStruct((512, 768), BF16),
         ),
-        in_specs=[VMEM] * 4,
+        in_specs=[VMEM] * 2,
         out_specs=[VMEM] * 8,
         cost_estimate=pl.CostEstimate(flops=1000000, bytes_accessed=4000000, transcendentals=0),
         compiler_params=pltpu.CompilerParams(vmem_limit_bytes=12 * MIB),
         name="prepare",
-    )(weight_one, weight_two, bias_one.reshape(1, C), bias_two.reshape(1, C))
-
-
-def cut(off_ref, xr, xl, r2, r3, r4, xo, after_ref, out_ref, tiles):
+    )(jnp.concatenate([weight_one, weight_two], axis=0), jnp.stack([bias_one, bias_two]))
+
+
+def pack(off_ref, lr_ref, out_ref):
+    out_ref[0:64, :] = lr_ref[64:128, :]
+    k = iota((16, CW), 0)
+    at = iota((16, CW), 1)
+    of_left = ((k < 2) & (at == k + 126)) | ((k >= 2) & (k < 4) & (at == k - 2))
+    of_right = (k >= 4) & (k < 6) & (at == k - 4)
+
+    def columns(chosen, rows):
+        return lax.dot_general(
+            jnp.where(chosen, 1.0, 0.0).astype(BF16),
+            rows,
+            (((1,), (1,)), ((), ())),
+            preferred_element_type=F32,
+        )
+
+    edge = columns(of_left, lr_ref[0:64, :]) + columns(of_right, lr_ref[64:128, :])
+    o = off_ref[0]
+    code = jnp.where(k == 6, o // 8, jnp.where(k == 7, o % 8, 0)).astype(F32)
+    edge = jnp.concatenate([edge, jnp.zeros((16, 64), F32)], axis=1) + code
+    out_ref[64:80, :] = edge.astype(BF16)
+
+
+def packed(offsets, lr):
+    return pl.pallas_call(
+        pack,
+        out_shape=jax.ShapeDtypeStruct((80, CW), BF16),
+        in_specs=[SMEM, VMEM],
+        out_specs=VMEM,
+        compiler_params=pltpu.CompilerParams(vmem_limit_bytes=2 * MIB),
+        name="pack",
+    )(offsets, lr)
+
+
+def cut(off_ref, xr, xl, x2, x3, x4, xo, lr_ref, after_ref, out_ref, tiles):
     col = lax.axis_index("cols")
-    last = lax.axis_size("cols") - 1
+    final = lax.axis_size("cols") - 1
     o = off_ref[0]
 
     def scalar_of(ref):
-        v = ref[128:144, :].astype(F32)
-        return jnp.max(v[0:1] * 8.0 + v[1:2]).astype(jnp.int32)
+        v = ref[64:80, :].astype(F32)
+        return jnp.max(v[6:7, 64:128] * 8.0 + v[7:8, 64:128]).astype(jnp.int32)
 
     o_l = scalar_of(xl)
     o_r = scalar_of(xr)
     dst = iota((64, 64), 0)
     src = iota((64, 64), 1)
     perm = jnp.where(src == (dst % C) * RH + dst // C, 1.0, 0.0).astype(BF16)
+    k = iota((16, CW), 0)
+    at = iota((16, CW), 1)
 
     def rows(x):
         return jnp.dot(perm, x, preferred_element_type=F32)
 
-    for t, x in enumerate((r4[...], r3[...], r2[...], xl[64:128, :], xo[64:128, :])):
+    def placed(ref, chosen):
+        edge = lax.dot_general(
+            ref[64:80, 0:64],
+            jnp.where(chosen, 1.0, 0.0).astype(BF16),
+            (((0,), (0,)), ((), ())),
+            preferred_element_type=F32,
+        )
+        return rows(edge.astype(BF16))
+
+    for t, x in enumerate((x4, x3, x2, xl, xo)):
         keep = (col + (t - 4) >= 0).astype(F32)
-        tiles[t] = rows(x) * keep
-    tiles[5] = rows(xr[64:128, :])
+        tiles[t] = rows(x[0:64, :]) * keep
+    tiles[5] = placed(xr, (k >= 4) & (k < 6) & (at == k - 4))
     lane = iota((64, CW), 1)
 
     def window(start):
@@ -179,31 +223,125 @@
     two = pltpu.roll(jnp.where(lane < s, tiles[t + 2], tiles[t + 1]), back, 1)
     wl = window(463 - o_l)[3]
     wr = window(529 - o_r)[3]
-    near = rows(xl[0:64, :]) * (col > 0).astype(F32)
-    far = rows(xr[0:64, :]) * (col < last).astype(F32)
-    border = jnp.where(lane < 50, wl, jnp.where(lane < 52, pltpu.roll(near, 52, 1), wr))
-    border = jnp.where((lane < 114), border, pltpu.roll(far, 114, 1))
-    border = jnp.where((lane < 116) & ((lane < 52) | (lane >= 64)), border, 0.0)
-    out_ref[0:64, :] = rows(xo[0:64, :]).astype(BF16)
+    near = placed(xl, (k < 2) & (at == k + 50)) * (col > 0).astype(F32)
+    far = placed(xr, (k >= 2) & (k < 4) & (at == k + 112)) * (col < final).astype(F32)
+    border = jnp.where(lane < 50, wl, jnp.where(lane < 64, near, jnp.where(lane < 114, wr, far)))
+    out_ref[0:64, :] = rows(lr_ref[0:64, :]).astype(BF16)
     out_ref[64:128, :] = one.astype(BF16)
     out_ref[128:192, :] = two.astype(BF16)
     out_ref[192:256, :] = border.astype(BF16)
 
 
-def windows(offsets, xr, xl, r2, r3, r4, xo, after):
+def windows(offsets, xr, xl, x2, x3, x4, xo, lr, after):
     return pl.pallas_call(
         cut,
         out_shape=jax.ShapeDtypeStruct((256, CW), BF16),
-        in_specs=[SMEM] + [VMEM] * 6 + [pl.BlockSpec(memory_space=pl.ANY)],
+        in_specs=[SMEM] + [VMEM] * 7 + [pl.BlockSpec(memory_space=pl.ANY)],
         out_specs=VMEM,
         scratch_shapes=[pltpu.VMEM((6, 64, CW), F32)],
         compiler_params=pltpu.CompilerParams(vmem_limit_bytes=4 * MIB),
         name="windows",
-    )(offsets, xr, xl, r2, r3, r4, xo, after)
+    )(offsets, xr, xl, x2, x3, x4, xo, lr, after)
+
+
+def border_cells(tiles, sel):
+    picked = jnp.dot(jnp.concatenate(tiles, axis=1), sel, preferred_element_type=F32)
+    cells = []
+    for e in range(3):
+        r = picked[:, (2 * e) * CW : (2 * e + 1) * CW]
+        lft = picked[:, (2 * e + 1) * CW : (2 * e + 2) * CW]
+        cells.append((r * lft).astype(BF16))
+    return cells
+
+
+class Rows:
+    def __init__(self, tiles, cells, refs):
+        left, self.win0, self.win1, _ = tiles
+        self.l0, self.l1, self.l2 = pltpu.roll(left, 1, 1), left, pltpu.roll(left, CW - 1, 1)
+        self.z = cells[1]
+        self.refs = refs
+        self.lane = iota((OD, CW), 1)
+        pad = jnp.zeros((OD, CW), BF16)
+        for ref in refs:
+            ref[0:OD, :] = pad
+            ref[(D + 1) * OD : (D + 2) * OD, :] = pad
+        self.held = {k: self.shifted(k) for k in (D, D + 1)}
+
+    def shifted(self, k):
+        if k == 0:
+            return self.win0
+        return pltpu.roll(jnp.where(self.lane < k, self.win1, self.win0), CW - k, 1)
+
+    def disparity(self, d):
+        k = D - 1 - d
+        base = (d + 1) * OD
+        self.held[k] = self.shifted(k)
+        border = pltpu.roll(self.z, (2 * CW - 1 - 2 * d) % CW, 1)
+        before, here, after = self.refs
+        before[base : base + OD, :] = jnp.where(self.lane == 0, border, self.l0 * self.held[k])
+        here[base : base + OD, :] = self.l1 * self.held[k + 1]
+        after[base : base + OD, :] = jnp.where(
+            self.lane == CW - 1, border, self.l2 * self.held.pop(k + 2)
+        )
+
+
+def window_rows(refs, j):
+    d0 = j * 4
+    return jnp.concatenate(
+        [
+            jnp.concatenate(
+                [ref[d0 * OD : d0 * OD + 256, :], ref[(d0 + 2) * OD : (d0 + 2) * OD + 256, :]], axis=1
+            )
+            for ref in refs
+        ],
+        axis=0,
+    )
+
+
+def blocks(groups, conv):
+    done = 0
+    for j in range(D // 4):
+        upto = min(D, 4 * j + 5)
+        for d in range(done, upto):
+            for g in groups:
+                g.disparity(d)
+        done = upto
+        conv(j)
+
+
+def begin(own, t_own, sel, vol_ref, cells_ref, acc_ref):
+    tiles = [own[t * 64 : t * 64 + 64, :] for t in range(4)]
+    cells = border_cells(tiles, sel[...])
+    for e in range(3):
+        cells_ref[e] = cells[e]
+    refs = [vol_ref.at[e] for e in range(3)]
+
+    def conv(j):
+        acc_ref[j] = jnp.dot(t_own[...], window_rows(refs, j), preferred_element_type=F32)
+
+    blocks([Rows(tiles, cells, refs)], conv)
+
+
+def begun(own, t_own, sel):
+    return pl.pallas_call(
+        begin,
+        out_shape=(
+            jax.ShapeDtypeStruct((3, (D + 2) * OD, CW), BF16),
+            jax.ShapeDtypeStruct((3, OD, CW), BF16),
+            jax.ShapeDtypeStruct((D // 4, 256, 256), F32),
+        ),
+        in_specs=[VMEM] * 3,
+        out_specs=[VMEM] * 3,
+        cost_estimate=pl.CostEstimate(
+            flops=2 * 12 * 256 * 768 * 256, bytes_accessed=6000000, transcendentals=0
+        ),
+        compiler_params=pltpu.CompilerParams(vmem_limit_bytes=12 * MIB),
+        name="begin",
+    )(own, t_own, sel)
 
 
 def aggregate(
-    own, pair, cross, t_own, t_halo, t_edge, t_mid, t_ends, c1, c2, sel, out_ref, vol, hid, stage
+    own_vol, own_cells, acc, pair, cross, t_halo, t_edge, t_mid, t_ends, c1, c2, sel, out_ref, vol, hid, stage
 ):
     row = lax.axis_index("rows")
     col = lax.axis_index("cols")
@@ -221,19 +359,20 @@
         down = jnp.where(odd, x, p)
         up = jnp.where(no_up, jnp.zeros_like(up), up)
         down = jnp.where(no_down, jnp.zeros_like(down), down)
-        return jnp.concatenate([up, own[part, :], down], axis=0)
-
-    left, win0, win1, edge = (tile(t) for t in range(4))
-
-    sources = jnp.concatenate([left, win0, win1, edge], axis=1)
-    picked = jnp.dot(sources, sel[...], preferred_element_type=F32)
-    cells = []
+        return up, down
+
+    ups, downs = zip(*(tile(t) for t in range(4)))
+    halo_cells = border_cells(
+        [jnp.concatenate([u, w], axis=0) for u, w in zip(ups, downs)], sel[...]
+    )
+    up_cells = [z[0:OD] for z in halo_cells]
+    down_cells = [z[OD:] for z in halo_cells]
+    up_refs = [vol.at[0, e] for e in range(3)]
+    down_refs = [vol.at[1, e] for e in range(3)]
+
+    around = []
     for e in range(3):
-        r = picked[:, (2 * e) * CW : (2 * e + 1) * CW]
-        lft = picked[:, (2 * e + 1) * CW : (2 * e + 2) * CW]
-        cells.append((r * lft).astype(BF16))
-    around = []
-    for z in cells:
+        z = jnp.concatenate([up_cells[e], own_cells[e], down_cells[e]], axis=0)
         around += [pltpu.roll(z, 2, 1), z, pltpu.roll(z, CW - 2, 1)]
     around.append(jnp.zeros((KE - 9 * VD, CW), BF16))
     h = jnp.dot(t_edge[...], jnp.concatenate(around, axis=0), preferred_element_type=F32)
@@ -243,44 +382,11 @@
     gone = (no_up & (hrow == 0)) | (no_down & (hrow == HR - 1))
     gone = gone | ((col == 0) & (lane % 2 == 1)) | ((col == cols_last) & (lane % 2 == 0))
     hcol = jnp.where(gone, 0.0, h).astype(BF16)
-    zcol = cells[1]
-
-    vlane = iota((OD, CW), 1)
-    first = vlane == 0
-    last = vlane == CW - 1
+
     pad = jnp.zeros((HD, CW), BF16)
     for e in range(3):
-        for g in range(3):
-            vol[g, e, 0:OD, :] = pad[0:OD]
-            vol[g, e, (D + 1) * OD : (D + 2) * OD, :] = pad[0:OD]
         hid[e, 0:HD, :] = pad
         hid[e, (D + 1) * HD : (D + 2) * HD, :] = pad
-    groups = []
-    for g in range(3):
-        part = slice(g * OD, (g + 1) * OD)
-        l1 = left[part]
-        groups.append(
-            (pltpu.roll(l1, 1, 1), l1, pltpu.roll(l1, CW - 1, 1), win0[part], win1[part], zcol[part])
-        )
-
-    def shifted(g, k):
-        w0, w1 = groups[g][3:5]
-        if k == 0:
-            return w0
-        return pltpu.roll(jnp.where(vlane < k, w1, w0), CW - k, 1)
-
-    held = {(g, k): shifted(g, k) for g in range(3) for k in (D, D + 1)}
-
-    def disparity(d):
-        k = D - 1 - d
-        base = (d + 1) * OD
-        for g in range(3):
-            l0, l1, l2, _, _, z = groups[g]
-            held[g, k] = shifted(g, k)
-            border = pltpu.roll(z, (2 * CW - 1 - 2 * d) % CW, 1)
-            vol[g, 0, base : base + OD, :] = jnp.where(first, border, l0 * held[g, k])
-            vol[g, 1, base : base + OD, :] = l1 * held[g, k + 1]
-            vol[g, 2, base : base + OD, :] = jnp.where(last, border, l2 * held.pop((g, k + 2)))
 
     hl = iota((C, CW), 1)
     hfirst = hl == 0
@@ -288,25 +394,8 @@
 
     def conv_one(j):
         d0 = j * 4
-
-        def rhs(g):
-            return jnp.concatenate(
-                [
-                    jnp.concatenate(
-                        [
-                            vol[g, e, d0 * OD : d0 * OD + 256, :],
-                            vol[g, e, (d0 + 2) * OD : (d0 + 2) * OD + 256, :],
-                        ],
-                        axis=1,
-                    )
-                    for e in range(3)
-                ],
-                axis=0,
-            )
-
-        mine = jnp.dot(t_own[...], rhs(1), preferred_element_type=F32)
-        top = jnp.dot(t_halo[0:128, :], rhs(0), preferred_element_type=F32)
-        bottom = jnp.dot(t_halo[128:256, :], rhs(2), preferred_element_type=F32)
+        top = jnp.dot(t_halo[0:128, :], window_rows(up_refs, j), preferred_element_type=F32)
+        bottom = jnp.dot(t_halo[128:256, :], window_rows(down_refs, j), preferred_element_type=F32)
         for i in range(2):
             cut = slice(i * CW, (i + 1) * CW)
             for dd in range(2):
@@ -316,7 +405,7 @@
                     at = (r * 2 + dd) * C
                     halo = top if r < 2 else bottom
                     ha = at % 128
-                    h = mine[at : at + C, cut] + halo[ha : ha + C, cut] + c1[0:C, :]
+                    h = acc[j, at : at + C, cut] + halo[ha : ha + C, cut] + c1[0:C, :]
                     h = jnp.maximum(h, 0.0)
                     if r == 0:
                         h = jnp.where(no_up, 0.0, h)
@@ -353,36 +442,30 @@
                 end = low if p < 4 else high
                 at = p * C
                 ea = at % 128
-                v = vol[1, 1, (d0 + 4 * i + 1) * OD + at : (d0 + 4 * i + 1) * OD + at + C, :]
+                v = own_vol[1, (d0 + 4 * i + 1) * OD + at : (d0 + 4 * i + 1) * OD + at + C, :]
                 a = mid[at : at + C, cut] + end[ea : ea + C, cut] + c2[0:C, :] + v.astype(F32)
                 stage[j % 2, pl.ds(8 * i + p, C, stride=16), :] = a
         out_ref[:, j * 16 : j * 16 + 16, :] = stage[j % 2].reshape(C, 16, CW).astype(BF16)
 
-    done = 0
-    for j in range(D // 4):
-        upto = min(D, 4 * j + 5)
-        for d in range(done, upto):
-            disparity(d)
-        done = upto
-        conv_one(j)
+    blocks([Rows(ups, up_cells, up_refs), Rows(downs, down_cells, down_refs)], conv_one)
     for j in range(D // 8):
         conv_two(j)
 
 
-def aggregated(own, pair, cross, *ready):
+def aggregated(first, pair, cross, t_own, *ready):
     return pl.pallas_call(
         aggregate,
         out_shape=jax.ShapeDtypeStruct((C, D * RH, CW), BF16),
-        in_specs=[VMEM] * 11,
+        in_specs=[VMEM] * 12,
         out_specs=VMEM,
         scratch_shapes=[
-            pltpu.VMEM((3, 3, (D + 2) * OD, CW), BF16),
+            pltpu.VMEM((2, 3, (D + 2) * OD, CW), BF16),
             pltpu.VMEM((3, (D + 2) * HD, CW), BF16),
             pltpu.VMEM((2, 512, CW), F32),
         ],
         compiler_params=pltpu.CompilerParams(vmem_limit_bytes=32 * MIB),
         name="aggregate",
-    )(own, pair, cross, *ready)
+    )(*first, pair, cross, *ready)
 
 
 def ring(x, axis, by):
@@ -400,22 +483,18 @@
 
 
 def body(left, right, offsets, weight_one, bias_one, weight_two, bias_two):
-    r = right.reshape(C * RH, CW)
-    l = left.reshape(C * RH, CW)
-    o = offsets[0]
-    place = jnp.arange(16, dtype=jnp.int32)[:, None]
-    code = jnp.where(place == 0, o // 8, jnp.where(place == 1, o % 8, 0)).astype(BF16)
-    x = jnp.concatenate([l, r, jnp.broadcast_to(code, (16, CW))], axis=0)
-    r4 = ring(r, "cols", 4)
-    r3 = ring(r, "cols", 3)
-    r2 = ring(r, "cols", 2)
+    lr = jnp.concatenate([left.reshape(C * RH, CW), right.reshape(C * RH, CW)], axis=0)
+    x = packed(offsets, lr)
+    xr = ring(x, "cols", -1)
     xl = ring(x, "cols", 1)
-    xr = ring(x, "cols", -1)
+    x2 = ring(x, "cols", 2)
+    x3 = ring(x, "cols", 3)
+    x4 = ring(x, "cols", 4)
     ready = prepared(weight_one, weight_two, bias_one, bias_two)
-    own = windows(offsets, xr, xl, r2, r3, r4, x, ready[5])
+    own = windows(offsets, xr, xl, x2, x3, x4, x, lr, ready[5])
     pair = swap(own, "rows", 0)
     cross = swap(own, "rows", 1)
-    out = aggregated(own, pair, cross, *ready)
+    out = aggregated(begun(own, ready[0], ready[7]), pair, cross, *ready)
     return out.reshape(C, D, RH, CW)
 
 

time: 32.3 us -> 29 us (0.90)
  the two profiles are of different devices: /device:TPU:56 before, /device:TPU:1 now
where the time goes in v4:
time: 29 us; the launch traced here: 28.7 us
  starting transfers between devices  17.3 us (60%)
  Pallas kernels  8.01 us (28%)
  other arithmetic  2.55 us (9%)
  between operations  0.72 us (2%)
    ppermute x5, starting transfers between devices, ring(): return lax.ppermute(x, axis, [(i, (i + by) % n) for i in range(n)])  14.2 us
    pallas_call x1, Pallas kernels, aggregated(): pl.pallas_call(aggregate, out_shape=jax.ShapeDtypeStruct((C, D * RH, CW),...  5.03 us
    ppermute x2, starting transfers between devices, swap(): return lax.ppermute(x, axis, pairs)  3.15 us
    pallas_call x1, Pallas kernels, begun(): pl.pallas_call(begin, out_shape=(jax.ShapeDtypeStruct((3, (D + 2) * OD, C...  1.84 us
    concatenate x1, other arithmetic, prepared(): jnp.concatenate([weight_one, weight_two], axis=0)  1.13 us
    concatenate x1, other arithmetic, body(): jnp.concatenate([left.reshape(C * RH, CW), right.reshape(C * RH, CW)], ax...  0.74 us
    another operation x1, other arithmetic, prepared(): jnp.stack([bias_one, bias_two])  0.68 us
    pallas_call x1, Pallas kernels, prepared(): pl.pallas_call(prepare, out_shape=(jax.ShapeDtypeStruct((256, KK), BF16),...  0.61 us
  transfers between devices with their start and end apart: 7, of which 1 were waited for; matrix products, arithmetic and copies ran while one was open for 6% of the time, Pallas kernels for 9%

profile of v4, /device:TPU:1, one launch (start us, length us, event | category | flops | bytes accessed | tf_op | source)
XLA Modules:
  0.0 28.7 jit_solution(15818795463004185682)
XLA Ops:
  0.7 0.7 %pad_maximum_fusion.1.lr_ref = bf16[128,128]{1,0:T(8,128)(2,1)S(1)} fusion(bf16[64,128]{1,0:T(8,128)(2,1)} %bitcast.5, bf16[64,128]{1,0:T(8,128)(2,1)} %bitcast.6), kind=kLoop, calls=%fused_computation.1 | loop fusion | flops 65536 | bytes 65536 | tf_op jit(solution)/shard_map/concatenate | solution.py:486
  1.4 0.1 pack.1.xo
  1.5 7.7 %collective-permute-start.4 = (bf16[80,128]{1,0:T(8,128)(2,1)S(1)}, bf16[80,128]{1,0:T(8,128)(2,1)S(1)}, u32[]{:S(2)}, u32[]{:S(2)}) collective-permute-start(bf16[80,128]{1,0:T(8,128)(2,1)S(1)} %pack.1.xo), channel_id=1, source_target_pairs={{0,4},{1,5},{2,6},{3,7},{4,8},{5,9},{6,10},{7,11},{8,12},{9,13},{1... | collective-permute-start | bytes 61448 | tf_op jit(solution)/shard_map/ppermute | solution.py:473
  9.3 1.6 %collective-permute-start.3 = (bf16[80,128]{1,0:T(8,128)(2,1)S(1)}, bf16[80,128]{1,0:T(8,128)(2,1)S(1)}, u32[]{:S(2)}, u32[]{:S(2)}) collective-permute-start(bf16[80,128]{1,0:T(8,128)(2,1)S(1)} %pack.1.xo), channel_id=1, source_target_pairs={{0,3},{1,4},{2,5},{3,6},{4,7},{5,8},{6,9},{7,10},{8,11},{9,12},{10... | collective-permute-start | bytes 61448 | tf_op jit(solution)/shard_map/ppermute | solution.py:473
  10.9 0.0 collective-permute-start.2
  10.9 1.1 %collective-permute-start.1 = (bf16[80,128]{1,0:T(8,128)(2,1)S(1)}, bf16[80,128]{1,0:T(8,128)(2,1)S(1)}, u32[]{:S(2)}, u32[]{:S(2)}) collective-permute-start(bf16[80,128]{1,0:T(8,128)(2,1)S(1)} %pack.1.xo), channel_id=1, source_target_pairs={{0,1},{1,2},{2,3},{3,4},{4,5},{5,6},{6,7},{7,8},{8,9},{9,10},{10,1... | collective-permute-start | bytes 61448 | tf_op jit(solution)/shard_map/ppermute | solution.py:473
  12.0 3.7 %collective-permute-start = (bf16[80,128]{1,0:T(8,128)(2,1)S(1)}, bf16[80,128]{1,0:T(8,128)(2,1)S(1)}, u32[]{:S(2)}, u32[]{:S(2)}) collective-permute-start(bf16[80,128]{1,0:T(8,128)(2,1)S(1)} %pack.1.xo), channel_id=1, source_target_pairs={{0,31},{1,0},{2,1},{3,2},{4,3},{5,4},{6,5},{7,6},{8,7},{9,8},{10,9... | collective-permute-start | bytes 61448 | tf_op jit(solution)/shard_map/ppermute | solution.py:473
  15.7 1.1 %pad_maximum_fusion.w_ref = bf16[54,32,32]{2,1,0:T(8,128)(2,1)S(1)} fusion(bf16[27,32,32]{2,1,0:T(8,128)(2,1)} %param.12, bf16[27,32,32]{2,1,0:T(8,128)(2,1)} %param.10), kind=kLoop, calls=%fused_computation | loop fusion | flops 55296 | bytes 221184 | tf_op jit(solution)/shard_map/concatenate | solution.py:143
  16.8 0.7 %pad_maximum_fusion.2.b_ref = f32[2,32]{1,0:T(2,128)S(1)} fusion(f32[1,32]{1,0:T(1,128)} %bitcast.7, f32[1,32]{1,0:T(1,128)} %bitcast.8), kind=kLoop, calls=%fused_computation.2 | loop fusion | flops 64 | bytes 512 | tf_op jit(solution)/shard_map/stack | solution.py:143
  17.5 0.6 %prepare.1 = (bf16[256,768]{1,0:T(8,128)(2,1)S(1)}, bf16[256,768]{1,0:T(8,128)(2,1)S(1)}, bf16[128,1792]{1,0:T(8,128)(2,1)S(1)}, bf16[256,768]{1,0:T(8,128)(2,1)...) custom-call(bf16[54,32,32]{2,1,0:T(8,128)(2,1)S(1)} %pad_maximum_fus, ...), custom_call_target="tpu_custom_call" | custom-call | flops 1000000 | bytes 4000000 | tf_op jit(solution)/shard_map/prepare/pallas_call | solution.py:126
  18.1 0.0 collective-permute-done.4.x4
  18.2 0.0 collective-permute-done.3.x3
  18.2 0.0 collective-permute-done.2.x2
  18.2 0.0 collective-permute-done.1.xl
  18.2 0.0 collective-permute-done.xr
  18.2 0.4 %windows.1.own = bf16[256,128]{1,0:T(8,128)(2,1)S(1)} custom-call(s32[1]{0:T(128)S(6)} %copy.8.off_ref, bf16[80,128]{1,0:T(8,128)(2,1)S(1)} %collective-permute-done.xr, bf16[80,128]{1,0:T(8,128)(2,1)S(1)} %collective-permute-done.1.xl, bf16[80,128]{1,0:T(8,128)(2,1)S(1)} %collective-permute-done.2.x2, bf16[80,128]{1,0:T(8,128)(2,1)S(1)} %collective-permute-done.3.x3, ...), custom_call_target="tpu_custom_call" | custom-call | tf_op jit(solution)/shard_map/windows/pallas_call | solution.py:236
  18.6 3.1 %collective-permute-start.6 = (bf16[256,128]{1,0:T(8,128)(2,1)S(1)}, bf16[256,128]{1,0:T(8,128)(2,1)S(1)}, u32[]{:S(2)}, u32[]{:S(2)}) collective-permute-start(bf16[256,128]{1,0:T(8,128)(2,1)S(1)} %windows.1.own), channel_id=1, source_target_pairs={{32,64},{64,32},{96,128},{128,96},{160,192},{192,160},{224,0},{0,2... | collective-permute-start | bytes 196616 | tf_op jit(solution)/shard_map/ppermute | solution.py:482
  21.8 0.0 collective-permute-start.5
  21.8 1.8 %begin.1 = (bf16[3,3200,128]{2,1,0:T(8,128)(2,1)S(1)}, bf16[3,64,128]{2,1,0:T(8,128)(2,1)S(1)}, f32[12,256,256]{2,1,0:T(8,128)S(1)}) custom-call(bf16[256,128]{1,0:T(8,128)(2,1)S(1)} %windows.1.own, bf16[256,768]{1,0:T(8,128)(2,1)S(1)} %get-tuple-element.17.t_own, bf16[512,768]{1,0:T(8,128)(2,1)S(1)} %get-tuple-element.18.sel), custom_call_target="tpu_custom_call" | custom-call | flops 1207959552 | bytes 6000000 | tf_op jit(solution)/shard_map/begin/pallas_call | solution.py:326
  23.6 0.1 collective-permute-done.6.cross
  23.7 0.0 collective-permute-done.5.pair
  23.7 5.0 %aggregate.1 = bf16[32,96,128]{2,1,0:T(8,128)(2,1)} custom-call(bf16[3,3200,128]{2,1,0:T(8,128)(2,1)S(1)} %get-tuple-element.19.own_vol, bf16[3,64,128]{2,1,0:T(8,128)(2,1)S(1)} %get-tuple-element.20.own_cells, f32[12,256,256]{2,1,0:T(8,128)S(1)} %get-tuple-element.21.acc, bf16[256,128]{1,0:T(8,128)(2,1)S(1)} %collective-permute-done.5.pair, ...), custom_call_target="tpu_custom_call" | custom-call | tf_op jit(solution)/shard_map/aggregate/pallas_call | solution.py:456
Async XLA Ops:
  1.5 16.6 %collective-permute-start.4 = (bf16[80,128]{1,0:T(8,128)(2,1)S(1)}, bf16[80,128]{1,0:T(8,128)(2,1)S(1)}, u32[]{:S(2)}, u32[]{:S(2)}) collective-permute-start(bf16[80,128]{1,0:T(8,128)(2,1)S(1)} %pack.1.xo), channel_id=1, source_target_pairs={{0,4},{1,5},{2,6},{3,7},{4,8},{5,9},{6,10},{7,11},{8,12},{9,13},{1... | collective-permute-start | bytes 61448 | tf_op jit(solution)/shard_map/ppermute | solution.py:473
  9.3 8.9 %collective-permute-start.3 = (bf16[80,128]{1,0:T(8,128)(2,1)S(1)}, bf16[80,128]{1,0:T(8,128)(2,1)S(1)}, u32[]{:S(2)}, u32[]{:S(2)}) collective-permute-start(bf16[80,128]{1,0:T(8,128)(2,1)S(1)} %pack.1.xo), channel_id=1, source_target_pairs={{0,3},{1,4},{2,5},{3,6},{4,7},{5,8},{6,9},{7,10},{8,11},{9,12},{10... | collective-permute-start | bytes 61448 | tf_op jit(solution)/shard_map/ppermute | solution.py:473
  10.9 7.2 %collective-permute-start.2 = (bf16[80,128]{1,0:T(8,128)(2,1)S(1)}, bf16[80,128]{1,0:T(8,128)(2,1)S(1)}, u32[]{:S(2)}, u32[]{:S(2)}) collective-permute-start(bf16[80,128]{1,0:T(8,128)(2,1)S(1)} %pack.1.xo), channel_id=1, source_target_pairs={{0,2},{1,3},{2,4},{3,5},{4,6},{5,7},{6,8},{7,9},{8,10},{9,11},{10,... | collective-permute-start | bytes 61448 | tf_op jit(solution)/shard_map/ppermute | solution.py:473
  10.9 7.3 %collective-permute-start.1 = (bf16[80,128]{1,0:T(8,128)(2,1)S(1)}, bf16[80,128]{1,0:T(8,128)(2,1)S(1)}, u32[]{:S(2)}, u32[]{:S(2)}) collective-permute-start(bf16[80,128]{1,0:T(8,128)(2,1)S(1)} %pack.1.xo), channel_id=1, source_target_pairs={{0,1},{1,2},{2,3},{3,4},{4,5},{5,6},{6,7},{7,8},{8,9},{9,10},{10,1... | collective-permute-start | bytes 61448 | tf_op jit(solution)/shard_map/ppermute | solution.py:473
  12.0 6.2 %collective-permute-start = (bf16[80,128]{1,0:T(8,128)(2,1)S(1)}, bf16[80,128]{1,0:T(8,128)(2,1)S(1)}, u32[]{:S(2)}, u32[]{:S(2)}) collective-permute-start(bf16[80,128]{1,0:T(8,128)(2,1)S(1)} %pack.1.xo), channel_id=1, source_target_pairs={{0,31},{1,0},{2,1},{3,2},{4,3},{5,4},{6,5},{7,6},{8,7},{9,8},{10,9... | collective-permute-start | bytes 61448 | tf_op jit(solution)/shard_map/ppermute | solution.py:473
  18.6 5.1 %collective-permute-start.6 = (bf16[256,128]{1,0:T(8,128)(2,1)S(1)}, bf16[256,128]{1,0:T(8,128)(2,1)S(1)}, u32[]{:S(2)}, u32[]{:S(2)}) collective-permute-start(bf16[256,128]{1,0:T(8,128)(2,1)S(1)} %windows.1.own), channel_id=1, source_target_pairs={{32,64},{64,32},{96,128},{128,96},{160,192},{192,160},{224,0},{0,2... | collective-permute-start | bytes 196616 | tf_op jit(solution)/shard_map/ppermute | solution.py:482
  21.8 2.0 %collective-permute-start.5 = (bf16[256,128]{1,0:T(8,128)(2,1)S(1)}, bf16[256,128]{1,0:T(8,128)(2,1)S(1)}, u32[]{:S(2)}, u32[]{:S(2)}) collective-permute-start(bf16[256,128]{1,0:T(8,128)(2,1)S(1)} %windows.1.own), channel_id=1, source_target_pairs={{0,32},{32,0},{64,96},{96,64},{128,160},{160,128},{192,224},{224,1... | collective-permute-start | bytes 196616 | tf_op jit(solution)/shard_map/ppermute | solution.py:482

commit v5 on v4

--- a/solution.py
+++ b/solution.py
@@ -309,7 +309,7 @@
         conv(j)
 
 
-def begin(own, t_own, sel, vol_ref, cells_ref, acc_ref):
+def begin(own, t_own, c1, sel, vol_ref, cells_ref, acc_ref):
     tiles = [own[t * 64 : t * 64 + 64, :] for t in range(4)]
     cells = border_cells(tiles, sel[...])
     for e in range(3):
@@ -317,12 +317,13 @@
     refs = [vol_ref.at[e] for e in range(3)]
 
     def conv(j):
-        acc_ref[j] = jnp.dot(t_own[...], window_rows(refs, j), preferred_element_type=F32)
+        y = jnp.dot(t_own[...], window_rows(refs, j), preferred_element_type=F32)
+        acc_ref[j] = y + jnp.concatenate([c1[...], c1[...]], axis=1)
 
     blocks([Rows(tiles, cells, refs)], conv)
 
 
-def begun(own, t_own, sel):
+def begun(own, t_own, c1, sel):
     return pl.pallas_call(
         begin,
         out_shape=(
@@ -330,18 +331,34 @@
             jax.ShapeDtypeStruct((3, OD, CW), BF16),
             jax.ShapeDtypeStruct((D // 4, 256, 256), F32),
         ),
-        in_specs=[VMEM] * 3,
+        in_specs=[VMEM] * 4,
         out_specs=[VMEM] * 3,
         cost_estimate=pl.CostEstimate(
             flops=2 * 12 * 256 * 768 * 256, bytes_accessed=6000000, transcendentals=0
         ),
         compiler_params=pltpu.CompilerParams(vmem_limit_bytes=12 * MIB),
         name="begin",
-    )(own, t_own, sel)
+    )(own, t_own, c1, sel)
 
 
 def aggregate(
-    own_vol, own_cells, acc, pair, cross, t_halo, t_edge, t_mid, t_ends, c1, c2, sel, out_ref, vol, hid, stage
+    own_vol,
+    own_cells,
+    acc,
+    pair,
+    cross,
+    t_halo,
+    t_edge,
+    t_mid,
+    t_ends,
+    c1,
+    c2,
+    sel,
+    out_ref,
+    vol,
+    hid,
+    ready,
+    sems,
 ):
     row = lax.axis_index("rows")
     col = lax.axis_index("cols")
@@ -405,7 +422,7 @@
                     at = (r * 2 + dd) * C
                     halo = top if r < 2 else bottom
                     ha = at % 128
-                    h = acc[j, at : at + C, cut] + halo[ha : ha + C, cut] + c1[0:C, :]
+                    h = acc[j, at : at + C, cut] + halo[ha : ha + C, cut]
                     h = jnp.maximum(h, 0.0)
                     if r == 0:
                         h = jnp.where(no_up, 0.0, h)
@@ -418,38 +435,53 @@
                     hid[1, base : base + C, :] = h
                     hid[2, base : base + C, :] = jnp.where(hlast, b, pltpu.roll(h, CW - 1, 1))
 
+    def hidden_rows(at, *more):
+        return jnp.concatenate(
+            [
+                jnp.concatenate([hid[e, x * HD : x * HD + 256, :] for x in (at, *more)], axis=1)
+                for e in range(3)
+            ],
+            axis=0,
+        )
+
+    ends = {}
+
     def conv_two(j):
         d0 = j * 8
-
-        def rhs(i):
-            at = (d0 + 2 * i) * HD
-            return jnp.concatenate(
-                [
-                    jnp.concatenate(
-                        [hid[e, at : at + 256, :], hid[e, at + 4 * HD : at + 4 * HD + 256, :]], axis=1
-                    )
-                    for e in range(3)
-                ],
-                axis=0,
-            )
-
-        mid = jnp.dot(t_mid[...], rhs(1), preferred_element_type=F32)
-        low = jnp.dot(t_ends[0:128, :], rhs(0), preferred_element_type=F32)
-        high = jnp.dot(t_ends[128:256, :], rhs(2), preferred_element_type=F32)
+        mid = jnp.dot(t_mid[...], hidden_rows(d0 + 2, d0 + 6), preferred_element_type=F32)
+        both = jnp.dot(t_ends[...], hidden_rows(d0, d0 + 4), preferred_element_type=F32)
+        ends[2 * j] = both[:, 0:CW]
+        ends[2 * j + 1] = both[:, CW:]
+        return mid
+
+    def result(j, mid):
+        d0 = j * 8
+        parts = []
         for i in range(2):
-            cut = slice(i * CW, (i + 1) * CW)
+            low = ends.pop(2 * j + i)
+            high = ends[2 * j + i + 1]
             for p in range(8):
-                end = low if p < 4 else high
                 at = p * C
-                ea = at % 128
+                end = low[at : at + C] if p < 4 else high[at : at + C]
                 v = own_vol[1, (d0 + 4 * i + 1) * OD + at : (d0 + 4 * i + 1) * OD + at + C, :]
-                a = mid[at : at + C, cut] + end[ea : ea + C, cut] + c2[0:C, :] + v.astype(F32)
-                stage[j % 2, pl.ds(8 * i + p, C, stride=16), :] = a
-        out_ref[:, j * 16 : j * 16 + 16, :] = stage[j % 2].reshape(C, 16, CW).astype(BF16)
+                a = mid[at : at + C, i * CW : (i + 1) * CW] + end + c2[0:C, :] + v.astype(F32)
+                parts.append(a)
+        ready[j] = jnp.swapaxes(jnp.stack(parts, axis=0).astype(BF16), 0, 1)
+        copy = pltpu.make_async_copy(ready.at[j], out_ref.at[:, pl.ds(j * 16, 16), :], sems.at[j])
+        copy.start()
+        return copy
 
     blocks([Rows(ups, up_cells, up_refs), Rows(downs, down_cells, down_refs)], conv_one)
-    for j in range(D // 8):
-        conv_two(j)
+    copies = []
+    mid = conv_two(0)
+    for j in range(1, D // 8):
+        later = conv_two(j)
+        copies.append(result(j - 1, mid))
+        mid = later
+    ends[D // 4] = jnp.dot(t_ends[...], hidden_rows(D), preferred_element_type=F32)
+    copies.append(result(D // 8 - 1, mid))
+    for copy in copies:
+        copy.wait()
 
 
 def aggregated(first, pair, cross, t_own, *ready):
@@ -457,11 +489,12 @@
         aggregate,
         out_shape=jax.ShapeDtypeStruct((C, D * RH, CW), BF16),
         in_specs=[VMEM] * 12,
-        out_specs=VMEM,
+        out_specs=pl.BlockSpec(memory_space=pl.ANY),
         scratch_shapes=[
             pltpu.VMEM((2, 3, (D + 2) * OD, CW), BF16),
             pltpu.VMEM((3, (D + 2) * HD, CW), BF16),
-            pltpu.VMEM((2, 512, CW), F32),
+            pltpu.VMEM((D // 8, C, 16, CW), BF16),
+            pltpu.SemaphoreType.DMA((D // 8,)),
         ],
         compiler_params=pltpu.CompilerParams(vmem_limit_bytes=32 * MIB),
         name="aggregate",
@@ -494,7 +527,7 @@
     own = windows(offsets, xr, xl, x2, x3, x4, x, lr, ready[5])
     pair = swap(own, "rows", 0)
     cross = swap(own, "rows", 1)
-    out = aggregated(begun(own, ready[0], ready[7]), pair, cross, *ready)
+    out = aggregated(begun(own, ready[0], ready[5], ready[7]), pair, cross, *ready)
     return out.reshape(C, D, RH, CW)
 
 

time: 29 us -> 28.5 us (0.983)
  Pallas kernels: 8.01 us -> 7.52 us
    pallas_call x1, Pallas kernels: 5.03 us -> 4.52 us  [aggregated(): pl.pallas_call(aggregate, out_shape=jax.ShapeDtypeStruct((C, D * RH, CW),...]
where the time goes in v5:
time: 28.5 us; the launch traced here: 28.2 us
  starting transfers between devices  17.3 us (61%)
  Pallas kernels  7.52 us (26%)
  other arithmetic  2.55 us (9%)
  between operations  0.72 us (3%)
    ppermute x5, starting transfers between devices, ring(): return lax.ppermute(x, axis, [(i, (i + by) % n) for i in range(n)])  14.2 us
    pallas_call x1, Pallas kernels, aggregated(): pl.pallas_call(aggregate, out_shape=jax.ShapeDtypeStruct((C, D * RH, CW),...  4.52 us
    ppermute x2, starting transfers between devices, swap(): return lax.ppermute(x, axis, pairs)  3.15 us
    pallas_call x1, Pallas kernels, begun(): pl.pallas_call(begin, out_shape=(jax.ShapeDtypeStruct((3, (D + 2) * OD, C...  1.86 us
    concatenate x1, other arithmetic, prepared(): jnp.concatenate([weight_one, weight_two], axis=0)  1.13 us
    concatenate x1, other arithmetic, body(): jnp.concatenate([left.reshape(C * RH, CW), right.reshape(C * RH, CW)], ax...  0.74 us
    another operation x1, other arithmetic, prepared(): jnp.stack([bias_one, bias_two])  0.68 us
    pallas_call x1, Pallas kernels, prepared(): pl.pallas_call(prepare, out_shape=(jax.ShapeDtypeStruct((256, KK), BF16),...  0.61 us
  transfers between devices with their start and end apart: 7, of which 1 were waited for; matrix products, arithmetic and copies ran while one was open for 6% of the time, Pallas kernels for 9%

profile of v5, /device:TPU:1, one launch (start us, length us, event | category | flops | bytes accessed | tf_op | source)
XLA Modules:
  0.0 28.2 jit_solution(8556522479432398388)
XLA Ops:
  0.7 0.7 %pad_maximum_fusion.1.lr_ref = bf16[128,128]{1,0:T(8,128)(2,1)S(1)} fusion(bf16[64,128]{1,0:T(8,128)(2,1)} %bitcast.5, bf16[64,128]{1,0:T(8,128)(2,1)} %bitcast.6), kind=kLoop, calls=%fused_computation.1 | loop fusion | flops 65536 | bytes 65536 | tf_op jit(solution)/shard_map/concatenate | solution.py:519
  1.4 0.1 pack.1.xo
  1.5 7.7 %collective-permute-start.4 = (bf16[80,128]{1,0:T(8,128)(2,1)S(1)}, bf16[80,128]{1,0:T(8,128)(2,1)S(1)}, u32[]{:S(2)}, u32[]{:S(2)}) collective-permute-start(bf16[80,128]{1,0:T(8,128)(2,1)S(1)} %pack.1.xo), channel_id=1, source_target_pairs={{0,4},{1,5},{2,6},{3,7},{4,8},{5,9},{6,10},{7,11},{8,12},{9,13},{1... | collective-permute-start | bytes 61448 | tf_op jit(solution)/shard_map/ppermute | solution.py:506
  9.3 1.6 %collective-permute-start.3 = (bf16[80,128]{1,0:T(8,128)(2,1)S(1)}, bf16[80,128]{1,0:T(8,128)(2,1)S(1)}, u32[]{:S(2)}, u32[]{:S(2)}) collective-permute-start(bf16[80,128]{1,0:T(8,128)(2,1)S(1)} %pack.1.xo), channel_id=1, source_target_pairs={{0,3},{1,4},{2,5},{3,6},{4,7},{5,8},{6,9},{7,10},{8,11},{9,12},{10... | collective-permute-start | bytes 61448 | tf_op jit(solution)/shard_map/ppermute | solution.py:506
  10.9 0.0 collective-permute-start.2
  10.9 1.1 %collective-permute-start.1 = (bf16[80,128]{1,0:T(8,128)(2,1)S(1)}, bf16[80,128]{1,0:T(8,128)(2,1)S(1)}, u32[]{:S(2)}, u32[]{:S(2)}) collective-permute-start(bf16[80,128]{1,0:T(8,128)(2,1)S(1)} %pack.1.xo), channel_id=1, source_target_pairs={{0,1},{1,2},{2,3},{3,4},{4,5},{5,6},{6,7},{7,8},{8,9},{9,10},{10,1... | collective-permute-start | bytes 61448 | tf_op jit(solution)/shard_map/ppermute | solution.py:506
  12.0 3.7 %collective-permute-start = (bf16[80,128]{1,0:T(8,128)(2,1)S(1)}, bf16[80,128]{1,0:T(8,128)(2,1)S(1)}, u32[]{:S(2)}, u32[]{:S(2)}) collective-permute-start(bf16[80,128]{1,0:T(8,128)(2,1)S(1)} %pack.1.xo), channel_id=1, source_target_pairs={{0,31},{1,0},{2,1},{3,2},{4,3},{5,4},{6,5},{7,6},{8,7},{9,8},{10,9... | collective-permute-start | bytes 61448 | tf_op jit(solution)/shard_map/ppermute | solution.py:506
  15.7 1.1 %pad_maximum_fusion.w_ref = bf16[54,32,32]{2,1,0:T(8,128)(2,1)S(1)} fusion(bf16[27,32,32]{2,1,0:T(8,128)(2,1)} %param.12, bf16[27,32,32]{2,1,0:T(8,128)(2,1)} %param.10), kind=kLoop, calls=%fused_computation | loop fusion | flops 55296 | bytes 221184 | tf_op jit(solution)/shard_map/concatenate | solution.py:143
  16.8 0.7 %pad_maximum_fusion.2.b_ref = f32[2,32]{1,0:T(2,128)S(1)} fusion(f32[1,32]{1,0:T(1,128)} %bitcast.7, f32[1,32]{1,0:T(1,128)} %bitcast.8), kind=kLoop, calls=%fused_computation.2 | loop fusion | flops 64 | bytes 512 | tf_op jit(solution)/shard_map/stack | solution.py:143
  17.5 0.6 %prepare.1 = (bf16[256,768]{1,0:T(8,128)(2,1)S(1)}, bf16[256,768]{1,0:T(8,128)(2,1)S(1)}, bf16[128,1792]{1,0:T(8,128)(2,1)S(1)}, bf16[256,768]{1,0:T(8,128)(2,1)...) custom-call(bf16[54,32,32]{2,1,0:T(8,128)(2,1)S(1)} %pad_maximum_fus, ...), custom_call_target="tpu_custom_call" | custom-call | flops 1000000 | bytes 4000000 | tf_op jit(solution)/shard_map/prepare/pallas_call | solution.py:126
  18.1 0.0 collective-permute-done.4.x4
  18.2 0.0 collective-permute-done.3.x3
  18.2 0.0 collective-permute-done.2.x2
  18.2 0.0 collective-permute-done.1.xl
  18.2 0.0 collective-permute-done.xr
  18.2 0.4 %windows.1.own = bf16[256,128]{1,0:T(8,128)(2,1)S(1)} custom-call(s32[1]{0:T(128)S(6)} %copy.8.off_ref, bf16[80,128]{1,0:T(8,128)(2,1)S(1)} %collective-permute-done.xr, bf16[80,128]{1,0:T(8,128)(2,1)S(1)} %collective-permute-done.1.xl, bf16[80,128]{1,0:T(8,128)(2,1)S(1)} %collective-permute-done.2.x2, bf16[80,128]{1,0:T(8,128)(2,1)S(1)} %collective-permute-done.3.x3, ...), custom_call_target="tpu_custom_call" | custom-call | tf_op jit(solution)/shard_map/windows/pallas_call | solution.py:236
  18.6 3.1 %collective-permute-start.6 = (bf16[256,128]{1,0:T(8,128)(2,1)S(1)}, bf16[256,128]{1,0:T(8,128)(2,1)S(1)}, u32[]{:S(2)}, u32[]{:S(2)}) collective-permute-start(bf16[256,128]{1,0:T(8,128)(2,1)S(1)} %windows.1.own), channel_id=1, source_target_pairs={{32,64},{64,32},{96,128},{128,96},{160,192},{192,160},{224,0},{0,2... | collective-permute-start | bytes 196616 | tf_op jit(solution)/shard_map/ppermute | solution.py:515
  21.8 0.0 collective-permute-start.5
  21.8 1.9 %begin.1 = (bf16[3,3200,128]{2,1,0:T(8,128)(2,1)S(1)}, bf16[3,64,128]{2,1,0:T(8,128)(2,1)S(1)}, f32[12,256,256]{2,1,0:T(8,128)S(1)}) custom-call(bf16[256,128]{1,0:T(8,128)(2,1)S(1)} %windows.1.own, bf16[256,768]{1,0:T(8,128)(2,1)S(1)} %get-tuple-element.17.t_own, f32[256,128]{1,0:T(8,128)S(1)} %get-tuple-element.16.after_ref.c1, ...), custom_call_target="tpu_custom_call" | custom-call | flops 1207959552 | bytes 6000000 | tf_op jit(solution)/shard_map/begin/pallas_call | solution.py:327
  23.6 0.1 collective-permute-done.6.cross
  23.7 0.0 collective-permute-done.5.pair
  23.7 4.5 %aggregate.1 = bf16[32,96,128]{2,1,0:T(8,128)(2,1)} custom-call(bf16[3,3200,128]{2,1,0:T(8,128)(2,1)S(1)} %get-tuple-element.19.own_vol, bf16[3,64,128]{2,1,0:T(8,128)(2,1)S(1)} %get-tuple-element.20.own_cells, f32[12,256,256]{2,1,0:T(8,128)S(1)} %get-tuple-element.21.acc, bf16[256,128]{1,0:T(8,128)(2,1)S(1)} %collective-permute-done.5.pair, ...), custom_call_target="tpu_custom_call" | custom-call | tf_op jit(solution)/shard_map/aggregate/pallas_call | solution.py:488
Async XLA Ops:
  1.5 16.6 %collective-permute-start.4 = (bf16[80,128]{1,0:T(8,128)(2,1)S(1)}, bf16[80,128]{1,0:T(8,128)(2,1)S(1)}, u32[]{:S(2)}, u32[]{:S(2)}) collective-permute-start(bf16[80,128]{1,0:T(8,128)(2,1)S(1)} %pack.1.xo), channel_id=1, source_target_pairs={{0,4},{1,5},{2,6},{3,7},{4,8},{5,9},{6,10},{7,11},{8,12},{9,13},{1... | collective-permute-start | bytes 61448 | tf_op jit(solution)/shard_map/ppermute | solution.py:506
  9.3 8.9 %collective-permute-start.3 = (bf16[80,128]{1,0:T(8,128)(2,1)S(1)}, bf16[80,128]{1,0:T(8,128)(2,1)S(1)}, u32[]{:S(2)}, u32[]{:S(2)}) collective-permute-start(bf16[80,128]{1,0:T(8,128)(2,1)S(1)} %pack.1.xo), channel_id=1, source_target_pairs={{0,3},{1,4},{2,5},{3,6},{4,7},{5,8},{6,9},{7,10},{8,11},{9,12},{10... | collective-permute-start | bytes 61448 | tf_op jit(solution)/shard_map/ppermute | solution.py:506
  10.9 7.2 %collective-permute-start.2 = (bf16[80,128]{1,0:T(8,128)(2,1)S(1)}, bf16[80,128]{1,0:T(8,128)(2,1)S(1)}, u32[]{:S(2)}, u32[]{:S(2)}) collective-permute-start(bf16[80,128]{1,0:T(8,128)(2,1)S(1)} %pack.1.xo), channel_id=1, source_target_pairs={{0,2},{1,3},{2,4},{3,5},{4,6},{5,7},{6,8},{7,9},{8,10},{9,11},{10,... | collective-permute-start | bytes 61448 | tf_op jit(solution)/shard_map/ppermute | solution.py:506
  10.9 7.3 %collective-permute-start.1 = (bf16[80,128]{1,0:T(8,128)(2,1)S(1)}, bf16[80,128]{1,0:T(8,128)(2,1)S(1)}, u32[]{:S(2)}, u32[]{:S(2)}) collective-permute-start(bf16[80,128]{1,0:T(8,128)(2,1)S(1)} %pack.1.xo), channel_id=1, source_target_pairs={{0,1},{1,2},{2,3},{3,4},{4,5},{5,6},{6,7},{7,8},{8,9},{9,10},{10,1... | collective-permute-start | bytes 61448 | tf_op jit(solution)/shard_map/ppermute | solution.py:506
  12.0 6.2 %collective-permute-start = (bf16[80,128]{1,0:T(8,128)(2,1)S(1)}, bf16[80,128]{1,0:T(8,128)(2,1)S(1)}, u32[]{:S(2)}, u32[]{:S(2)}) collective-permute-start(bf16[80,128]{1,0:T(8,128)(2,1)S(1)} %pack.1.xo), channel_id=1, source_target_pairs={{0,31},{1,0},{2,1},{3,2},{4,3},{5,4},{6,5},{7,6},{8,7},{9,8},{10,9... | collective-permute-start | bytes 61448 | tf_op jit(solution)/shard_map/ppermute | solution.py:506
  18.6 5.1 %collective-permute-start.6 = (bf16[256,128]{1,0:T(8,128)(2,1)S(1)}, bf16[256,128]{1,0:T(8,128)(2,1)S(1)}, u32[]{:S(2)}, u32[]{:S(2)}) collective-permute-start(bf16[256,128]{1,0:T(8,128)(2,1)S(1)} %windows.1.own), channel_id=1, source_target_pairs={{32,64},{64,32},{96,128},{128,96},{160,192},{192,160},{224,0},{0,2... | collective-permute-start | bytes 196616 | tf_op jit(solution)/shard_map/ppermute | solution.py:515
  21.8 2.0 %collective-permute-start.5 = (bf16[256,128]{1,0:T(8,128)(2,1)S(1)}, bf16[256,128]{1,0:T(8,128)(2,1)S(1)}, u32[]{:S(2)}, u32[]{:S(2)}) collective-permute-start(bf16[256,128]{1,0:T(8,128)(2,1)S(1)} %windows.1.own), channel_id=1, source_target_pairs={{0,32},{32,0},{64,96},{96,64},{128,160},{160,128},{192,224},{224,1... | collective-permute-start | bytes 196616 | tf_op jit(solution)/shard_map/ppermute | solution.py:515

commit v6 on v5

--- a/solution.py
+++ b/solution.py
@@ -176,13 +176,17 @@
     )(offsets, lr)
 
 
-def cut(off_ref, xr, xl, x2, x3, x4, xo, lr_ref, after_ref, out_ref, tiles):
+def cut(off_ref, even_ref, odd_ref, x2, x3, x4, xo, lr_ref, after_ref, out_ref, tiles):
     col = lax.axis_index("cols")
     final = lax.axis_size("cols") - 1
     o = off_ref[0]
+    even, odd = even_ref[...], odd_ref[...]
+    second = col % 2 == 1
+    xl = jnp.where(second, even, odd)
+    xr = jnp.where(second, odd, even)
 
     def scalar_of(ref):
-        v = ref[64:80, :].astype(F32)
+        v = ref[64:80].astype(F32)
         return jnp.max(v[6:7, 64:128] * 8.0 + v[7:8, 64:128]).astype(jnp.int32)
 
     o_l = scalar_of(xl)
@@ -232,7 +236,7 @@
     out_ref[192:256, :] = border.astype(BF16)
 
 
-def windows(offsets, xr, xl, x2, x3, x4, xo, lr, after):
+def windows(offsets, even, odd, x2, x3, x4, xo, lr, after):
     return pl.pallas_call(
         cut,
         out_shape=jax.ShapeDtypeStruct((256, CW), BF16),
@@ -241,7 +245,7 @@
         scratch_shapes=[pltpu.VMEM((6, 64, CW), F32)],
         compiler_params=pltpu.CompilerParams(vmem_limit_bytes=4 * MIB),
         name="windows",
-    )(offsets, xr, xl, x2, x3, x4, xo, lr, after)
+    )(offsets, even, odd, x2, x3, x4, xo, lr, after)
 
 
 def border_cells(tiles, sel):
@@ -367,6 +371,8 @@
     odd = row % 2 == 1
     no_up = row == 0
     no_down = row == rows_last
+    keep_up = 1.0 - no_up.astype(F32)
+    keep_down = 1.0 - no_down.astype(F32)
 
     def tile(t):
         part = slice(t * 64, t * 64 + 64)
@@ -425,9 +431,9 @@
                     h = acc[j, at : at + C, cut] + halo[ha : ha + C, cut]
                     h = jnp.maximum(h, 0.0)
                     if r == 0:
-                        h = jnp.where(no_up, 0.0, h)
+                        h = h * keep_up
                     if r == HR - 1:
-                        h = jnp.where(no_down, 0.0, h)
+                        h = h * keep_down
                     h = h.astype(BF16)
                     b = border[r * C : (r + 1) * C]
                     base = (d + 1) * HD + r * C
@@ -501,9 +507,9 @@
     )(*first, pair, cross, *ready)
 
 
-def ring(x, axis, by):
-    n = lax.axis_size(axis)
-    return lax.ppermute(x, axis, [(i, (i + by) % n) for i in range(n)])
+def ahead(x, by):
+    n = lax.axis_size("cols")
+    return lax.ppermute(x, "cols", [(i, i + by if i + by < n else n - 1 - i) for i in range(n)])
 
 
 def swap(x, axis, first):
@@ -515,16 +521,30 @@
     return lax.ppermute(x, axis, pairs)
 
 
+def swap_inner(x):
+    rows, cols = lax.axis_size("rows"), lax.axis_size("cols")
+    pairs = []
+    for r in range(rows):
+        near = r ^ 1 if (r ^ 1) < rows else r
+        for c in range(cols):
+            if c in (0, cols - 1):
+                to = near * cols + c
+            else:
+                to = r * cols + (c + 1 if c % 2 else c - 1)
+            pairs.append((r * cols + c, to))
+    return lax.ppermute(x, ("rows", "cols"), pairs)
+
+
 def body(left, right, offsets, weight_one, bias_one, weight_two, bias_two):
     lr = jnp.concatenate([left.reshape(C * RH, CW), right.reshape(C * RH, CW)], axis=0)
     x = packed(offsets, lr)
-    xr = ring(x, "cols", -1)
-    xl = ring(x, "cols", 1)
-    x2 = ring(x, "cols", 2)
-    x3 = ring(x, "cols", 3)
-    x4 = ring(x, "cols", 4)
+    even = swap(x, "cols", 0)
+    odd = swap_inner(x)
+    x2 = ahead(x, 2)
+    x3 = ahead(x, 3)
+    x4 = ahead(x, 4)
     ready = prepared(weight_one, weight_two, bias_one, bias_two)
-    own = windows(offsets, xr, xl, x2, x3, x4, x, lr, ready[5])
+    own = windows(offsets, even, odd, x2, x3, x4, x, lr, ready[5])
     pair = swap(own, "rows", 0)
     cross = swap(own, "rows", 1)
     out = aggregated(begun(own, ready[0], ready[5], ready[7]), pair, cross, *ready)

time: 28.5 us -> 27.7 us (0.972)
  starting transfers between devices: 17.3 us -> 15.1 us
  waiting for transfers between devices: 0.1 us -> 1.46 us
    ppermute x5 -> x4, starting transfers between devices: 14.2 us -> 10.6 us  [the longest x3 9.4 us: ahead(): lax.ppermute(x, 'cols', [(i, i + by if i + by < n else n - 1 - i) for i i...]
    ppermute x5 -> x4, waiting for transfers between devices: 0.01 us -> 1.4 us  [the longest x3 1.4 us: ahead(): lax.ppermute(x, 'cols', [(i, i + by if i + by < n else n - 1 - i) for i i...]
    ppermute x2 -> x3, starting transfers between devices: 3.15 us -> 4.46 us  [swap(): return lax.ppermute(x, axis, pairs)]
  transfers between devices with their start and end apart: 7 -> 7, of which waited for: 1 -> 2; matrix products, arithmetic and copies ran while one was open for 6% -> 7% of each run, Pallas kernels for 9% -> 9%
where the time goes in v6:
time: 27.7 us; the launch traced here: 27.3 us
  starting transfers between devices  15.1 us (55%)
  Pallas kernels  7.51 us (27%)
  other arithmetic  2.55 us (9%)
  waiting for transfers between devices  1.46 us (5%)
  between operations  0.7 us (3%)
    ppermute x3, starting transfers between devices, ahead(): lax.ppermute(x, 'cols', [(i, i + by if i + by < n else n - 1 - i) for i i...  9.4 us
    pallas_call x1, Pallas kernels, aggregated(): pl.pallas_call(aggregate, out_shape=jax.ShapeDtypeStruct((C, D * RH, CW),...  4.5 us
    ppermute x3, starting transfers between devices, swap(): return lax.ppermute(x, axis, pairs)  4.46 us
    pallas_call x1, Pallas kernels, begun(): pl.pallas_call(begin, out_shape=(jax.ShapeDtypeStruct((3, (D + 2) * OD, C...  1.86 us
    ppermute x3, waiting for transfers between devices, ahead(): lax.ppermute(x, 'cols', [(i, i + by if i + by < n else n - 1 - i) for i i...  1.4 us
    ppermute x1, starting transfers between devices, swap_inner(): return lax.ppermute(x, ('rows', 'cols'), pairs)  1.24 us
    concatenate x1, other arithmetic, prepared(): jnp.concatenate([weight_one, weight_two], axis=0)  1.13 us
    concatenate x1, other arithmetic, body(): jnp.concatenate([left.reshape(C * RH, CW), right.reshape(C * RH, CW)], ax...  0.74 us
  transfers between devices with their start and end apart: 7, of which 2 were waited for; matrix products, arithmetic and copies ran while one was open for 7% of the time, Pallas kernels for 9%

profile of v6, /device:TPU:1, one launch (start us, length us, event | category | flops | bytes accessed | tf_op | source)
XLA Modules:
  0.0 27.3 jit_solution(13049944836338043678)
XLA Ops:
  0.7 0.7 %pad_maximum_fusion.1.lr_ref = bf16[128,128]{1,0:T(8,128)(2,1)S(1)} fusion(bf16[64,128]{1,0:T(8,128)(2,1)} %bitcast.5, bf16[64,128]{1,0:T(8,128)(2,1)} %bitcast.6), kind=kLoop, calls=%fused_computation.1 | loop fusion | flops 65536 | bytes 65536 | tf_op jit(solution)/shard_map/concatenate | solution.py:539
  1.4 0.1 pack.1.xo
  1.5 7.7 %collective-permute-start.4 = (bf16[80,128]{1,0:T(8,128)(2,1)S(1)}, bf16[80,128]{1,0:T(8,128)(2,1)S(1)}, u32[]{:S(2)}, u32[]{:S(2)}) collective-permute-start(bf16[80,128]{1,0:T(8,128)(2,1)S(1)} %pack.1.xo), channel_id=1, source_target_pairs={{0,4},{1,5},{2,6},{3,7},{4,8},{5,9},{6,10},{7,11},{8,12},{9,13},{1... | collective-permute-start | bytes 61448 | tf_op jit(solution)/shard_map/ppermute | solution.py:512
  9.3 1.6 %collective-permute-start.3 = (bf16[80,128]{1,0:T(8,128)(2,1)S(1)}, bf16[80,128]{1,0:T(8,128)(2,1)S(1)}, u32[]{:S(2)}, u32[]{:S(2)}) collective-permute-start(bf16[80,128]{1,0:T(8,128)(2,1)S(1)} %pack.1.xo), channel_id=1, source_target_pairs={{0,3},{1,4},{2,5},{3,6},{4,7},{5,8},{6,9},{7,10},{8,11},{9,12},{10... | collective-permute-start | bytes 61448 | tf_op jit(solution)/shard_map/ppermute | solution.py:512
  10.9 0.0 collective-permute-start.2
  10.9 1.2 %collective-permute-start.1 = (bf16[80,128]{1,0:T(8,128)(2,1)S(1)}, bf16[80,128]{1,0:T(8,128)(2,1)S(1)}, u32[]{:S(2)}, u32[]{:S(2)}) collective-permute-start(bf16[80,128]{1,0:T(8,128)(2,1)S(1)} %pack.1.xo), channel_id=1, source_target_pairs={{0,32},{1,2},{2,1},{3,4},{4,3},{5,6},{6,5},{7,8},{8,7},{9,10},{10,... | collective-permute-start | bytes 61448 | tf_op jit(solution)/shard_map/ppermute | solution.py:535
  12.2 1.5 %collective-permute-start = (bf16[80,128]{1,0:T(8,128)(2,1)S(1)}, bf16[80,128]{1,0:T(8,128)(2,1)S(1)}, u32[]{:S(2)}, u32[]{:S(2)}) collective-permute-start(bf16[80,128]{1,0:T(8,128)(2,1)S(1)} %pack.1.xo), channel_id=1, source_target_pairs={{0,1},{1,0},{2,3},{3,2},{4,5},{5,4},{6,7},{7,6},{8,9},{9,8},{10,11... | collective-permute-start | bytes 61448 | tf_op jit(solution)/shard_map/ppermute | solution.py:521
  13.7 1.1 %pad_maximum_fusion.w_ref = bf16[54,32,32]{2,1,0:T(8,128)(2,1)S(1)} fusion(bf16[27,32,32]{2,1,0:T(8,128)(2,1)} %param.12, bf16[27,32,32]{2,1,0:T(8,128)(2,1)} %param.10), kind=kLoop, calls=%fused_computation | loop fusion | flops 55296 | bytes 221184 | tf_op jit(solution)/shard_map/concatenate | solution.py:143
  14.8 0.7 %pad_maximum_fusion.2.b_ref = f32[2,32]{1,0:T(2,128)S(1)} fusion(f32[1,32]{1,0:T(1,128)} %bitcast.7, f32[1,32]{1,0:T(1,128)} %bitcast.8), kind=kLoop, calls=%fused_computation.2 | loop fusion | flops 64 | bytes 512 | tf_op jit(solution)/shard_map/stack | solution.py:143
  15.5 0.6 %prepare.1 = (bf16[256,768]{1,0:T(8,128)(2,1)S(1)}, bf16[256,768]{1,0:T(8,128)(2,1)S(1)}, bf16[128,1792]{1,0:T(8,128)(2,1)S(1)}, bf16[256,768]{1,0:T(8,128)(2,1)...) custom-call(bf16[54,32,32]{2,1,0:T(8,128)(2,1)S(1)} %pad_maximum_fus, ...), custom_call_target="tpu_custom_call" | custom-call | flops 1000000 | bytes 4000000 | tf_op jit(solution)/shard_map/prepare/pallas_call | solution.py:126
  16.1 0.0 collective-permute-done.4.x4
  16.1 0.0 collective-permute-done.3.x3
  16.1 1.4 %collective-permute-done.2.x2 = bf16[80,128]{1,0:T(8,128)(2,1)S(1)} collective-permute-done((bf16[80,128]{1,0:T(8,128)(2,1)S(1)}, bf16[80,128]{1,0:T(8,128)(2,1)S(1)}, u32[]{:S(2)}, u32[]{:S(2)}) %collective-permute-start.2) | collective-permute-done | bytes 20512 | tf_op jit(solution)/shard_map/ppermute | solution.py:512
  17.5 0.0 collective-permute-done.1.odd_ref
  17.5 0.0 collective-permute-done.even_ref
  17.5 0.4 %windows.1.own = bf16[256,128]{1,0:T(8,128)(2,1)S(1)} custom-call(s32[1]{0:T(128)S(6)} %copy.8.off_ref, bf16[80,128]{1,0:T(8,128)(2,1)S(1)} %collective-permute-done.even_ref, bf16[80,128]{1,0:T(8,128)(2,1)S(1)} %collective-permute-done.1.odd_ref, bf16[80,128]{1,0:T(8,128)(2,1)S(1)} %collective-permute-done.2.x2, ...), custom_call_target="tpu_custom_call" | custom-call | tf_op jit(solution)/shard_map/windows/pallas_call | solution.py:240
  17.9 2.9 %collective-permute-start.6 = (bf16[256,128]{1,0:T(8,128)(2,1)S(1)}, bf16[256,128]{1,0:T(8,128)(2,1)S(1)}, u32[]{:S(2)}, u32[]{:S(2)}) collective-permute-start(bf16[256,128]{1,0:T(8,128)(2,1)S(1)} %windows.1.own), channel_id=1, source_target_pairs={{32,64},{64,32},{96,128},{128,96},{160,192},{192,160},{224,0},{0,2... | collective-permute-start | bytes 196616 | tf_op jit(solution)/shard_map/ppermute | solution.py:521
  20.9 0.0 collective-permute-start.5
  20.9 1.9 %begin.1 = (bf16[3,3200,128]{2,1,0:T(8,128)(2,1)S(1)}, bf16[3,64,128]{2,1,0:T(8,128)(2,1)S(1)}, f32[12,256,256]{2,1,0:T(8,128)S(1)}) custom-call(bf16[256,128]{1,0:T(8,128)(2,1)S(1)} %windows.1.own, bf16[256,768]{1,0:T(8,128)(2,1)S(1)} %get-tuple-element.17.t_own, f32[256,128]{1,0:T(8,128)S(1)} %get-tuple-element.16.after_ref.c1, ...), custom_call_target="tpu_custom_call" | custom-call | flops 1207959552 | bytes 6000000 | tf_op jit(solution)/shard_map/begin/pallas_call | solution.py:331
  22.8 0.1 collective-permute-done.6.cross
  22.8 0.0 collective-permute-done.5.pair
  22.8 4.5 %aggregate.1 = bf16[32,96,128]{2,1,0:T(8,128)(2,1)} custom-call(bf16[3,3200,128]{2,1,0:T(8,128)(2,1)S(1)} %get-tuple-element.19.own_vol, bf16[3,64,128]{2,1,0:T(8,128)(2,1)S(1)} %get-tuple-element.20.own_cells, f32[12,256,256]{2,1,0:T(8,128)S(1)} %get-tuple-element.21.acc, bf16[256,128]{1,0:T(8,128)(2,1)S(1)} %collective-permute-done.5.pair, ...), custom_call_target="tpu_custom_call" | custom-call | tf_op jit(solution)/shard_map/aggregate/pallas_call | solution.py:494
Async XLA Ops:
  1.5 14.6 %collective-permute-start.4 = (bf16[80,128]{1,0:T(8,128)(2,1)S(1)}, bf16[80,128]{1,0:T(8,128)(2,1)S(1)}, u32[]{:S(2)}, u32[]{:S(2)}) collective-permute-start(bf16[80,128]{1,0:T(8,128)(2,1)S(1)} %pack.1.xo), channel_id=1, source_target_pairs={{0,4},{1,5},{2,6},{3,7},{4,8},{5,9},{6,10},{7,11},{8,12},{9,13},{1... | collective-permute-start | bytes 61448 | tf_op jit(solution)/shard_map/ppermute | solution.py:512
  9.3 6.8 %collective-permute-start.3 = (bf16[80,128]{1,0:T(8,128)(2,1)S(1)}, bf16[80,128]{1,0:T(8,128)(2,1)S(1)}, u32[]{:S(2)}, u32[]{:S(2)}) collective-permute-start(bf16[80,128]{1,0:T(8,128)(2,1)S(1)} %pack.1.xo), channel_id=1, source_target_pairs={{0,3},{1,4},{2,5},{3,6},{4,7},{5,8},{6,9},{7,10},{8,11},{9,12},{10... | collective-permute-start | bytes 61448 | tf_op jit(solution)/shard_map/ppermute | solution.py:512
  10.9 6.6 %collective-permute-start.2 = (bf16[80,128]{1,0:T(8,128)(2,1)S(1)}, bf16[80,128]{1,0:T(8,128)(2,1)S(1)}, u32[]{:S(2)}, u32[]{:S(2)}) collective-permute-start(bf16[80,128]{1,0:T(8,128)(2,1)S(1)} %pack.1.xo), channel_id=1, source_target_pairs={{0,2},{1,3},{2,4},{3,5},{4,6},{5,7},{6,8},{7,9},{8,10},{9,11},{10,... | collective-permute-start | bytes 61448 | tf_op jit(solution)/shard_map/ppermute | solution.py:512
  10.9 6.6 %collective-permute-start.1 = (bf16[80,128]{1,0:T(8,128)(2,1)S(1)}, bf16[80,128]{1,0:T(8,128)(2,1)S(1)}, u32[]{:S(2)}, u32[]{:S(2)}) collective-permute-start(bf16[80,128]{1,0:T(8,128)(2,1)S(1)} %pack.1.xo), channel_id=1, source_target_pairs={{0,32},{1,2},{2,1},{3,4},{4,3},{5,6},{6,5},{7,8},{8,7},{9,10},{10,... | collective-permute-start | bytes 61448 | tf_op jit(solution)/shard_map/ppermute | solution.py:535
  12.2 5.4 %collective-permute-start = (bf16[80,128]{1,0:T(8,128)(2,1)S(1)}, bf16[80,128]{1,0:T(8,128)(2,1)S(1)}, u32[]{:S(2)}, u32[]{:S(2)}) collective-permute-start(bf16[80,128]{1,0:T(8,128)(2,1)S(1)} %pack.1.xo), channel_id=1, source_target_pairs={{0,1},{1,0},{2,3},{3,2},{4,5},{5,4},{6,7},{7,6},{8,9},{9,8},{10,11... | collective-permute-start | bytes 61448 | tf_op jit(solution)/shard_map/ppermute | solution.py:521
  17.9 4.9 %collective-permute-start.6 = (bf16[256,128]{1,0:T(8,128)(2,1)S(1)}, bf16[256,128]{1,0:T(8,128)(2,1)S(1)}, u32[]{:S(2)}, u32[]{:S(2)}) collective-permute-start(bf16[256,128]{1,0:T(8,128)(2,1)S(1)} %windows.1.own), channel_id=1, source_target_pairs={{32,64},{64,32},{96,128},{128,96},{160,192},{192,160},{224,0},{0,2... | collective-permute-start | bytes 196616 | tf_op jit(solution)/shard_map/ppermute | solution.py:521
  20.9 2.0 %collective-permute-start.5 = (bf16[256,128]{1,0:T(8,128)(2,1)S(1)}, bf16[256,128]{1,0:T(8,128)(2,1)S(1)}, u32[]{:S(2)}, u32[]{:S(2)}) collective-permute-start(bf16[256,128]{1,0:T(8,128)(2,1)S(1)} %windows.1.own), channel_id=1, source_target_pairs={{0,32},{32,0},{64,96},{96,64},{128,160},{160,128},{192,224},{224,1... | collective-permute-start | bytes 196616 | tf_op jit(solution)/shard_map/ppermute | solution.py:521

commit v7 on v6

--- a/solution.py
+++ b/solution.py
@@ -137,7 +137,7 @@
         ),
         in_specs=[VMEM] * 2,
         out_specs=[VMEM] * 8,
-        cost_estimate=pl.CostEstimate(flops=1000000, bytes_accessed=4000000, transcendentals=0),
+        cost_estimate=pl.CostEstimate(flops=0, bytes_accessed=0, transcendentals=0),
         compiler_params=pltpu.CompilerParams(vmem_limit_bytes=12 * MIB),
         name="prepare",
     )(jnp.concatenate([weight_one, weight_two], axis=0), jnp.stack([bias_one, bias_two]))
@@ -536,13 +536,14 @@
 
 
 def body(left, right, offsets, weight_one, bias_one, weight_two, bias_two):
-    lr = jnp.concatenate([left.reshape(C * RH, CW), right.reshape(C * RH, CW)], axis=0)
+    r = right.reshape(C * RH, CW)
+    lr = jnp.concatenate([left.reshape(C * RH, CW), r], axis=0)
     x = packed(offsets, lr)
     even = swap(x, "cols", 0)
     odd = swap_inner(x)
-    x2 = ahead(x, 2)
-    x3 = ahead(x, 3)
-    x4 = ahead(x, 4)
+    x2 = ahead(r, 2)
+    x3 = ahead(r, 3)
+    x4 = ahead(r, 4)
     ready = prepared(weight_one, weight_two, bias_one, bias_two)
     own = windows(offsets, even, odd, x2, x3, x4, x, lr, ready[5])
     pair = swap(own, "rows", 0)

time: 27.7 us -> 27.7 us (level)
  the two profiles are of different devices: /device:TPU:1 before, /device:TPU:8 now
where the time goes in v7:
time: 27.7 us; the launch traced here: 27.5 us
  starting transfers between devices  14.4 us (52%)
  Pallas kernels  7.52 us (27%)
  other arithmetic  2.55 us (9%)
  waiting for transfers between devices  2.28 us (8%)
  between operations  0.72 us (3%)
    ppermute x3, starting transfers between devices, ahead(): lax.ppermute(x, 'cols', [(i, i + by if i + by < n else n - 1 - i) for i i...  9.12 us
    pallas_call x1, Pallas kernels, aggregated(): pl.pallas_call(aggregate, out_shape=jax.ShapeDtypeStruct((C, D * RH, CW),...  4.51 us
    ppermute x1, starting transfers between devices, swap_inner(): return lax.ppermute(x, ('rows', 'cols'), pairs)  3.12 us
    ppermute x3, waiting for transfers between devices, swap(): return lax.ppermute(x, axis, pairs)  2.27 us
    ppermute x3, starting transfers between devices, swap(): return lax.ppermute(x, axis, pairs)  2.15 us
    pallas_call x1, Pallas kernels, begun(): pl.pallas_call(begin, out_shape=(jax.ShapeDtypeStruct((3, (D + 2) * OD, C...  1.86 us
    concatenate x1, other arithmetic, prepared(): jnp.concatenate([weight_one, weight_two], axis=0)  1.13 us
    concatenate x1, other arithmetic, body(): lr = jnp.concatenate([left.reshape(C * RH, CW), r], axis=0)  0.74 us
  transfers between devices with their start and end apart: 7, of which 2 were waited for; matrix products, arithmetic and copies ran while one was open for 9% of the time, Pallas kernels for 9%

profile of v7, /device:TPU:8, one launch (start us, length us, event | category | flops | bytes accessed | tf_op | source)
XLA Modules:
  0.0 27.5 jit_solution(10407054614136197122)
XLA Ops:
  0.0 7.2 %collective-permute-start.4 = (bf16[64,128]{1,0:T(8,128)(2,1)}, bf16[64,128]{1,0:T(8,128)(2,1)S(1)}, u32[]{:S(2)}, u32[]{:S(2)}) collective-permute-start(bf16[64,128]{1,0:T(8,128)(2,1)} %bitcast.6), channel_id=1, source_target_pairs={{0,4},{1,5},{2,6},{3,7},{4,8},{5,9},{6,10},{7,11},{8,12},{9,13},{1... | collective-permute-start | bytes 49160 | tf_op jit(solution)/shard_map/ppermute | solution.py:512
  7.2 1.9 %collective-permute-start.3 = (bf16[64,128]{1,0:T(8,128)(2,1)}, bf16[64,128]{1,0:T(8,128)(2,1)S(1)}, u32[]{:S(2)}, u32[]{:S(2)}) collective-permute-start(bf16[64,128]{1,0:T(8,128)(2,1)} %bitcast.7), channel_id=1, source_target_pairs={{0,3},{1,4},{2,5},{3,6},{4,7},{5,8},{6,9},{7,10},{8,11},{9,12},{10... | collective-permute-start | bytes 49160 | tf_op jit(solution)/shard_map/ppermute | solution.py:512
  9.1 0.0 collective-permute-start.2
  9.8 0.7 %pad_maximum_fusion.1.lr_ref = bf16[128,128]{1,0:T(8,128)(2,1)S(1)} fusion(bf16[64,128]{1,0:T(8,128)(2,1)} %bitcast.9, bf16[64,128]{1,0:T(8,128)(2,1)} %bitcast.5), kind=kLoop, calls=%fused_computation.1 | loop fusion | flops 65536 | bytes 65536 | tf_op jit(solution)/shard_map/concatenate | solution.py:540
  10.5 0.1 pack.1.xo
  10.6 3.1 %collective-permute-start.1 = (bf16[80,128]{1,0:T(8,128)(2,1)S(1)}, bf16[80,128]{1,0:T(8,128)(2,1)S(1)}, u32[]{:S(2)}, u32[]{:S(2)}) collective-permute-start(bf16[80,128]{1,0:T(8,128)(2,1)S(1)} %pack.1.xo), channel_id=1, source_target_pairs={{0,32},{1,2},{2,1},{3,4},{4,3},{5,6},{6,5},{7,8},{8,7},{9,10},{10,... | collective-permute-start | bytes 61448 | tf_op jit(solution)/shard_map/ppermute | solution.py:535
  13.8 0.5 %collective-permute-start = (bf16[80,128]{1,0:T(8,128)(2,1)S(1)}, bf16[80,128]{1,0:T(8,128)(2,1)S(1)}, u32[]{:S(2)}, u32[]{:S(2)}) collective-permute-start(bf16[80,128]{1,0:T(8,128)(2,1)S(1)} %pack.1.xo), channel_id=1, source_target_pairs={{0,1},{1,0},{2,3},{3,2},{4,5},{5,4},{6,7},{7,6},{8,9},{9,8},{10,11... | collective-permute-start | bytes 61448 | tf_op jit(solution)/shard_map/ppermute | solution.py:521
  14.2 1.1 %pad_maximum_fusion.w_ref = bf16[54,32,32]{2,1,0:T(8,128)(2,1)S(1)} fusion(bf16[27,32,32]{2,1,0:T(8,128)(2,1)} %param.12, bf16[27,32,32]{2,1,0:T(8,128)(2,1)} %param.10), kind=kLoop, calls=%fused_computation | loop fusion | flops 55296 | bytes 221184 | tf_op jit(solution)/shard_map/concatenate | solution.py:143
  15.4 0.7 %pad_maximum_fusion.2.b_ref = f32[2,32]{1,0:T(2,128)S(1)} fusion(f32[1,32]{1,0:T(1,128)} %bitcast.10, f32[1,32]{1,0:T(1,128)} %bitcast.11), kind=kLoop, calls=%fused_computation.2 | loop fusion | flops 64 | bytes 512 | tf_op jit(solution)/shard_map/stack | solution.py:143
  16.0 0.6 %prepare.1 = (bf16[256,768]{1,0:T(8,128)(2,1)S(1)}, bf16[256,768]{1,0:T(8,128)(2,1)S(1)}, bf16[128,1792]{1,0:T(8,128)(2,1)S(1)}, bf16[256,768]{1,0:T(8,128)(2,1)...) custom-call(bf16[54,32,32]{2,1,0:T(8,128)(2,1)S(1)} %pad_maximum_fus, ...), custom_call_target="tpu_custom_call" | custom-call | tf_op jit(solution)/shard_map/prepare/pallas_call | solution.py:126
  16.7 0.0 collective-permute-done.4.x4
  16.7 0.0 collective-permute-done.3.x3
  16.7 0.0 collective-permute-done.2.x2
  16.7 0.0 collective-permute-done.1.odd_ref
  16.7 0.8 %collective-permute-done.even_ref = bf16[80,128]{1,0:T(8,128)(2,1)S(1)} collective-permute-done((bf16[80,128]{1,0:T(8,128)(2,1)S(1)}, bf16[80,128]{1,0:T(8,128)(2,1)S(1)}, u32[]{:S(2)}, u32[]{:S(2)}) %collective-permute-start) | collective-permute-done | bytes 20512 | tf_op jit(solution)/shard_map/ppermute | solution.py:521
  17.6 0.4 %windows.1.own = bf16[256,128]{1,0:T(8,128)(2,1)S(1)} custom-call(s32[1]{0:T(128)S(6)} %copy.8.off_ref, bf16[80,128]{1,0:T(8,128)(2,1)S(1)} %collective-permute-done.even_ref, bf16[80,128]{1,0:T(8,128)(2,1)S(1)} %collective-permute-done.1.odd_ref, bf16[64,128]{1,0:T(8,128)(2,1)S(1)} %collective-permute-done.2.x2, ...), custom_call_target="tpu_custom_call" | custom-call | tf_op jit(solution)/shard_map/windows/pallas_call | solution.py:240
  18.0 0.6 %collective-permute-start.6 = (bf16[256,128]{1,0:T(8,128)(2,1)S(1)}, bf16[256,128]{1,0:T(8,128)(2,1)S(1)}, u32[]{:S(2)}, u32[]{:S(2)}) collective-permute-start(bf16[256,128]{1,0:T(8,128)(2,1)S(1)} %windows.1.own), channel_id=1, source_target_pairs={{32,64},{64,32},{96,128},{128,96},{160,192},{192,160},{224,0},{0,2... | collective-permute-start | bytes 196616 | tf_op jit(solution)/shard_map/ppermute | solution.py:521
  18.6 1.1 %collective-permute-start.5 = (bf16[256,128]{1,0:T(8,128)(2,1)S(1)}, bf16[256,128]{1,0:T(8,128)(2,1)S(1)}, u32[]{:S(2)}, u32[]{:S(2)}) collective-permute-start(bf16[256,128]{1,0:T(8,128)(2,1)S(1)} %windows.1.own), channel_id=1, source_target_pairs={{0,32},{32,0},{64,96},{96,64},{128,160},{160,128},{192,224},{224,1... | collective-permute-start | bytes 196616 | tf_op jit(solution)/shard_map/ppermute | solution.py:521
  19.7 1.9 %begin.1 = (bf16[3,3200,128]{2,1,0:T(8,128)(2,1)S(1)}, bf16[3,64,128]{2,1,0:T(8,128)(2,1)S(1)}, f32[12,256,256]{2,1,0:T(8,128)S(1)}) custom-call(bf16[256,128]{1,0:T(8,128)(2,1)S(1)} %windows.1.own, bf16[256,768]{1,0:T(8,128)(2,1)S(1)} %get-tuple-element.17.t_own, f32[256,128]{1,0:T(8,128)S(1)} %get-tuple-element.16.after_ref.c1, ...), custom_call_target="tpu_custom_call" | custom-call | flops 1207959552 | bytes 6000000 | tf_op jit(solution)/shard_map/begin/pallas_call | solution.py:331
  21.5 1.4 %collective-permute-done.6.cross = bf16[256,128]{1,0:T(8,128)(2,1)S(1)} collective-permute-done((bf16[256,128]{1,0:T(8,128)(2,1)S(1)}, bf16[256,128]{1,0:T(8,128)(2,1)S(1)}, u32[]{:S(2)}, u32[]{:S(2)}) %collective-permute-start.6) | collective-permute-done | bytes 65568 | tf_op jit(solution)/shard_map/ppermute | solution.py:521
  23.0 0.0 collective-permute-done.5.pair
  23.0 4.5 %aggregate.1 = bf16[32,96,128]{2,1,0:T(8,128)(2,1)} custom-call(bf16[3,3200,128]{2,1,0:T(8,128)(2,1)S(1)} %get-tuple-element.19.own_vol, bf16[3,64,128]{2,1,0:T(8,128)(2,1)S(1)} %get-tuple-element.20.own_cells, f32[12,256,256]{2,1,0:T(8,128)S(1)} %get-tuple-element.21.acc, bf16[256,128]{1,0:T(8,128)(2,1)S(1)} %collective-permute-done.5.pair, ...), custom_call_target="tpu_custom_call" | custom-call | tf_op jit(solution)/shard_map/aggregate/pallas_call | solution.py:494
Async XLA Ops:
  0.0 16.7 %collective-permute-start.4 = (bf16[64,128]{1,0:T(8,128)(2,1)}, bf16[64,128]{1,0:T(8,128)(2,1)S(1)}, u32[]{:S(2)}, u32[]{:S(2)}) collective-permute-start(bf16[64,128]{1,0:T(8,128)(2,1)} %bitcast.6), channel_id=1, source_target_pairs={{0,4},{1,5},{2,6},{3,7},{4,8},{5,9},{6,10},{7,11},{8,12},{9,13},{1... | collective-permute-start | bytes 49160 | tf_op jit(solution)/shard_map/ppermute | solution.py:512
  7.2 9.5 %collective-permute-start.3 = (bf16[64,128]{1,0:T(8,128)(2,1)}, bf16[64,128]{1,0:T(8,128)(2,1)S(1)}, u32[]{:S(2)}, u32[]{:S(2)}) collective-permute-start(bf16[64,128]{1,0:T(8,128)(2,1)} %bitcast.7), channel_id=1, source_target_pairs={{0,3},{1,4},{2,5},{3,6},{4,7},{5,8},{6,9},{7,10},{8,11},{9,12},{10... | collective-permute-start | bytes 49160 | tf_op jit(solution)/shard_map/ppermute | solution.py:512
  9.1 7.6 %collective-permute-start.2 = (bf16[64,128]{1,0:T(8,128)(2,1)}, bf16[64,128]{1,0:T(8,128)(2,1)S(1)}, u32[]{:S(2)}, u32[]{:S(2)}) collective-permute-start(bf16[64,128]{1,0:T(8,128)(2,1)} %bitcast.8), channel_id=1, source_target_pairs={{0,2},{1,3},{2,4},{3,5},{4,6},{5,7},{6,8},{7,9},{8,10},{9,11},{10,... | collective-permute-start | bytes 49160 | tf_op jit(solution)/shard_map/ppermute | solution.py:512
  10.6 6.1 %collective-permute-start.1 = (bf16[80,128]{1,0:T(8,128)(2,1)S(1)}, bf16[80,128]{1,0:T(8,128)(2,1)S(1)}, u32[]{:S(2)}, u32[]{:S(2)}) collective-permute-start(bf16[80,128]{1,0:T(8,128)(2,1)S(1)} %pack.1.xo), channel_id=1, source_target_pairs={{0,32},{1,2},{2,1},{3,4},{4,3},{5,6},{6,5},{7,8},{8,7},{9,10},{10,... | collective-permute-start | bytes 61448 | tf_op jit(solution)/shard_map/ppermute | solution.py:535
  13.8 3.8 %collective-permute-start = (bf16[80,128]{1,0:T(8,128)(2,1)S(1)}, bf16[80,128]{1,0:T(8,128)(2,1)S(1)}, u32[]{:S(2)}, u32[]{:S(2)}) collective-permute-start(bf16[80,128]{1,0:T(8,128)(2,1)S(1)} %pack.1.xo), channel_id=1, source_target_pairs={{0,1},{1,0},{2,3},{3,2},{4,5},{5,4},{6,7},{7,6},{8,9},{9,8},{10,11... | collective-permute-start | bytes 61448 | tf_op jit(solution)/shard_map/ppermute | solution.py:521
  18.0 5.0 %collective-permute-start.6 = (bf16[256,128]{1,0:T(8,128)(2,1)S(1)}, bf16[256,128]{1,0:T(8,128)(2,1)S(1)}, u32[]{:S(2)}, u32[]{:S(2)}) collective-permute-start(bf16[256,128]{1,0:T(8,128)(2,1)S(1)} %windows.1.own), channel_id=1, source_target_pairs={{32,64},{64,32},{96,128},{128,96},{160,192},{192,160},{224,0},{0,2... | collective-permute-start | bytes 196616 | tf_op jit(solution)/shard_map/ppermute | solution.py:521
  18.6 4.4 %collective-permute-start.5 = (bf16[256,128]{1,0:T(8,128)(2,1)S(1)}, bf16[256,128]{1,0:T(8,128)(2,1)S(1)}, u32[]{:S(2)}, u32[]{:S(2)}) collective-permute-start(bf16[256,128]{1,0:T(8,128)(2,1)S(1)} %windows.1.own), channel_id=1, source_target_pairs={{0,32},{32,0},{64,96},{96,64},{128,160},{160,128},{192,224},{224,1... | collective-permute-start | bytes 196616 | tf_op jit(solution)/shard_map/ppermute | solution.py:521

commit v8 on v6

--- a/solution.py
+++ b/solution.py
@@ -176,7 +176,7 @@
     )(offsets, lr)
 
 
-def cut(off_ref, even_ref, odd_ref, x2, x3, x4, xo, lr_ref, after_ref, out_ref, tiles):
+def cut(off_ref, even_ref, odd_ref, x2, x4, x3, xo, lr_ref, after_ref, out_ref, tiles):
     col = lax.axis_index("cols")
     final = lax.axis_size("cols") - 1
     o = off_ref[0]
@@ -236,7 +236,7 @@
     out_ref[192:256, :] = border.astype(BF16)
 
 
-def windows(offsets, even, odd, x2, x3, x4, xo, lr, after):
+def windows(offsets, even, odd, x2, x4, x3, xo, lr, after):
     return pl.pallas_call(
         cut,
         out_shape=jax.ShapeDtypeStruct((256, CW), BF16),
@@ -245,7 +245,7 @@
         scratch_shapes=[pltpu.VMEM((6, 64, CW), F32)],
         compiler_params=pltpu.CompilerParams(vmem_limit_bytes=4 * MIB),
         name="windows",
-    )(offsets, even, odd, x2, x3, x4, xo, lr, after)
+    )(offsets, even, odd, x2, x4, x3, xo, lr, after)
 
 
 def border_cells(tiles, sel):
@@ -544,7 +544,7 @@
     x3 = ahead(x, 3)
     x4 = ahead(x, 4)
     ready = prepared(weight_one, weight_two, bias_one, bias_two)
-    own = windows(offsets, even, odd, x2, x3, x4, x, lr, ready[5])
+    own = windows(offsets, even, odd, x2, x4, x3, x, lr, ready[5])
     pair = swap(own, "rows", 0)
     cross = swap(own, "rows", 1)
     out = aggregated(begun(own, ready[0], ready[5], ready[7]), pair, cross, *ready)

time: 27.7 us -> 27.7 us (level)
  starting transfers between devices: 15.1 us -> 15.6 us
  waiting for transfers between devices: 1.46 us -> 0.99 us
    ppermute x3, waiting for transfers between devices: 1.4 us -> 0.91 us  [ahead(): lax.ppermute(x, 'cols', [(i, i + by if i + by < n else n - 1 - i) for i i...]
    ppermute x3, starting transfers between devices: 4.46 us -> 4.93 us  [swap(): return lax.ppermute(x, axis, pairs)]
where the time goes in v8:
time: 27.7 us; the launch traced here: 27.3 us
  starting transfers between devices  15.6 us (56%)
  Pallas kernels  7.51 us (27%)
  other arithmetic  2.55 us (9%)
  waiting for transfers between devices  0.99 us (4%)
  between operations  0.7 us (3%)
    ppermute x3, starting transfers between devices, ahead(): lax.ppermute(x, 'cols', [(i, i + by if i + by < n else n - 1 - i) for i i...  9.4 us
    ppermute x3, starting transfers between devices, swap(): return lax.ppermute(x, axis, pairs)  4.93 us
    pallas_call x1, Pallas kernels, aggregated(): pl.pallas_call(aggregate, out_shape=jax.ShapeDtypeStruct((C, D * RH, CW),...  4.5 us
    pallas_call x1, Pallas kernels, begun(): pl.pallas_call(begin, out_shape=(jax.ShapeDtypeStruct((3, (D + 2) * OD, C...  1.86 us
    ppermute x1, starting transfers between devices, swap_inner(): return lax.ppermute(x, ('rows', 'cols'), pairs)  1.24 us
    concatenate x1, other arithmetic, prepared(): jnp.concatenate([weight_one, weight_two], axis=0)  1.13 us
    ppermute x3, waiting for transfers between devices, ahead(): lax.ppermute(x, 'cols', [(i, i + by if i + by < n else n - 1 - i) for i i...  0.91 us
    concatenate x1, other arithmetic, body(): jnp.concatenate([left.reshape(C * RH, CW), right.reshape(C * RH, CW)], ax...  0.74 us
  transfers between devices with their start and end apart: 7, of which 2 were waited for; matrix products, arithmetic and copies ran while one was open for 7% of the time, Pallas kernels for 9%

profile of v8, /device:TPU:1, one launch (start us, length us, event | category | flops | bytes accessed | tf_op | source)
XLA Modules:
  0.0 27.3 jit_solution(14895585698392476605)
XLA Ops:
  0.7 0.7 %pad_maximum_fusion.1.lr_ref = bf16[128,128]{1,0:T(8,128)(2,1)S(1)} fusion(bf16[64,128]{1,0:T(8,128)(2,1)} %bitcast.5, bf16[64,128]{1,0:T(8,128)(2,1)} %bitcast.6), kind=kLoop, calls=%fused_computation.1 | loop fusion | flops 65536 | bytes 65536 | tf_op jit(solution)/shard_map/concatenate | solution.py:539
  1.4 0.1 pack.1.xo
  1.5 5.2 %collective-permute-start.4 = (bf16[80,128]{1,0:T(8,128)(2,1)S(1)}, bf16[80,128]{1,0:T(8,128)(2,1)S(1)}, u32[]{:S(2)}, u32[]{:S(2)}) collective-permute-start(bf16[80,128]{1,0:T(8,128)(2,1)S(1)} %pack.1.xo), channel_id=1, source_target_pairs={{0,3},{1,4},{2,5},{3,6},{4,7},{5,8},{6,9},{7,10},{8,11},{9,12},{10... | collective-permute-start | bytes 61448 | tf_op jit(solution)/shard_map/ppermute | solution.py:512
  6.7 4.2 %collective-permute-start.3 = (bf16[80,128]{1,0:T(8,128)(2,1)S(1)}, bf16[80,128]{1,0:T(8,128)(2,1)S(1)}, u32[]{:S(2)}, u32[]{:S(2)}) collective-permute-start(bf16[80,128]{1,0:T(8,128)(2,1)S(1)} %pack.1.xo), channel_id=1, source_target_pairs={{0,4},{1,5},{2,6},{3,7},{4,8},{5,9},{6,10},{7,11},{8,12},{9,13},{1... | collective-permute-start | bytes 61448 | tf_op jit(solution)/shard_map/ppermute | solution.py:512
  10.9 0.0 collective-permute-start.2
  10.9 1.2 %collective-permute-start.1 = (bf16[80,128]{1,0:T(8,128)(2,1)S(1)}, bf16[80,128]{1,0:T(8,128)(2,1)S(1)}, u32[]{:S(2)}, u32[]{:S(2)}) collective-permute-start(bf16[80,128]{1,0:T(8,128)(2,1)S(1)} %pack.1.xo), channel_id=1, source_target_pairs={{0,32},{1,2},{2,1},{3,4},{4,3},{5,6},{6,5},{7,8},{8,7},{9,10},{10,... | collective-permute-start | bytes 61448 | tf_op jit(solution)/shard_map/ppermute | solution.py:535
  12.2 1.5 %collective-permute-start = (bf16[80,128]{1,0:T(8,128)(2,1)S(1)}, bf16[80,128]{1,0:T(8,128)(2,1)S(1)}, u32[]{:S(2)}, u32[]{:S(2)}) collective-permute-start(bf16[80,128]{1,0:T(8,128)(2,1)S(1)} %pack.1.xo), channel_id=1, source_target_pairs={{0,1},{1,0},{2,3},{3,2},{4,5},{5,4},{6,7},{7,6},{8,9},{9,8},{10,11... | collective-permute-start | bytes 61448 | tf_op jit(solution)/shard_map/ppermute | solution.py:521
  13.7 1.1 %pad_maximum_fusion.w_ref = bf16[54,32,32]{2,1,0:T(8,128)(2,1)S(1)} fusion(bf16[27,32,32]{2,1,0:T(8,128)(2,1)} %param.12, bf16[27,32,32]{2,1,0:T(8,128)(2,1)} %param.10), kind=kLoop, calls=%fused_computation | loop fusion | flops 55296 | bytes 221184 | tf_op jit(solution)/shard_map/concatenate | solution.py:143
  14.8 0.7 %pad_maximum_fusion.2.b_ref = f32[2,32]{1,0:T(2,128)S(1)} fusion(f32[1,32]{1,0:T(1,128)} %bitcast.7, f32[1,32]{1,0:T(1,128)} %bitcast.8), kind=kLoop, calls=%fused_computation.2 | loop fusion | flops 64 | bytes 512 | tf_op jit(solution)/shard_map/stack | solution.py:143
  15.5 0.6 %prepare.1 = (bf16[256,768]{1,0:T(8,128)(2,1)S(1)}, bf16[256,768]{1,0:T(8,128)(2,1)S(1)}, bf16[128,1792]{1,0:T(8,128)(2,1)S(1)}, bf16[256,768]{1,0:T(8,128)(2,1)...) custom-call(bf16[54,32,32]{2,1,0:T(8,128)(2,1)S(1)} %pad_maximum_fus, ...), custom_call_target="tpu_custom_call" | custom-call | flops 1000000 | bytes 4000000 | tf_op jit(solution)/shard_map/prepare/pallas_call | solution.py:126
  16.1 0.0 collective-permute-done.4.x3
  16.1 0.0 collective-permute-done.3.x4
  16.1 0.9 %collective-permute-done.2.x2 = bf16[80,128]{1,0:T(8,128)(2,1)S(1)} collective-permute-done((bf16[80,128]{1,0:T(8,128)(2,1)S(1)}, bf16[80,128]{1,0:T(8,128)(2,1)S(1)}, u32[]{:S(2)}, u32[]{:S(2)}) %collective-permute-start.2) | collective-permute-done | bytes 20512 | tf_op jit(solution)/shard_map/ppermute | solution.py:512
  17.0 0.0 collective-permute-done.1.odd_ref
  17.0 0.0 collective-permute-done.even_ref
  17.0 0.4 %windows.1.own = bf16[256,128]{1,0:T(8,128)(2,1)S(1)} custom-call(s32[1]{0:T(128)S(6)} %copy.8.off_ref, bf16[80,128]{1,0:T(8,128)(2,1)S(1)} %collective-permute-done.even_ref, bf16[80,128]{1,0:T(8,128)(2,1)S(1)} %collective-permute-done.1.odd_ref, bf16[80,128]{1,0:T(8,128)(2,1)S(1)} %collective-permute-done.2.x2, ...), custom_call_target="tpu_custom_call" | custom-call | tf_op jit(solution)/shard_map/windows/pallas_call | solution.py:240
  17.4 3.4 %collective-permute-start.6 = (bf16[256,128]{1,0:T(8,128)(2,1)S(1)}, bf16[256,128]{1,0:T(8,128)(2,1)S(1)}, u32[]{:S(2)}, u32[]{:S(2)}) collective-permute-start(bf16[256,128]{1,0:T(8,128)(2,1)S(1)} %windows.1.own), channel_id=1, source_target_pairs={{32,64},{64,32},{96,128},{128,96},{160,192},{192,160},{224,0},{0,2... | collective-permute-start | bytes 196616 | tf_op jit(solution)/shard_map/ppermute | solution.py:521
  20.9 0.0 collective-permute-start.5
  20.9 1.9 %begin.1 = (bf16[3,3200,128]{2,1,0:T(8,128)(2,1)S(1)}, bf16[3,64,128]{2,1,0:T(8,128)(2,1)S(1)}, f32[12,256,256]{2,1,0:T(8,128)S(1)}) custom-call(bf16[256,128]{1,0:T(8,128)(2,1)S(1)} %windows.1.own, bf16[256,768]{1,0:T(8,128)(2,1)S(1)} %get-tuple-element.17.t_own, f32[256,128]{1,0:T(8,128)S(1)} %get-tuple-element.16.after_ref.c1, ...), custom_call_target="tpu_custom_call" | custom-call | flops 1207959552 | bytes 6000000 | tf_op jit(solution)/shard_map/begin/pallas_call | solution.py:331
  22.7 0.1 collective-permute-done.6.cross
  22.8 0.0 collective-permute-done.5.pair
  22.8 4.5 %aggregate.1 = bf16[32,96,128]{2,1,0:T(8,128)(2,1)} custom-call(bf16[3,3200,128]{2,1,0:T(8,128)(2,1)S(1)} %get-tuple-element.19.own_vol, bf16[3,64,128]{2,1,0:T(8,128)(2,1)S(1)} %get-tuple-element.20.own_cells, f32[12,256,256]{2,1,0:T(8,128)S(1)} %get-tuple-element.21.acc, bf16[256,128]{1,0:T(8,128)(2,1)S(1)} %collective-permute-done.5.pair, ...), custom_call_target="tpu_custom_call" | custom-call | tf_op jit(solution)/shard_map/aggregate/pallas_call | solution.py:494
Async XLA Ops:
  1.5 14.6 %collective-permute-start.4 = (bf16[80,128]{1,0:T(8,128)(2,1)S(1)}, bf16[80,128]{1,0:T(8,128)(2,1)S(1)}, u32[]{:S(2)}, u32[]{:S(2)}) collective-permute-start(bf16[80,128]{1,0:T(8,128)(2,1)S(1)} %pack.1.xo), channel_id=1, source_target_pairs={{0,3},{1,4},{2,5},{3,6},{4,7},{5,8},{6,9},{7,10},{8,11},{9,12},{10... | collective-permute-start | bytes 61448 | tf_op jit(solution)/shard_map/ppermute | solution.py:512
  6.7 9.4 %collective-permute-start.3 = (bf16[80,128]{1,0:T(8,128)(2,1)S(1)}, bf16[80,128]{1,0:T(8,128)(2,1)S(1)}, u32[]{:S(2)}, u32[]{:S(2)}) collective-permute-start(bf16[80,128]{1,0:T(8,128)(2,1)S(1)} %pack.1.xo), channel_id=1, source_target_pairs={{0,4},{1,5},{2,6},{3,7},{4,8},{5,9},{6,10},{7,11},{8,12},{9,13},{1... | collective-permute-start | bytes 61448 | tf_op jit(solution)/shard_map/ppermute | solution.py:512
  10.9 6.1 %collective-permute-start.2 = (bf16[80,128]{1,0:T(8,128)(2,1)S(1)}, bf16[80,128]{1,0:T(8,128)(2,1)S(1)}, u32[]{:S(2)}, u32[]{:S(2)}) collective-permute-start(bf16[80,128]{1,0:T(8,128)(2,1)S(1)} %pack.1.xo), channel_id=1, source_target_pairs={{0,2},{1,3},{2,4},{3,5},{4,6},{5,7},{6,8},{7,9},{8,10},{9,11},{10,... | collective-permute-start | bytes 61448 | tf_op jit(solution)/shard_map/ppermute | solution.py:512
  10.9 6.1 %collective-permute-start.1 = (bf16[80,128]{1,0:T(8,128)(2,1)S(1)}, bf16[80,128]{1,0:T(8,128)(2,1)S(1)}, u32[]{:S(2)}, u32[]{:S(2)}) collective-permute-start(bf16[80,128]{1,0:T(8,128)(2,1)S(1)} %pack.1.xo), channel_id=1, source_target_pairs={{0,32},{1,2},{2,1},{3,4},{4,3},{5,6},{6,5},{7,8},{8,7},{9,10},{10,... | collective-permute-start | bytes 61448 | tf_op jit(solution)/shard_map/ppermute | solution.py:535
  12.2 4.9 %collective-permute-start = (bf16[80,128]{1,0:T(8,128)(2,1)S(1)}, bf16[80,128]{1,0:T(8,128)(2,1)S(1)}, u32[]{:S(2)}, u32[]{:S(2)}) collective-permute-start(bf16[80,128]{1,0:T(8,128)(2,1)S(1)} %pack.1.xo), channel_id=1, source_target_pairs={{0,1},{1,0},{2,3},{3,2},{4,5},{5,4},{6,7},{7,6},{8,9},{9,8},{10,11... | collective-permute-start | bytes 61448 | tf_op jit(solution)/shard_map/ppermute | solution.py:521
  17.4 5.4 %collective-permute-start.6 = (bf16[256,128]{1,0:T(8,128)(2,1)S(1)}, bf16[256,128]{1,0:T(8,128)(2,1)S(1)}, u32[]{:S(2)}, u32[]{:S(2)}) collective-permute-start(bf16[256,128]{1,0:T(8,128)(2,1)S(1)} %windows.1.own), channel_id=1, source_target_pairs={{32,64},{64,32},{96,128},{128,96},{160,192},{192,160},{224,0},{0,2... | collective-permute-start | bytes 196616 | tf_op jit(solution)/shard_map/ppermute | solution.py:521
  20.9 2.0 %collective-permute-start.5 = (bf16[256,128]{1,0:T(8,128)(2,1)S(1)}, bf16[256,128]{1,0:T(8,128)(2,1)S(1)}, u32[]{:S(2)}, u32[]{:S(2)}) collective-permute-start(bf16[256,128]{1,0:T(8,128)(2,1)S(1)} %windows.1.own), channel_id=1, source_target_pairs={{0,32},{32,0},{64,96},{96,64},{128,160},{160,128},{192,224},{224,1... | collective-permute-start | bytes 196616 | tf_op jit(solution)/shard_map/ppermute | solution.py:521
